TPU v7x, 128 devices: a whole 4x4x4 slice. The times are simulated.
128 devices in a mesh: seq: 8 (over x, y_lo), rep: 16 (over z, y_hi, core).
Axes of the slice: x: 4, y: 4 (y_hi: 2, y_lo: 2; y = y_hi * 2 + y_lo), z: 4, core: 2. Of those that a mesh axis runs over, the one named last changes fastest.
Arguments:
- activations: bfloat16 [16, 1024, 2048], P('rep', 'seq'), may hold values from -6 to 6
- gate_values: bfloat16 [16, 1024, 2048], P('rep', 'seq'), may hold values from -6 to 6
- in_weight: bfloat16 [2048, 2048], P(('seq', 'rep')), may hold values from -0.125 to 0.125
- long_filter: bfloat16 [1024, 2048], P('seq'), may hold values from -0.1875 to 0.1875
- out_cotangent: bfloat16 [16, 1024, 2048], P('rep', 'seq'), may hold values from -6 to 6
Outputs:
- mixed_out: bfloat16 [16, 1024, 2048], P('rep', 'seq')
- gate_grad: bfloat16 [16, 1024, 2048], P('rep', 'seq')
- input_grad: bfloat16 [16, 1024, 2048], P('rep', 'seq')
- weight_grad: float32 [2048, 2048], P(('seq', 'rep'))
- filter_grad: float32 [1024, 2048], P(('seq', 'rep'))
All inputs are finite; a program needn't handle non-finite values.
Results may differ from a plain program's by a relative error of at most 0.018.
Values may be sent and summed in bfloat16 or wider, within the bound.
No kernel may reach another device: no remote copies, remote signals or barrier semaphores. Data moves between devices by JAX's collectives and lax.ppermute only.
A program may use at most 256 MiB of HBM per device.

v0:
```python
import math

import jax
import jax.numpy as jnp
from jax import lax
from jax.sharding import PartitionSpec as P


def shifted(value, axis, steps):
    count = lax.axis_size(axis)
    leading, last = (max(0, -steps), min(count, count - steps))
    return lax.ppermute(value, axis, [(source, source + steps) for source in range(leading, last)])


def tables(length):
    counter = jnp.arange(length, dtype=jnp.int32)
    phase = counter[:, None] * counter[None, :] % length
    angle = phase.astype(jnp.float32) * (2.0 * math.pi / length)
    return (jnp.cos(angle), jnp.sin(angle))


def halves(table):
    upper = table.astype(jnp.bfloat16)
    lower = (table - upper.astype(jnp.float32)).astype(jnp.bfloat16)
    return (upper, lower)


def apply_exact(table, data):
    return jnp.dot(table[0], data, preferred_element_type=jnp.float32) + jnp.dot(
        table[1], data, preferred_element_type=jnp.float32
    )


def apply_float(table, data):
    d_upper, d_lower = halves(data)
    return (
        jnp.dot(table[0], d_upper, preferred_element_type=jnp.float32)
        + jnp.dot(table[1], d_upper, preferred_element_type=jnp.float32)
        + jnp.dot(table[0], d_lower, preferred_element_type=jnp.float32)
    )


def pick(stacked, distance):
    return lax.dynamic_index_in_dim(stacked, distance, 0, keepdims=False)


def local(activations, gate_values, in_weight, long_filter, out_cotangent):
    tokens = activations[0]
    gates = gate_values[0].astype(jnp.float32)
    upstream = out_cotangent[0].astype(jnp.float32)
    block = tokens.shape[0]
    span = 2 * block
    channels = gate_values.shape[2]
    groups = lax.axis_size("seq")
    replicas = lax.axis_size("rep")
    position = lax.axis_index("seq")
    cosine, sine = tables(span)
    cos_whole, sin_whole = (halves(cosine), halves(sine))
    cos_head, sin_head = (halves(cosine[:, :block]), halves(sine[:, :block]))
    cos_tail, sin_tail = (halves(cosine[:, block:]), halves(sine[:, block:]))
    cos_late, sin_late = (halves(cosine[block:]), halves(sine[block:]))
    cos_early, sin_early = (halves(cosine[:block]), halves(sine[:block]))
    zeros = jnp.zeros((span, channels), jnp.float32)
    full_weight = lax.all_gather(in_weight, ("seq", "rep"), axis=0, tiled=True)
    values = jnp.dot(tokens, full_weight, preferred_element_type=jnp.float32)
    values = values.astype(jnp.bfloat16)
    whole_filter = lax.all_gather(long_filter, "seq", axis=0, tiled=True)
    padded = jnp.concatenate([jnp.zeros((block, channels), jnp.bfloat16), whole_filter], axis=0)
    pieces = padded.reshape(groups + 1, block, channels)
    segments = jnp.concatenate([pieces[:-1], pieces[1:]], axis=1)
    seg_real = jnp.einsum(
        "kn,dnc->dkc", cos_whole[0], segments, preferred_element_type=jnp.float32
    ) + jnp.einsum("kn,dnc->dkc", cos_whole[1], segments, preferred_element_type=jnp.float32)
    seg_imag = -(
        jnp.einsum("kn,dnc->dkc", sin_whole[0], segments, preferred_element_type=jnp.float32)
        + jnp.einsum("kn,dnc->dkc", sin_whole[1], segments, preferred_element_type=jnp.float32)
    )

    def head_spectrum(stretch):
        return (apply_exact(cos_head, stretch), -apply_exact(sin_head, stretch))

    def tail_spectrum(stretch):
        return (apply_exact(cos_tail, stretch), -apply_exact(sin_tail, stretch))

    def add_forward(totals, spectrum, distance, keep):
        s_real = pick(seg_real, distance)
        s_imag = pick(seg_imag, distance)
        u_real, u_imag = spectrum
        return (
            totals[0] + keep * (s_real * u_real - s_imag * u_imag),
            totals[1] + keep * (s_real * u_imag + s_imag * u_real),
        )

    own_real, own_imag = head_spectrum(values)
    first = add_forward((zeros, zeros), (own_real, own_imag), 0, 1.0)

    def forward_turn(turn, state):
        moving = shifted(state[0], "seq", 1)
        keep = (turn <= position).astype(jnp.float32)
        totals = add_forward((state[1], state[2]), head_spectrum(moving), turn, keep)
        return (moving, totals[0], totals[1])

    state = lax.fori_loop(1, groups, forward_turn, (values, first[0], first[1]))
    total_real, total_imag = (state[1], state[2])
    conv = (apply_float(cos_late, total_real) - apply_float(sin_late, total_imag)) / span
    mixed_out = (gates * conv).astype(jnp.bfloat16)
    gate_grad = (upstream * conv).astype(jnp.bfloat16)
    inner = (upstream * gates).astype(jnp.bfloat16)

    def add_backward(state, spectrum, distance, keep):
        back_real, back_imag, grad_pad = state
        w_real, w_imag = spectrum
        s_real = pick(seg_real, distance)
        s_imag = pick(seg_imag, distance)
        back_real = back_real + keep * (s_real * w_real + s_imag * w_imag)
        back_imag = back_imag + keep * (s_real * w_imag - s_imag * w_real)
        g_real = w_real * own_real + w_imag * own_imag
        g_imag = w_imag * own_real - w_real * own_imag
        seg_grad = (apply_float(cos_whole, g_real) - apply_float(sin_whole, g_imag)) * (keep / span)
        window = lax.dynamic_slice_in_dim(grad_pad, distance * block, span, 0)
        grad_pad = lax.dynamic_update_slice_in_dim(grad_pad, window + seg_grad, distance * block, 0)
        return (back_real, back_imag, grad_pad)

    grad_start = jnp.zeros(((groups + 1) * block, channels), jnp.float32)
    first_back = add_backward((zeros, zeros, grad_start), tail_spectrum(inner), 0, 1.0)

    def backward_turn(turn, state):
        moving = shifted(state[0], "seq", -1)
        keep = (position + turn < groups).astype(jnp.float32)
        rest = add_backward(state[1:], tail_spectrum(moving), turn, keep)
        return (moving,) + rest

    state = lax.fori_loop(1, groups, backward_turn, (inner,) + first_back)
    back_real, back_imag, grad_pad = (state[1], state[2], state[3])
    value_grad = (
        (apply_float(cos_early, back_real) - apply_float(sin_early, back_imag)) / span
    ).astype(jnp.bfloat16)
    input_grad = jnp.einsum(
        "tc,dc->td", value_grad, full_weight, preferred_element_type=jnp.float32
    )
    input_grad = input_grad.astype(jnp.bfloat16)
    scale = 1.0 / math.sqrt(block * groups * replicas)
    weight_grad = lax.psum_scatter(
        jnp.einsum("td,tc->dc", tokens, value_grad, preferred_element_type=jnp.float32) * scale,
        ("seq", "rep"),
        scatter_dimension=0,
        tiled=True,
    )
    filter_grad = lax.psum_scatter(
        grad_pad[block:] * scale, ("seq", "rep"), scatter_dimension=0, tiled=True
    )
    return (mixed_out[None], gate_grad[None], input_grad[None], weight_grad, filter_grad)


def solution(mesh):
    in_specs = (
        P("rep", "seq", None),
        P("rep", "seq", None),
        P(("seq", "rep"), None),
        P("seq", None),
        P("rep", "seq", None),
    )
    out_specs = (
        P("rep", "seq", None),
        P("rep", "seq", None),
        P("rep", "seq", None),
        P(("seq", "rep"), None),
        P(("seq", "rep"), None),
    )
    return jax.shard_map(local, mesh=mesh, in_specs=in_specs, out_specs=out_specs, check_vma=False)
```

profile of v0, /device:TPU:0, one launch (start us, length us, event | category | flops | bytes accessed | tf_op | source)
XLA Modules:
  0.0 1957.7 jit_solution(6728854236854329786)
XLA Ops:
  13.9 3.0 fusion.183
  16.9 2.8 convolution_add_fusion.12
  19.8 82.1 %all-gather.5.cloned.1.call-done = bf16[1024,2048]{1,0:T(8,128)(2,1)} async-done(((bf16[128,2048]{1,0:T(8,128)(2,1)}), bf16[1024,2048]{1,0:T(8,128)(2,1)}) %all-gather.5.cloned.1.call-update) | async-done | bytes 4194320 | tf_op jit(solution)/shard_map/all_gather | solution.py:67
  101.9 6.6 copy.55
  108.5 4.6 pad_slice_fusion
  113.1 6.4 copy.54
  119.6 12.7 fusion.101
  132.2 13.7 add_bitcast_fusion
  145.9 16.6 copy.62
  162.5 12.7 fusion.98
  175.2 14.1 negate_bitcast_fusion
  189.3 16.5 copy.63
  205.7 103.9 %all-gather.3.cloned.1.call-done = bf16[2048,2048]{1,0:T(8,128)(2,1)} async-done(((bf16[16,2048]{1,0:T(8,128)(2,1)}), bf16[2048,2048]{1,0:T(8,128)(2,1)}) %all-gather.3.cloned.1.call-update) | async-done | bytes 8388624 | tf_op jit(solution)/shard_map/all_gather | solution.py:64
  309.6 4.6 convolution_convert_fusion.1
  321.9 8.2 multiply_subtract_fusion.2
  330.1 2.9 copy.68
  333.0 3.3 copy.69
  345.8 3.2 copy.74
  349.0 3.6 fusion.77
  352.6 4.8 dynamic_update_slice.13.clone2
  357.4 265.7 %while.43 = (s32[]{:T(128)}, bf16[128,2048]{1,0:T(8,128)(2,1)}, f32[256,2048]{1,0:T(8,128)}, f32[256,2048]{1,0:T(8,128)}, f32[1152,2048]{1,0:T(8,128)}, /*index=...) while((s32[]{:T(128)}, bf16[128,2048]{1,0:T(8,128)(2,1)}, ...), condition=%wide.region_3.4_spmd.clone.clone, body=%wide.region_2.3_spmd.clone.clone.sunk | while | flops 2173698048 | bytes 152306240 | solution.py:133
  362.5 10.9 collective-permute-done.1
  377.0 4.2 multiply_subtract_fusion.5
  402.5 10.4 collective-permute-done.1
  416.6 4.2 multiply_subtract_fusion.5
  442.1 9.5 collective-permute-done.1
  455.2 4.2 multiply_subtract_fusion.5
  480.7 8.6 collective-permute-done.1
  492.9 4.2 multiply_subtract_fusion.5
  518.4 7.6 collective-permute-done.1
  529.7 4.3 multiply_subtract_fusion.5
  555.2 7.0 collective-permute-done.1
  565.9 4.2 multiply_subtract_fusion.5
  591.4 7.3 collective-permute-done.1
  602.3 4.2 multiply_subtract_fusion.5
  623.1 8.4 slice_multiply_fusion
  636.4 8.1 multiply_bitcast_fusion
  644.5 17.6 copy.85
  664.1 2.9 copy.61
  667.0 148.8 %while.42 = (s32[]{:T(128)}, bf16[128,2048]{1,0:T(8,128)(2,1)}, f32[256,2048]{1,0:T(8,128)S(1)}, f32[256,2048]{1,0:T(8,128)}, s32[]{:T(128)}, /*index=5*/f32[8,2...) while((s32[]{:T(128)}, bf16[128,2048]{1,0:T(8,128)(2,1)}, ...), condition=%wide.region_1.2_spmd, body=%wide.region_0.1_spmd.sunk | while | flops 543686656 | bytes 47710524 | solution.py:103
  667.0 4.9 collective-permute-start
  671.9 6.9 collective-permute-done
  682.9 4.0 fusion.266
  688.3 4.3 collective-permute-start
  692.6 6.9 collective-permute-done
  703.6 4.0 fusion.266
  709.0 4.3 collective-permute-start
  713.3 7.0 collective-permute-done
  724.4 4.0 fusion.266
  729.7 4.3 collective-permute-start
  734.0 7.3 collective-permute-done
  745.4 4.0 fusion.266
  750.8 4.5 collective-permute-start
  755.3 7.5 collective-permute-done
  766.9 4.1 fusion.266
  772.3 4.8 collective-permute-start
  777.1 7.5 collective-permute-done
  788.7 4.1 fusion.266
  794.0 4.8 collective-permute-start
  798.8 7.6 collective-permute-done
  810.5 4.0 fusion.266
  822.7 3.7 fusion.83
  826.3 456.2 %reduce-scatter.5.cloned.1.call-done = f32[8,2048]{1,0:T(8,128)} async-done(((f32[1024,2048]{1,0:T(8,128)}), f32[8,2048]{1,0:T(8,128)}) %reduce-scatter.5.cloned.1.call-update) | async-done | bytes 65552 | tf_op jit(solution)/shard_map/reduce_scatter | solution.py:149
  1282.5 668.4 %reduce-scatter.7.cloned.1.call-done = f32[16,2048]{1,0:T(8,128)} async-done(((f32[2048,2048]{1,0:T(8,128)}), f32[16,2048]{1,0:T(8,128)}) %reduce-scatter.7.cloned.1.call-update) | async-done | bytes 131088
  (373 shorter events, 247.9 us)
Async XLA Ops:
  7.2 302.4 %copy-start = (bf16[1,128,2048]{2,1,0:T(8,128)(2,1)S(1)}, bf16[1,128,2048]{2,1,0:T(8,128)(2,1)}, u32[]{:S(2)}) copy-start(bf16[1,128,2048]{2,1,0:T(8,128)(2,1)} %param.9) | copy-start | bytes 1572868
  7.2 4.3 copy-start.35
  7.2 4.3 copy-start.37
  7.2 94.7 %all-gather.5.cloned.1.call-start = ((), (), s32[]{:S(2)}) async-start(), calls=%async_computation.3 | async-start | bytes 4718592 | tf_op jit(solution)/shard_map/all_gather | solution.py:67
  7.9 301.7 %all-gather.3.cloned.1.call-start = ((), (), s32[]{:S(2)}) async-start(), calls=%async_computation.2 | async-start | bytes 8454144 | tf_op jit(solution)/shard_map/all_gather | solution.py:64
  8.7 1273.9 %reduce-scatter.5.cloned.1.call-start = ((), (), s32[]{:S(2)}) async-start(), calls=%async_computation.4 | async-start | bytes 8454144 | tf_op jit(solution)/shard_map/reduce_scatter | solution.py:149
  11.4 302.9 %copy-start.28 = (bf16[256,128]{1,0:T(8,128)(2,1)}, bf16[256,128]{1,0:T(8,128)(2,1)S(1)}, u32[]{:S(2)}) copy-start(bf16[256,128]{1,0:T(8,128)(2,1)S(1)} %get-tuple-element.1121) | copy-start | bytes 196612
  11.4 307.6 %copy-start.32 = (bf16[256,128]{1,0:T(8,128)(2,1)}, bf16[256,128]{1,0:T(8,128)(2,1)S(1)}, u32[]{:S(2)}) copy-start(bf16[256,128]{1,0:T(8,128)(2,1)S(1)} %get-tuple-element.1122) | copy-start | bytes 196612
  11.5 304.6 %copy-start.30 = (bf16[256,128]{1,0:T(8,128)(2,1)}, bf16[256,128]{1,0:T(8,128)(2,1)S(1)}, u32[]{:S(2)}) copy-start(bf16[256,128]{1,0:T(8,128)(2,1)S(1)} %get-tuple-element.1118) | copy-start | bytes 196612
  11.5 305.1 %copy-start.33 = (bf16[256,128]{1,0:T(8,128)(2,1)}, bf16[256,128]{1,0:T(8,128)(2,1)S(1)}, u32[]{:S(2)}) copy-start(bf16[256,128]{1,0:T(8,128)(2,1)S(1)} %get-tuple-element.1119) | copy-start | bytes 196612
  119.6 12.7 copy-start.11
  162.5 12.7 copy-start.12
  314.3 4.8 copy-start.19
  319.0 2.2 copy-start.18
  319.0 2.8 copy-start.20
  339.0 2.7 copy-start.15
  345.8 3.2 copy-start.16
  357.6 15.8 collective-permute-start.1
  374.2 2.2 copy-start.2
  374.2 2.8 copy-start.5
  381.3 2.1 copy-start.6
  397.6 15.3 collective-permute-start.1
  413.8 2.2 copy-start.2
  413.8 2.8 copy-start.5
  420.8 2.1 copy-start.6
  437.2 14.4 collective-permute-start.1
  452.4 2.2 copy-start.2
  452.5 2.8 copy-start.5
  459.5 2.1 copy-start.6
  475.8 13.4 collective-permute-start.1
  490.1 2.2 copy-start.2
  490.1 2.8 copy-start.5
  497.1 2.1 copy-start.6
  513.5 12.5 collective-permute-start.1
  526.9 2.2 copy-start.2
  526.9 2.8 copy-start.5
  550.3 11.9 collective-permute-start.1
  563.1 2.2 copy-start.2
  563.1 2.8 copy-start.5
  586.5 12.2 collective-permute-start.1
  599.5 2.2 copy-start.2
  599.5 2.8 copy-start.5
  606.6 2.1 copy-start.6
  631.6 1319.3 %reduce-scatter.7.cloned.1.call-start = ((), (), s32[]{:S(2)}) async-start(), calls=%async_computation.5 | async-start | bytes 16908288
  631.6 2.3 copy-start.7
  664.1 2.9 copy-start.29
  664.1 2.9 copy-start.31
  667.0 11.8 collective-permute-start
  671.9 9.0 copy-start.34
  688.3 11.3 collective-permute-start
  692.6 9.0 copy-start.34
  709.0 11.3 collective-permute-start
  713.3 9.0 copy-start.34
  729.7 11.6 collective-permute-start
  734.0 9.4 copy-start.34
  750.8 12.0 collective-permute-start
  755.3 9.5 copy-start.34
  772.3 12.3 collective-permute-start
  777.1 9.5 copy-start.34
  794.0 12.3 collective-permute-start
  798.8 9.6 copy-start.34
  818.2 3.2 slice-start
  818.9 3.6 slice-start.1
  819.9 2.7 copy-start.27
  (55 other events, 83.9 us)
Sparse Core Ops, SparseCore 0:
  9.7 92.1 all-gather.4
  103.6 205.9 all-gather.2
  631.7 650.8 reduce-scatter.4
  1285.5 665.3 reduce-scatter.6
where the time goes:
time: 1960 us
  waiting for transfers between devices  1420 us (72%)
  matrix products  260 us (13%)
  local copies, waits for them, and re-layouts  205 us (10%)
  starting transfers between devices  41 us (2%)
    unnamed x5, waiting for transfers between devices  670 us
    reduce_scatter x1, waiting for transfers between devices, local(): lax.psum_scatter(grad_pad[block:] * scale, ('seq', 'rep'), scatter_dimens...  456 us
    ppermute x14, waiting for transfers between devices, shifted(): lax.ppermute(value, axis, [(source, source + steps) for source in range(l...  112 us
    all_gather x1, waiting for transfers between devices, local(): full_weight = lax.all_gather(in_weight, ('seq', 'rep'), axis=0, tiled=True)  104 us
    all_gather x1, waiting for transfers between devices, local(): whole_filter = lax.all_gather(long_filter, 'seq', axis=0, tiled=True)  82.1 us
    dot_general x32, matrix products, apply_exact(): jnp.dot(table[0], data, preferred_element_type=jnp.float32)  70.8 us
    while x154, local copies, waits for them, and re-layouts  60.4 us
    ppermute x14, starting transfers between devices, shifted(): lax.ppermute(value, axis, [(source, source + steps) for source in range(l...  40.8 us
  transfers between devices with their start and end apart: 18, of which 18 were waited for; matrix products, arithmetic and copies ran while one was open for 12% of the time, Pallas kernels for 0%

commit v1 on v0

v1 whole, which is shorter than its diff:
```python
import math

import jax
import jax.numpy as jnp
import numpy as np
from jax import lax
from jax.sharding import PartitionSpec as P

F32 = jnp.float32
BF16 = jnp.bfloat16


def tables(length):
    odd = 2 * np.arange(length, dtype=np.int64)[:, None] + 1
    phase = odd * np.arange(length, dtype=np.int64)[None, :] % (4 * length)
    angle = phase.astype(np.float64) * (math.pi / (2 * length))
    return (np.cos(angle), np.sin(angle))


def dot(a, b, dims=((1,), (0,))):
    return lax.dot_general(a, b, (dims, ((), ())), preferred_element_type=F32)


def local(activations, gate_values, in_weight, long_filter, out_cotangent):
    tokens = activations[0]
    gates = gate_values[0].astype(F32)
    upstream = out_cotangent[0].astype(F32)
    groups = lax.axis_size("seq")
    replicas = lax.axis_size("rep")
    block, channels = gates.shape
    features = tokens.shape[1]
    length = block * groups
    part = channels // groups
    rows = in_weight.shape[0]

    cosine, sine = tables(length)
    cos_t = jnp.asarray(cosine.astype(np.float32)).astype(BF16)
    sin_t = jnp.asarray(sine.astype(np.float32)).astype(BF16)

    def to_channels(x):
        return lax.all_to_all(x, "seq", 1, 0, tiled=True)

    def to_tokens(x):
        return lax.all_to_all(x, "seq", 0, 1, tiled=True)

    def spectrum(x):
        return (dot(cos_t, x), dot(sin_t, x))

    def inverse(real, imag):
        return (
            dot(cos_t, real.astype(BF16), ((0,), (0,))) + dot(sin_t, imag.astype(BF16), ((0,), (0,)))
        ) * (1.0 / length)

    inner = to_channels((upstream * gates).astype(BF16))
    taps = to_channels(long_filter)
    acts = lax.all_gather(tokens, "seq", axis=0, tiled=True)
    piece = to_channels(in_weight)
    weight = lax.all_gather(piece, "rep", axis=0, tiled=True)
    weight = weight.reshape(replicas, groups, rows, part).transpose(1, 0, 2, 3).reshape(features, part)

    f_c, f_s = spectrum(taps)
    i_c, i_s = spectrum(inner)
    value_grad = inverse(f_c * i_c + f_s * i_s, f_c * i_s - f_s * i_c).astype(BF16)

    values = dot(acts, weight).astype(BF16)
    v_c, v_s = spectrum(values)
    conv = inverse(f_c * v_c - f_s * v_s, f_c * v_s + f_s * v_c)
    conv = to_tokens(conv.astype(BF16)).astype(F32)
    mixed_out = (gates * conv).astype(BF16)
    gate_grad = (upstream * conv).astype(BF16)

    scale = 1.0 / math.sqrt(length * replicas)
    filter_part = inverse(v_c * i_c + v_s * i_s, v_c * i_s - v_s * i_c) * scale

    partial = dot(value_grad, weight, ((1,), (1,)))
    input_grad = lax.psum_scatter(partial.astype(BF16), "seq", scatter_dimension=0, tiled=True)

    weight_part = dot(acts, value_grad, ((0,), (0,))) * scale

    def reduce_rows(x):
        x = x.reshape(groups, replicas, -1, part).transpose(1, 0, 2, 3).reshape(-1, part)
        x = lax.psum_scatter(x, "rep", scatter_dimension=0, tiled=True)
        return lax.all_to_all(x, "seq", 0, 1, tiled=True)

    weight_grad = reduce_rows(weight_part)
    filter_grad = reduce_rows(filter_part)
    return (mixed_out[None], gate_grad[None], input_grad[None], weight_grad, filter_grad)


def solution(mesh):
    in_specs = (
        P("rep", "seq", None),
        P("rep", "seq", None),
        P(("seq", "rep"), None),
        P("seq", None),
        P("rep", "seq", None),
    )
    out_specs = (
        P("rep", "seq", None),
        P("rep", "seq", None),
        P("rep", "seq", None),
        P(("seq", "rep"), None),
        P(("seq", "rep"), None),
    )
    return jax.shard_map(local, mesh=mesh, in_specs=in_specs, out_specs=out_specs, check_vma=False)
```

time: 1960 us -> 454 us (0.23)
  waiting for transfers between devices: 1420 us -> 322 us
  matrix products: 260 us -> 25.2 us
  local copies, waits for them, and re-layouts: 205 us -> 30.6 us
  blocking collectives: 0 us -> 46.2 us
  starting transfers between devices: 41 us -> 10.6 us
    unnamed x5, waiting for transfers between devices: 670 us -> 0.76 us
    reduce_scatter x1 -> x3, waiting for transfers between devices: 456 us -> 194 us  [the longest x2 114 us: reduce_rows(): x = lax.psum_scatter(x, 'rep', scatter_dimension=0, tiled=True)]
    dot_general x131 -> x15, matrix products: 260 us -> 25.2 us  [dot(): return lax.dot_general(a, b, (dims, ((), ())), preferred_element_type=F32)]
    ppermute x14 -> x0, waiting for transfers between devices: 112 us -> none  [shifted(): lax.ppermute(value, axis, [(source, source + steps) for source in range(l...]
    while x158 -> x0, local copies, waits for them, and re-layouts: 98.2 us -> none
    all_gather x2, waiting for transfers between devices: 186 us -> 117 us  [the longest x1 88.7 us: local(): acts = lax.all_gather(tokens, 'seq', axis=0, tiled=True)]
    all_to_all x0 -> x4, blocking collectives: none -> 46.2 us  [the longest x3 35.4 us: to_channels(): return lax.all_to_all(x, 'seq', 1, 0, tiled=True)]
    ppermute x14 -> x0, starting transfers between devices: 40.8 us -> none  [shifted(): lax.ppermute(value, axis, [(source, source + steps) for source in range(l...]
  transfers between devices with their start and end apart: 18 -> 7, of which waited for: 18 -> 7; matrix products, arithmetic and copies ran while one was open for 12% -> 6% of each run, Pallas kernels for 0% -> 0%
where the time goes in v1:
time: 454 us; the launch traced here: 452 us
  waiting for transfers between devices  322 us (71%)
  blocking collectives  46.2 us (10%)
  local copies, waits for them, and re-layouts  30.6 us (7%)
  matrix products  25.2 us (6%)
  between operations  14 us (3%)
  starting transfers between devices  10.6 us (2%)
    reduce_scatter x2, waiting for transfers between devices, reduce_rows(): x = lax.psum_scatter(x, 'rep', scatter_dimension=0, tiled=True)  114 us
    all_gather x1, waiting for transfers between devices, local(): acts = lax.all_gather(tokens, 'seq', axis=0, tiled=True)  88.7 us
    reduce_scatter x1, waiting for transfers between devices, local(): lax.psum_scatter(partial.astype(BF16), 'seq', scatter_dimension=0, tiled=...  80.5 us
    all_to_all x3, blocking collectives, to_channels(): return lax.all_to_all(x, 'seq', 1, 0, tiled=True)  35.4 us
    all_gather x1, waiting for transfers between devices, local(): weight = lax.all_gather(piece, 'rep', axis=0, tiled=True)  28.6 us
    dot_general x15, matrix products, dot(): return lax.dot_general(a, b, (dims, ((), ())), preferred_element_type=F32)  25.2 us
    unnamed x50, local copies, waits for them, and re-layouts  15.9 us
    all_to_all x1, blocking collectives, reduce_rows(): return lax.all_to_all(x, 'seq', 0, 1, tiled=True)  10.8 us
  transfers between devices with their start and end apart: 7, of which 7 were waited for; matrix products, arithmetic and copies ran while one was open for 6% of the time, Pallas kernels for 0%

profile of v1, /device:TPU:0, one launch (start us, length us, event | category | flops | bytes accessed | tf_op | source)
XLA Modules:
  0.0 452.1 jit_solution(6610905542552235703)
XLA Ops:
  7.2 0.0 all-gather.4.cloned.1.call-start
  7.2 1.0 copy.76
  8.2 11.5 %all_to_all.105 = bf16[16,8,256]{2,0,1:T(8,128)(2,1)} all-to-all(bf16[16,8,256]{2,0,1:T(8,128)(2,1)S(1)} %bitcast.99), channel_id=1, replica_groups=mesh['seq'=8,'rep'=16] {'seq'}, dimensions={1} | all-to-all | bytes 131072 | tf_op jit(solution)/shard_map/all_to_all | solution.py:41
  19.8 0.0 all-gather.6.cloned.1.call-start
  19.8 0.7 all-gather.6.cloned.1.call-update
  20.5 1.3 copy.38
  21.8 0.2 copy.39
  22.1 11.2 %all_to_all.106 = bf16[128,8,256]{2,0,1:T(8,128)(2,1)S(1)} all-to-all(bf16[128,8,256]{2,0,1:T(8,128)(2,1)S(1)} %copy.39), channel_id=1, replica_groups=mesh['seq'=8,'rep'=16] {'seq'}, dimensions={1} | all-to-all | bytes 1048576 | tf_op jit(solution)/shard_map/all_to_all | solution.py:41
  33.3 0.8 fusion.27
  34.1 0.8 copy-done.20
  34.9 1.9 fusion.29
  36.7 28.6 %all-gather.4.cloned.1.call-done = bf16[2048,256]{1,0:T(8,128)(2,1)} async-done(((bf16[128,256]{1,0:T(8,128)(2,1)}), bf16[2048,256]{1,0:T(8,128)(2,1)}) %all-gather.4.cloned.1.call-update) | async-done | bytes 1048592 | tf_op jit(solution)/shard_map/all_gather | solution.py:58
  65.3 1.3 copy.42
  66.7 88.7 %all-gather.6.cloned.1.call-done = bf16[1,1024,2048]{2,1,0:T(8,128)(2,1)} async-done(((bf16[1,128,2048]{2,1,0:T(8,128)(2,1)}), bf16[1,1024,2048]{2,1,0:T(8,128)(2,1)}) %all-gather.6.cloned.1.call-update) | async-done | bytes 4194320 | tf_op jit(solution)/shard_map/all_gather | solution.py:56
  155.4 3.6 fusion.16
  159.0 0.7 fusion.39
  159.7 0.9 copy-done
  160.6 0.7 fusion.38
  161.3 0.9 copy-done.4
  162.2 0.9 fusion.31
  163.1 0.1 copy-done.8
  163.2 0.9 fusion.19
  164.1 0.9 copy.75
  165.0 5.8 %all-to-all-start.2 = ((bf16[8,128,256]{1,2,0:T(8,128)(2,1)}), bf16[8,128,256]{1,2,0:T(8,128)(2,1)}, u32[]{:S(2)}, u32[]{:S(2)}) async-start(bf16[8,128,256]{1,2,0:T(8,128)(2,1)} %bitcast.93), calls=%async_computation.2 | async-start | bytes 1048576 | tf_op jit(solution)/shard_map/all_to_all | solution.py:44
  170.8 0.0 reduce-scatter.8.cloned.1.call-start
  170.8 2.0 copy.37
  172.9 2.0 copy.44
  174.9 5.3 %all-to-all-done.2 = bf16[8,128,256]{1,2,0:T(8,128)(2,1)} async-done(((bf16[8,128,256]{1,2,0:T(8,128)(2,1)}), bf16[8,128,256]{1,2,0:T(8,128)(2,1)}, u32[]{:S(2)}, u32[]{:S(2)}) %all-to-all-start.2) | async-done | bytes 524320 | tf_op jit(solution)/shard_map/all_to_all | solution.py:44
  180.2 1.1 convert_element_type.107
  181.3 2.6 fusion.21
  183.9 2.0 copy.45
  185.9 12.6 %all_to_all.107 = bf16[128,8,256]{2,0,1:T(8,128)(2,1)S(1)} all-to-all(bf16[128,8,256]{2,0,1:T(8,128)(2,1)} %copy.45), channel_id=1, replica_groups=mesh['seq'=8,'rep'=16] {'seq'}, dimensions={1} | all-to-all | bytes 1048576 | tf_op jit(solution)/shard_map/all_to_all | solution.py:41
  198.6 2.6 fusion.23
  201.2 0.8 fusion.25
  202.0 0.8 copy-done.7
  202.8 0.3 copy-done.9
  203.1 0.9 fusion.33
  204.0 0.1 copy-done.12
  204.1 0.9 copy-done.2
  205.0 1.9 fusion.11
  206.9 2.6 copy.50
  209.5 2.4 copy.51
  211.9 0.2 reduce-scatter.6.cloned.1.call-start
  212.2 2.8 fusion.32
  215.0 0.3 copy-done.11
  215.3 0.3 copy-done.13
  215.6 0.9 fusion.15
  216.5 1.3 copy-done.18
  217.8 2.6 fusion.7
  220.4 1.9 copy.47
  222.4 1.6 copy.48
  224.0 0.0 reduce-scatter.4.cloned.1.call-start
  224.1 1.2 copy-done.15
  225.2 3.3 convolution_convert_fusion
  228.5 50.0 %reduce-scatter.8.cloned.1.call-done = f32[64,256]{1,0:T(8,128)} async-done(((f32[1024,256]{1,0:T(8,128)}), f32[64,256]{1,0:T(8,128)}) %reduce-scatter.8.cloned.1.call-update) | async-done | bytes 65552 | tf_op jit(solution)/shard_map/reduce_scatter | solution.py:82
  278.5 10.8 %all_to_all.108 = f32[8,8,256]{2,1,0:T(8,128)S(1)} all-to-all(f32[8,8,256]{2,1,0:T(8,128)} %bitcast.103), channel_id=1, replica_groups=mesh['seq'=8,'rep'=16] {'seq'}, dimensions={0} | all-to-all | bytes 131072 | tf_op jit(solution)/shard_map/all_to_all | solution.py:83
  289.3 63.6 %reduce-scatter.6.cloned.1.call-done = f32[128,256]{1,0:T(8,128)} async-done(((f32[2048,256]{1,0:T(8,128)}), f32[128,256]{1,0:T(8,128)}) %reduce-scatter.6.cloned.1.call-update) | async-done | bytes 131088 | tf_op jit(solution)/shard_map/reduce_scatter | solution.py:82
  352.9 4.5 all-to-all-start.4
  357.4 1.0 copy.53
  358.4 1.0 copy.52
  359.4 4.4 all-to-all-done.4
  363.8 0.7 copy.56
  364.4 80.5 %reduce-scatter.4.cloned.1.call-done = bf16[128,2048]{1,0:T(8,128)(2,1)} async-done(((bf16[1024,2048]{1,0:T(8,128)(2,1)}), bf16[128,2048]{1,0:T(8,128)(2,1)}) %reduce-scatter.4.cloned.1.call-update) | async-done | bytes 524304 | tf_op jit(solution)/shard_map/reduce_scatter | solution.py:76
  444.9 0.6 copy.78
  (36 shorter events, 0.1 us)
Async XLA Ops:
  7.2 26.1 %copy-start.19 = (bf16[1024,1024]{1,0:T(8,128)(2,1)S(1)}, bf16[1024,1024]{1,0:T(8,128)(2,1)}, u32[]{:S(2)}) copy-start(bf16[1024,1024]{1,0:T(8,128)(2,1)} %constant.24) | copy-start | bytes 6291460
  7.2 58.2 %all-gather.4.cloned.1.call-start = ((), (), s32[]{:S(2)}) async-start(), calls=%async_computation.9 | async-start | bytes 1114112 | tf_op jit(solution)/shard_map/all_gather | solution.py:58
  19.8 135.6 %all-gather.6.cloned.1.call-start = ((), (), s32[]{:S(2)}) async-start(), calls=%async_computation.13 | async-start | bytes 4718592 | tf_op jit(solution)/shard_map/all_gather | solution.py:56
  33.3 1.6 copy-start.20
  66.7 88.7 %copy-start.14 = (bf16[16,8,16,256]{3,2,0,1:T(8,128)(2,1)}, bf16[16,8,16,256]{3,2,0,1:T(8,128)(2,1)S(1)}, u32[]{:S(2)}) copy-start(bf16[16,8,16,256]{3,2,0,1:T(8,128)(2,1)S(1)} %copy.42) | copy-start | bytes 3145732
  155.4 3.6 copy-start.1
  159.0 1.6 copy-start
  160.6 2.5 copy-start.6
  160.6 1.6 copy-start.4
  162.2 1.0 copy-start.8
  165.0 15.2 %all-to-all-start.2 = ((bf16[8,128,256]{1,2,0:T(8,128)(2,1)}), bf16[8,128,256]{1,2,0:T(8,128)(2,1)}, u32[]{:S(2)}, u32[]{:S(2)}) async-start(bf16[8,128,256]{1,2,0:T(8,128)(2,1)} %bitcast.93), calls=%async_computation.2 | async-start | bytes 1048576 | tf_op jit(solution)/shard_map/all_to_all | solution.py:44
  170.8 107.7 %reduce-scatter.8.cloned.1.call-start = ((), (), s32[]{:S(2)}) async-start(), calls=%async_computation.12 | async-start | bytes 1114112 | tf_op jit(solution)/shard_map/reduce_scatter | solution.py:82
  198.6 2.6 copy-start.21
  201.1 2.8 copy-start.10
  201.2 1.6 copy-start.7
  201.2 1.9 copy-start.9
  203.1 1.0 copy-start.12
  203.1 2.0 copy-start.2
  211.9 141.0 %reduce-scatter.6.cloned.1.call-start = ((), (), s32[]{:S(2)}) async-start(), calls=%async_computation.11 | async-start | bytes 2228224 | tf_op jit(solution)/shard_map/reduce_scatter | solution.py:82
  212.2 2.8 copy-start.3
  212.2 2.8 copy-start.5
  212.2 3.1 copy-start.11
  212.2 3.4 copy-start.13
  215.6 2.2 copy-start.18
  224.0 1.2 copy-start.15
  224.0 220.9 %reduce-scatter.4.cloned.1.call-start = ((), (), s32[]{:S(2)}) async-start(), calls=%async_computation.10 | async-start | bytes 4718592 | tf_op jit(solution)/shard_map/reduce_scatter | solution.py:76
  228.5 128.9 %copy-start.17 = (bf16[1,128,2048]{1,2,0:T(8,128)(2,1)S(1)}, bf16[1,128,2048]{1,2,0:T(8,128)(2,1)}, u32[]{:S(2)}) copy-start(bf16[1,128,2048]{1,2,0:T(8,128)(2,1)} %get-tuple-element.10) | copy-start | bytes 1572868
  228.5 129.9 %copy-start.16 = (bf16[1,128,2048]{1,2,0:T(8,128)(2,1)S(1)}, bf16[1,128,2048]{1,2,0:T(8,128)(2,1)}, u32[]{:S(2)}) copy-start(bf16[1,128,2048]{1,2,0:T(8,128)(2,1)} %get-tuple-element.11) | copy-start | bytes 1572868
  352.9 10.9 %all-to-all-start.4 = ((f32[8,16,256]{2,1,0:T(8,128)}), f32[8,16,256]{2,1,0:T(8,128)S(1)}, u32[]{:S(2)}, u32[]{:S(2)}) async-start(f32[8,16,256]{2,1,0:T(8,128)} %bitcast.100), calls=%async_computation.6 | async-start | bytes 262144 | tf_op jit(solution)/shard_map/all_to_all | solution.py:83
Sparse Core Ops, SparseCore 0:
  19.9 45.3 all-gather.3
  67.0 88.3 all-gather.5
  212.1 66.4 reduce-scatter.7
  282.7 70.1 reduce-scatter.5
  355.7 89.1 reduce-scatter.3

commit v2 on v1

--- a/solution.py
+++ b/solution.py
@@ -38,7 +38,8 @@
     sin_t = jnp.asarray(sine.astype(np.float32)).astype(BF16)
 
     def to_channels(x):
-        return lax.all_to_all(x, "seq", 1, 0, tiled=True)
+        x = x.reshape(x.shape[0], groups, part).transpose(1, 0, 2)
+        return lax.all_to_all(x, "seq", 0, 0, tiled=True)
 
     def to_tokens(x):
         return lax.all_to_all(x, "seq", 0, 1, tiled=True)
@@ -51,10 +52,13 @@
             dot(cos_t, real.astype(BF16), ((0,), (0,))) + dot(sin_t, imag.astype(BF16), ((0,), (0,)))
         ) * (1.0 / length)
 
-    inner = to_channels((upstream * gates).astype(BF16))
-    taps = to_channels(long_filter)
-    acts = lax.all_gather(tokens, "seq", axis=0, tiled=True)
-    piece = to_channels(in_weight)
+    inner = (upstream * gates).astype(BF16)
+    slices = to_channels(jnp.concatenate([inner, long_filter, in_weight], axis=0))
+    inner = slices[:, :block].reshape(length, part)
+    taps = slices[:, block : 2 * block].reshape(length, part)
+    piece = slices[:, 2 * block :].reshape(groups * rows, part)
+    acts = jnp.broadcast_to(tokens, (groups, block, features))
+    acts = lax.all_to_all(acts, "seq", 0, 0, tiled=True).reshape(length, features)
     weight = lax.all_gather(piece, "rep", axis=0, tiled=True)
     weight = weight.reshape(replicas, groups, rows, part).transpose(1, 0, 2, 3).reshape(features, part)
 
@@ -77,13 +81,18 @@
 
     weight_part = dot(acts, value_grad, ((0,), (0,))) * scale
 
-    def reduce_rows(x):
-        x = x.reshape(groups, replicas, -1, part).transpose(1, 0, 2, 3).reshape(-1, part)
-        x = lax.psum_scatter(x, "rep", scatter_dimension=0, tiled=True)
-        return lax.all_to_all(x, "seq", 0, 1, tiled=True)
-
-    weight_grad = reduce_rows(weight_part)
-    filter_grad = reduce_rows(filter_part)
+    owned = jnp.concatenate(
+        [
+            weight_part.astype(BF16).reshape(groups, replicas, -1, part),
+            filter_part.astype(BF16).reshape(groups, replicas, -1, part),
+        ],
+        axis=2,
+    )
+    owned = lax.all_to_all(owned.transpose(1, 0, 2, 3), "rep", 0, 0, tiled=True)
+    owned = jnp.sum(owned.astype(F32), axis=0)
+    owned = lax.all_to_all(owned, "seq", 0, 0, tiled=True).transpose(1, 0, 2).reshape(-1, channels)
+    weight_grad = owned[:rows]
+    filter_grad = owned[rows:]
     return (mixed_out[None], gate_grad[None], input_grad[None], weight_grad, filter_grad)
 
 

time: 454 us -> 227 us (0.50)
  waiting for transfers between devices: 322 us -> 122 us
  blocking collectives: 46.2 us -> 21.7 us
  local copies, waits for them, and re-layouts: 30.6 us -> 17.9 us
  starting transfers between devices: 10.6 us -> 17.7 us
    reduce_scatter x2 -> x0, waiting for transfers between devices: 114 us -> none  [reduce_rows(): x = lax.psum_scatter(x, 'rep', scatter_dimension=0, tiled=True)]
    all_gather x1 -> x0, waiting for transfers between devices: 88.7 us -> none  [local(): acts = lax.all_gather(tokens, 'seq', axis=0, tiled=True)]
    reduce_scatter x1, waiting for transfers between devices: 80.5 us -> 1.87 us  [local(): lax.psum_scatter(partial.astype(BF16), 'seq', scatter_dimension=0, tiled=...]
    all_to_all x1 -> x3, waiting for transfers between devices: 4.38 us -> 62.3 us  [the longest x1 56.2 us: local(): owned = lax.all_to_all(owned.transpose(1, 0, 2, 3), 'rep', 0, 0, tiled=True)]
    all_gather x1, waiting for transfers between devices: 28.6 us -> 53.9 us  [local(): weight = lax.all_gather(piece, 'rep', axis=0, tiled=True)]
    all_to_all x4 -> x1, blocking collectives: 46.2 us -> 21.7 us  [to_channels(): return lax.all_to_all(x, 'seq', 0, 0, tiled=True)]
    unnamed x50 -> x40, local copies, waits for them, and re-layouts: 15.9 us -> 5.36 us
    all_to_all x1 -> x3, starting transfers between devices: 4.47 us -> 14 us  [the longest x1 5.56 us: local(): owned = lax.all_to_all(owned.transpose(1, 0, 2, 3), 'rep', 0, 0, tiled=True)]
  transfers between devices with their start and end apart: 7 -> 6, of which waited for: 7 -> 5; matrix products, arithmetic and copies ran while one was open for 6% -> 17% of each run, Pallas kernels for 0% -> 0%
where the time goes in v2:
time: 227 us; the launch traced here: 225 us
  waiting for transfers between devices  122 us (54%)
  matrix products  23.6 us (10%)
  blocking collectives  21.7 us (10%)
  local copies, waits for them, and re-layouts  17.9 us (8%)
  starting transfers between devices  17.7 us (8%)
  between operations  14.4 us (6%)
  other arithmetic  7.91 us (3%)
    all_to_all x1, waiting for transfers between devices, local(): owned = lax.all_to_all(owned.transpose(1, 0, 2, 3), 'rep', 0, 0, tiled=True)  56.2 us
    all_gather x1, waiting for transfers between devices, local(): weight = lax.all_gather(piece, 'rep', axis=0, tiled=True)  53.9 us
    dot_general x15, matrix products, dot(): return lax.dot_general(a, b, (dims, ((), ())), preferred_element_type=F32)  23.6 us
    all_to_all x1, blocking collectives, to_channels(): return lax.all_to_all(x, 'seq', 0, 0, tiled=True)  21.7 us
    all_to_all x1, waiting for transfers between devices, local(): lax.all_to_all(owned, 'seq', 0, 0, tiled=True).transpose(1, 0, 2)  6.07 us
    all_to_all x1, starting transfers between devices, local(): owned = lax.all_to_all(owned.transpose(1, 0, 2, 3), 'rep', 0, 0, tiled=True)  5.56 us
    unnamed x40, local copies, waits for them, and re-layouts  5.36 us
    all_to_all x1, starting transfers between devices, local(): lax.all_to_all(acts, 'seq', 0, 0, tiled=True).reshape(length, features)  4.56 us
  transfers between devices with their start and end apart: 6, of which 5 were waited for; matrix products, arithmetic and copies ran while one was open for 17% of the time, Pallas kernels for 0%

profile of v2, /device:TPU:0, one launch (start us, length us, event | category | flops | bytes accessed | tf_op | source)
XLA Modules:
  0.0 225.2 jit_solution(11574558336647462048)
XLA Ops:
  7.2 1.3 fusion.13
  8.5 1.2 pad_maximum_fusion
  9.7 0.3 copy.38
  10.0 0.0 copy-start.18
  10.0 0.2 copy.27
  10.3 21.7 %all_to_all.33 = bf16[8,272,256]{2,1,0:T(8,128)(2,1)S(1)} all-to-all(bf16[8,272,256]{2,1,0:T(8,128)(2,1)S(1)} %copy.27), channel_id=1, replica_groups=mesh['seq'=8,'rep'=16] {'seq'}, dimensions={0} | all-to-all | bytes 2228224 | tf_op jit(solution)/shard_map/all_to_all | solution.py:42
  32.0 2.5 %broadcast_in_dim.8 = bf16[8,128,2048]{2,1,0:T(8,128)(2,1)} broadcast(bf16[128,2048]{1,0:T(8,128)(2,1)S(1)} %bitcast.76), dimensions={1,2} | broadcast | bytes 4718592 | tf_op jit(solution)/shard_map/broadcast_in_dim | solution.py:60
  34.5 4.6 %all-to-all-start.1 = ((bf16[8,128,2048]{2,1,0:T(8,128)(2,1)}), bf16[8,128,2048]{2,1,0:T(8,128)(2,1)}, u32[]{:S(2)}, u32[]{:S(2)}) async-start(bf16[8,128,2048]{2,1,0:T(8,128)(2,1)} %broadcast_in_dim.8), calls=%async_computation.1 | async-start | bytes 8388608 | tf_op jit(solution)/shard_map/all_to_all | solution.py:61
  39.1 0.0 copy-start
  39.1 0.0 all-gather.2.cloned.1.call-start
  39.1 0.6 slice.29
  39.8 0.0 all-gather.2.cloned.1.call-update
  39.8 0.0 reduce-scatter.2.cloned.1.call-start
  39.9 0.1 fusion.17
  40.0 0.0 copy-start.1
  40.0 0.7 copy-done
  40.7 0.8 fusion.22
  41.4 0.3 copy-done.1
  41.7 0.8 fusion.23
  42.5 0.8 fusion.18
  43.3 0.8 fusion.20
  44.1 0.8 fusion.15
  44.9 0.2 copy-done.4
  45.1 1.6 fusion.6
  46.7 53.9 %all-gather.2.cloned.1.call-done = bf16[2048,256]{1,0:T(8,128)(2,1)} async-done(((bf16[128,256]{1,0:T(8,128)(2,1)}), bf16[2048,256]{1,0:T(8,128)(2,1)}) %all-gather.2.cloned.1.call-update) | async-done | bytes 1048592 | tf_op jit(solution)/shard_map/all_gather | solution.py:62
  100.5 1.4 copy.28
  101.9 1.0 copy-done.14
  102.9 3.3 %convolution_convert_fusion = bf16[1024,2048]{1,0:T(8,128)(2,1)} fusion(bf16[256,1024]{1,0:T(8,128)(2,1)S(1)} %copy-done.15, bf16[2048,256]{1,0:T(8,128)(2,1)S(1)} %bitcast.68), kind=kOutput, calls=%fused_computation | convolution fusion | flops 1075838976 | bytes 5767168 | tf_op jit(solution)/shard_map/dot_general | solution.py:21
  106.2 0.0 reduce-scatter.2.cloned.1.call-update
  106.2 3.8 %convolution_convert_fusion.1 = bf16[256,1024]{1,0:T(8,128)(2,1)S(1)} fusion(bf16[2048,256]{1,0:T(8,128)(2,1)} %bitcast.69, bf16[1024,2048]{1,0:T(8,128)(2,1)} %bitcast.8), kind=kOutput, calls=%fused_computation.18 | convolution fusion | flops 1074003968 | bytes 5767168 | tf_op jit(solution)/shard_map/dot_general | solution.py:21
  110.0 0.0 copy-start.2
  110.0 0.7 fusion.19
  110.8 0.8 copy-done.2
  111.6 0.7 fusion.21
  112.4 0.9 copy-done.7
  113.3 0.3 copy-done.9
  113.6 0.8 fusion.16
  114.4 0.2 copy-done.12
  114.6 1.6 fusion.8
  116.2 2.1 copy.33
  118.3 2.8 %fusion.14 = f32[256,1024]{1,0:T(8,128)S(1)} fusion(bf16[1024,1024]{1,0:T(8,128)(2,1)S(1)} %copy-done, f32[256,1024]{1,0:T(8,128)} %copy-done.4, f32[256,1024]{1,0:T(8,128)} %copy-done.12, f32[256,1024]{1,0:T(8,128)S(1)} %fusion.18, f32[256,1024]{1,0:T(8,128)} %copy-done.10), kind=kOutput, calls=%fused_computation.33 | convolution fusion | flops 537919488 | bytes 7340032 | tf_op jit(solution)/shard_map/dot_general | solution.py:21
  121.1 0.0 copy-done.5
  121.1 0.3 copy-done.11
  121.4 0.3 copy-done.13
  121.7 0.8 fusion.9
  122.5 0.0 copy-start.16
  122.6 0.9 copy.40
  123.4 3.7 %all-to-all-start.2 = ((bf16[8,128,256]{1,2,0:T(8,128)(2,1)}), bf16[8,128,256]{1,2,0:T(8,128)(2,1)S(1)}, u32[]{:S(2)}, u32[]{:S(2)}) async-start(bf16[8,128,256]{1,2,0:T(8,128)(2,1)} %bitcast.61), calls=%async_computation.2 | async-start | bytes 1048576 | tf_op jit(solution)/shard_map/all_to_all | solution.py:45
  127.1 3.5 %fusion.1 = bf16[2048,256]{0,1:T(8,128)(2,1)S(1)} fusion(bf16[256,1024]{1,0:T(8,128)(2,1)S(1)} %copy-done.16, bf16[1024,2048]{1,0:T(8,128)(2,1)} %bitcast.8), kind=kOutput, calls=%fused_computation.4 | convolution fusion | flops 1074790400 | bytes 5767168 | tf_op jit(solution)/shard_map/dot_general | solution.py:21
  130.6 0.5 copy.32
  131.2 1.1 maximum_bitcast_fusion
  132.3 1.3 copy.34
  133.7 4.0 %all-to-all-done.2 = bf16[8,128,256]{1,2,0:T(8,128)(2,1)S(1)} async-done(((bf16[8,128,256]{1,2,0:T(8,128)(2,1)}), bf16[8,128,256]{1,2,0:T(8,128)(2,1)S(1)}, u32[]{:S(2)}, u32[]{:S(2)}) %all-to-all-start.2) | async-done | bytes 524320 | tf_op jit(solution)/shard_map/all_to_all | solution.py:45
  137.6 5.6 %all-to-all-start.3 = ((bf16[16,8,24,256]{3,2,1,0:T(8,128)(2,1)}), bf16[16,8,24,256]{3,2,1,0:T(8,128)(2,1)S(1)}, u32[]{:S(2)}, u32[]{:S(2)}) async-start(bf16[16,8,24,256]{3,2,1,0:T(8,128)(2,1)} %copy.34), calls=%async_computation.4 | async-start | bytes 3145728 | tf_op jit(solution)/shard_map/all_to_all | solution.py:91
  143.2 1.1 convert_element_type.131
  144.3 1.6 copy.30
  145.9 56.2 %all-to-all-done.3 = bf16[16,8,24,256]{3,2,1,0:T(8,128)(2,1)S(1)} async-done(((bf16[16,8,24,256]{3,2,1,0:T(8,128)(2,1)}), bf16[16,8,24,256]{3,2,1,0:T(8,128)(2,1)S(1)}, u32[]{:S(2)}, u32[]{:S(2)}) %all-to-all-start.3) | async-done | bytes 1572896 | tf_op jit(solution)/shard_map/all_to_all | solution.py:91
  202.1 0.9 convert_reduce_fusion
  203.0 3.8 %all-to-all-start.4 = ((f32[8,24,256]{2,1,0:T(8,128)}), f32[8,24,256]{2,1,0:T(8,128)S(1)}, u32[]{:S(2)}, u32[]{:S(2)}) async-start(f32[8,24,256]{2,1,0:T(8,128)} %convert_reduce_fusion), calls=%async_computation.5 | async-start | bytes 393216 | tf_op jit(solution)/shard_map/all_to_all | solution.py:93
  206.8 2.3 %fusion.12 = (bf16[1,128,2048]{2,1,0:T(8,128)(2,1)}, bf16[1,128,2048]{2,1,0:T(8,128)(2,1)}) fusion(f32[1,128,2048]{2,1,0:T(8,128)S(1)} %copy.30, bf16[1,128,2048]{2,1,0:T(8,128)(2,1)} %param.11, bf16[1,128,2048]{2,1,0:T(8,128)(2,1)S(1)} %copy-done.17), kind=kLoop, calls=%fused_computation.24 | loop fusion | flops 1572864 | bytes 3145728 | tf_op jit(solution)/shard_map/convert_element_type | solution.py:74
  209.1 6.1 %all-to-all-done.4 = f32[8,24,256]{2,1,0:T(8,128)S(1)} async-done(((f32[8,24,256]{2,1,0:T(8,128)}), f32[8,24,256]{2,1,0:T(8,128)S(1)}, u32[]{:S(2)}, u32[]{:S(2)}) %all-to-all-start.4) | async-done | bytes 196640 | tf_op jit(solution)/shard_map/all_to_all | solution.py:93
  215.2 0.6 slice.32
  215.8 0.7 copy.37
  216.5 1.9 reduce-scatter.2.cloned.1.call-done
  (24 shorter events, 0.1 us)
Async XLA Ops:
  10.0 22.0 %copy-start.18 = (bf16[1,128,2048]{2,1,0:T(8,128)(2,1)S(1)}, bf16[1,128,2048]{2,1,0:T(8,128)(2,1)}, u32[]{:S(2)}) copy-start(bf16[1,128,2048]{2,1,0:T(8,128)(2,1)} %param.7) | copy-start | bytes 1572868
  34.5 71.7 %all-to-all-start.1 = ((bf16[8,128,2048]{2,1,0:T(8,128)(2,1)}), bf16[8,128,2048]{2,1,0:T(8,128)(2,1)}, u32[]{:S(2)}, u32[]{:S(2)}) async-start(bf16[8,128,2048]{2,1,0:T(8,128)(2,1)} %broadcast_in_dim.8), calls=%async_computation.1 | async-start | bytes 8388608 | tf_op jit(solution)/shard_map/all_to_all | solution.py:61
  39.1 1.6 copy-start
  39.1 61.4 %all-gather.2.cloned.1.call-start = ((), (), s32[]{:S(2)}) async-start(), calls=%async_computation.6 | async-start | bytes 1114112 | tf_op jit(solution)/shard_map/all_gather | solution.py:62
  39.8 178.6 %reduce-scatter.2.cloned.1.call-start = ((), (), s32[]{:S(2)}) async-start(), calls=%async_computation.7 | async-start | bytes 4718592 | tf_op jit(solution)/shard_map/reduce_scatter | solution.py:80
  40.0 1.8 copy-start.1
  41.7 3.2 %copy-start.6 = (f32[256,1024]{1,0:T(8,128)}, f32[256,1024]{1,0:T(8,128)S(1)}, u32[]{:S(2)}) copy-start(f32[256,1024]{1,0:T(8,128)S(1)} %fusion.22) | copy-start | bytes 3145732
  42.5 2.4 %copy-start.8 = (f32[256,1024]{1,0:T(8,128)}, f32[256,1024]{1,0:T(8,128)S(1)}, u32[]{:S(2)}) copy-start(f32[256,1024]{1,0:T(8,128)S(1)} %fusion.23) | copy-start | bytes 3145732
  44.0 1.0 copy-start.4
  100.5 2.4 %copy-start.15 = (bf16[256,1024]{1,0:T(8,128)(2,1)S(1)}, bf16[256,1024]{1,0:T(8,128)(2,1)}, u32[]{:S(2)}) copy-start(bf16[256,1024]{1,0:T(8,128)(2,1)} %fusion.6) | copy-start | bytes 1572868
  101.9 1.0 copy-start.14
  110.0 1.6 copy-start.2
  111.6 2.8 %copy-start.10 = (f32[256,1024]{1,0:T(8,128)}, f32[256,1024]{1,0:T(8,128)S(1)}, u32[]{:S(2)}) copy-start(f32[256,1024]{1,0:T(8,128)S(1)} %fusion.19) | copy-start | bytes 3145732
  111.6 1.7 copy-start.7
  111.6 2.0 copy-start.9
  113.6 1.0 copy-start.12
  118.2 2.8 %copy-start.3 = (bf16[1024,1024]{1,0:T(8,128)(2,1)S(1)}, bf16[1024,1024]{1,0:T(8,128)(2,1)}, u32[]{:S(2)}) copy-start(bf16[1024,1024]{1,0:T(8,128)(2,1)} %constant.20) | copy-start | bytes 6291460
  118.2 2.9 %copy-start.5 = (f32[256,1024]{1,0:T(8,128)S(1)}, f32[256,1024]{1,0:T(8,128)}, u32[]{:S(2)}) copy-start(f32[256,1024]{1,0:T(8,128)} %copy-done.4) | copy-start | bytes 3145732
  118.2 3.2 %copy-start.11 = (f32[256,1024]{1,0:T(8,128)S(1)}, f32[256,1024]{1,0:T(8,128)}, u32[]{:S(2)}) copy-start(f32[256,1024]{1,0:T(8,128)} %copy-done.10) | copy-start | bytes 3145732
  118.2 3.5 %copy-start.13 = (f32[256,1024]{1,0:T(8,128)S(1)}, f32[256,1024]{1,0:T(8,128)}, u32[]{:S(2)}) copy-start(f32[256,1024]{1,0:T(8,128)} %copy-done.12) | copy-start | bytes 3145732
  122.5 4.6 %copy-start.16 = (bf16[256,1024]{1,0:T(8,128)(2,1)S(1)}, bf16[256,1024]{1,0:T(8,128)(2,1)}, u32[]{:S(2)}) copy-start(bf16[256,1024]{1,0:T(8,128)(2,1)} %fusion.6) | copy-start | bytes 1572868
  123.4 14.2 %all-to-all-start.2 = ((bf16[8,128,256]{1,2,0:T(8,128)(2,1)}), bf16[8,128,256]{1,2,0:T(8,128)(2,1)S(1)}, u32[]{:S(2)}, u32[]{:S(2)}) async-start(bf16[8,128,256]{1,2,0:T(8,128)(2,1)} %bitcast.61), calls=%async_computation.2 | async-start | bytes 1048576 | tf_op jit(solution)/shard_map/all_to_all | solution.py:45
  137.6 64.5 %all-to-all-start.3 = ((bf16[16,8,24,256]{3,2,1,0:T(8,128)(2,1)}), bf16[16,8,24,256]{3,2,1,0:T(8,128)(2,1)S(1)}, u32[]{:S(2)}, u32[]{:S(2)}) async-start(bf16[16,8,24,256]{3,2,1,0:T(8,128)(2,1)} %copy.34), calls=%async_computation.4 | async-start | bytes 3145728 | tf_op jit(solution)/shard_map/all_to_all | solution.py:91
  144.3 62.6 %copy-start.17 = (bf16[1,128,2048]{2,1,0:T(8,128)(2,1)S(1)}, bf16[1,128,2048]{2,1,0:T(8,128)(2,1)}, u32[]{:S(2)}) copy-start(bf16[1,128,2048]{2,1,0:T(8,128)(2,1)} %param.8) | copy-start | bytes 1572868
  203.0 12.2 %all-to-all-start.4 = ((f32[8,24,256]{2,1,0:T(8,128)}), f32[8,24,256]{2,1,0:T(8,128)S(1)}, u32[]{:S(2)}, u32[]{:S(2)}) async-start(f32[8,24,256]{2,1,0:T(8,128)} %convert_reduce_fusion), calls=%async_computation.5 | async-start | bytes 393216 | tf_op jit(solution)/shard_map/all_to_all | solution.py:93
Sparse Core Ops, SparseCore 0:
  42.9 57.5 all-gather.1
  106.3 112.0 reduce-scatter.1

commit v3 on v2

v3 whole, which is shorter than its diff:
```python
import math

import jax
import jax.numpy as jnp
import numpy as np
from jax import lax
from jax.sharding import Mesh
from jax.sharding import PartitionSpec as P

F32 = jnp.float32
BF16 = jnp.bfloat16
SEQ = ("x", "yl")
REP = ("z", "yh", "core")
X, YL, Z, YH, CORE = 4, 2, 4, 2, 2


def tables(length):
    odd = 2 * np.arange(length, dtype=np.int64)[:, None] + 1
    phase = odd * np.arange(length, dtype=np.int64)[None, :] % (4 * length)
    angle = phase.astype(np.float64) * (math.pi / (2 * length))
    return (np.cos(angle), np.sin(angle))


def dot(a, b, dims=((1,), (0,))):
    return lax.dot_general(a, b, (dims, ((), ())), preferred_element_type=F32)


def up(x, axis):
    n = lax.axis_size(axis)
    return lax.ppermute(x, axis, [(i, (i + 1) % n) for i in range(n)])


def down(x, axis):
    n = lax.axis_size(axis)
    return lax.ppermute(x, axis, [(i, (i - 1) % n) for i in range(n)])


def swap(x, axis):
    return lax.ppermute(x, axis, [(0, 1), (1, 0)])


def pick(x, index, axis=0):
    return lax.dynamic_index_in_dim(x, index, axis, keepdims=False)


def ring_gather(block, axis):
    lower = up(block, axis)
    upper = down(block, axis)
    half = block.shape[0] // 2
    far = jnp.concatenate([up(lower[:half], axis), down(upper[half:], axis)], axis=0)
    return [block, upper, far, lower]


def ring_reduce(part, axis):
    far = part(2).astype(BF16)
    half = far.shape[0] // 2
    from_below = up(far[:half], axis).astype(F32)
    from_above = down(far[half:], axis).astype(F32)
    zero = jnp.zeros_like(from_below)
    one = (part(1) + jnp.concatenate([from_below, zero], axis=0)).astype(BF16)
    three = (part(3) + jnp.concatenate([zero, from_above], axis=0)).astype(BF16)
    lower = up(one, axis)
    upper = down(three, axis)
    return part(0) + lower.astype(F32) + upper.astype(F32)


def local(activations, gate_values, in_weight, long_filter, out_cotangent):
    tokens = activations[0]
    gates = gate_values[0].astype(F32)
    upstream = out_cotangent[0].astype(F32)
    groups = X * YL
    replicas = Z * YH * CORE
    block, channels = gates.shape
    features = tokens.shape[1]
    length = block * groups
    part = channels // groups
    rows = in_weight.shape[0]
    taps_rows = block // replicas
    own_rows = rows + taps_rows
    cut = features * 5 // 8
    xi, yi, zi, hi, ci = (lax.axis_index(a) for a in SEQ + REP)
    rep = (zi * YH + hi) * CORE + ci

    cosine, sine = tables(length)
    cos_t = jnp.asarray(cosine.astype(np.float32)).astype(BF16)
    sin_t = jnp.asarray(sine.astype(np.float32)).astype(BF16)

    def spectrum(x):
        return (dot(cos_t, x), dot(sin_t, x))

    def inverse(real, imag):
        return (
            dot(cos_t, real.astype(BF16), ((0,), (0,))) + dot(sin_t, imag.astype(BF16), ((0,), (0,)))
        ) * (1.0 / length)

    early = ring_gather(tokens[:, cut:], "x")
    other = swap(tokens[:, :cut], "yl")
    pair = jnp.where(yi == 0, jnp.concatenate([tokens[:, :cut], other]), jnp.concatenate([other, tokens[:, :cut]]))
    late = ring_gather(pair, "x")
    early_other = swap(jnp.stack(early), "yl")
    acts = jnp.zeros((X, YL, block, features), BF16)
    for k in range(X):
        owner = (xi + k) % X
        acts = lax.dynamic_update_slice(acts, late[k].reshape(1, YL, block, cut), (owner, 0, 0, 0))
        acts = lax.dynamic_update_slice(acts, early[k][None, None], (owner, yi, 0, cut))
        acts = lax.dynamic_update_slice(acts, early_other[k][None, None], (owner, 1 - yi, 0, cut))
    acts = acts.reshape(length, features)

    inner = (upstream * gates).astype(BF16)
    own_taps = lax.dynamic_slice_in_dim(long_filter, rep * taps_rows, taps_rows, 0)
    sent = jnp.concatenate([inner, in_weight, own_taps], axis=0)
    sent = sent.reshape(block + own_rows, groups, part).transpose(1, 0, 2)
    got = lax.all_to_all(sent, SEQ, 0, 0, tiled=True)
    inner = got[:, :block].reshape(length, part)
    piece = got[:, block:]
    other = swap(piece, "yh")
    piece = jnp.where(hi == 0, jnp.stack([piece, other]), jnp.stack([other, piece]))
    ring = ring_gather(piece.reshape(YH * groups, own_rows, part), "z")
    slab = jnp.zeros((Z, YH * groups, own_rows, part), BF16)
    for k in range(Z):
        slab = lax.dynamic_update_slice(slab, ring[k][None], ((zi + k) % Z, 0, 0, 0))
    other = swap(slab, "core")
    slab = jnp.where(ci == 0, jnp.stack([slab, other]), jnp.stack([other, slab]))
    slab = slab.reshape(CORE, Z, YH, groups, own_rows, part).transpose(3, 1, 2, 0, 4, 5)
    weight = slab[..., :rows, :].reshape(features, part)
    taps = slab[..., rows:, :].reshape(length, part)

    f_c, f_s = spectrum(taps)
    i_c, i_s = spectrum(inner)
    value_grad = inverse(f_c * i_c + f_s * i_s, f_c * i_s - f_s * i_c).astype(BF16)

    grad = value_grad.reshape(X, YL, block, part)

    def late_part(k):
        return dot(pick(grad, (xi + k) % X).reshape(YL * block, part), weight[:cut], ((1,), (1,)))

    mine = pick(grad, yi, 1).reshape(X * block, part)
    theirs = pick(grad, 1 - yi, 1).reshape(X * block, part)
    crossed = swap(dot(theirs, weight[cut:], ((1,), (1,))).astype(BF16), "yl")
    late_sum = ring_reduce(late_part, "x").reshape(YL, block, cut)
    late_other = swap(pick(late_sum, 1 - yi).astype(BF16), "yl")
    late_sum = pick(late_sum, yi) + late_other.astype(F32)
    crossed = (dot(mine, weight[cut:], ((1,), (1,))) + crossed.astype(F32)).reshape(X, block, features - cut)
    early_sum = ring_reduce(lambda k: pick(crossed, (xi + k) % X), "x")
    input_grad = jnp.concatenate([late_sum, early_sum], axis=1).astype(BF16)

    values = dot(acts, weight).astype(BF16)
    v_c, v_s = spectrum(values)
    conv = inverse(f_c * v_c - f_s * v_s, f_c * v_s + f_s * v_c)
    conv = lax.all_to_all(conv.astype(BF16).reshape(groups, block, part), SEQ, 0, 0, tiled=True)
    conv = conv.transpose(1, 0, 2).reshape(block, channels).astype(F32)
    mixed_out = (gates * conv).astype(BF16)
    gate_grad = (upstream * conv).astype(BF16)

    scale = 1.0 / math.sqrt(length * replicas)
    filter_part = inverse(v_c * i_c + v_s * i_s, v_c * i_s - v_s * i_c) * scale
    weight_part = dot(acts, value_grad, ((0,), (0,))) * scale
    owned = jnp.concatenate(
        [
            weight_part.reshape(groups, Z, YH, CORE, rows, part),
            filter_part.reshape(groups, Z, YH, CORE, taps_rows, part),
        ],
        axis=4,
    )
    other = swap(pick(owned, 1 - ci, 3).astype(BF16), "core")
    owned = pick(owned, ci, 3) + other.astype(F32)
    owned = ring_reduce(lambda k: pick(owned, (zi + k) % Z, 1), "z")
    owned = lax.all_to_all(owned.reshape(groups * YH, own_rows, part), SEQ + ("yh",), 0, 0, tiled=True)
    owned = jnp.sum(owned.reshape(groups, YH, own_rows, part), axis=1)
    owned = owned.transpose(1, 0, 2).reshape(own_rows, channels)
    return (mixed_out[None], gate_grad[None], input_grad[None], owned[:rows], owned[rows:])


def solution(mesh):
    mesh = Mesh(mesh.devices.reshape(X, YL, Z, YH, CORE), SEQ + REP)
    split = P(REP, SEQ, None)
    in_specs = (split, split, P(SEQ + REP, None), P(SEQ, None), split)
    out_specs = (split, split, split, P(SEQ + REP, None), P(SEQ + REP, None))
    return jax.shard_map(local, mesh=mesh, in_specs=in_specs, out_specs=out_specs, check_vma=False)
```

time: 227 us -> 203 us (0.89)
  waiting for transfers between devices: 122 us -> 43.6 us
  starting transfers between devices: 17.7 us -> 60.4 us
  local copies, waits for them, and re-layouts: 17.9 us -> 44.3 us
  blocking collectives: 21.7 us -> 0 us
  between operations: 14.4 us -> 1.53 us
  matrix products: 23.6 us -> 34.2 us
  other arithmetic: 7.91 us -> 17.9 us
    all_to_all x4 -> x3, waiting for transfers between devices: 66.2 us -> 10.5 us  [the longest x1 7 us: local(): lax.all_to_all(conv.astype(BF16).reshape(groups, block, part), SEQ, 0, 0,...]
    all_gather x1 -> x0, waiting for transfers between devices: 53.9 us -> none  [local(): weight = lax.all_gather(piece, 'rep', axis=0, tiled=True)]
    ppermute x0 -> x31, starting transfers between devices: none -> 46.2 us  [the longest x12 32.3 us: down(): return lax.ppermute(x, axis, [(i, (i - 1) % n) for i in range(n)])]
    ppermute x0 -> x31, waiting for transfers between devices: none -> 33.2 us  [the longest x12 13.2 us: up(): return lax.ppermute(x, axis, [(i, (i + 1) % n) for i in range(n)])]
    all_to_all x1 -> x0, blocking collectives: 21.7 us -> none  [to_channels(): return lax.all_to_all(x, 'seq', 0, 0, tiled=True)]
    dynamic_update_slice x0 -> x15, local copies, waits for them, and re-layouts: none -> 16.2 us  [the longest x4 6.52 us: local(): lax.dynamic_update_slice(acts, early_other[k][None, None], (owner, 1 - yi...]
    dot_general x15 -> x20, matrix products: 23.6 us -> 34.2 us  [dot(): return lax.dot_general(a, b, (dims, ((), ())), preferred_element_type=F32)]
    slice x4 -> x22, local copies, waits for them, and re-layouts: 2.03 us -> 7.69 us  [the longest x2 1.07 us: late_part(): weight[:cut]]
  transfers between devices with their start and end apart: 6 -> 34, of which waited for: 5 -> 13; matrix products, arithmetic and copies ran while one was open for 17% -> 28% of each run, Pallas kernels for 0% -> 0%
where the time goes in v3:
time: 203 us; the launch traced here: 202 us
  starting transfers between devices  60.4 us (30%)
  local copies, waits for them, and re-layouts  44.3 us (22%)
  waiting for transfers between devices  43.6 us (21%)
  matrix products  34.2 us (17%)
  other arithmetic  17.9 us (9%)
    dot_general x20, matrix products, dot(): return lax.dot_general(a, b, (dims, ((), ())), preferred_element_type=F32)  34.2 us
    ppermute x12, starting transfers between devices, down(): return lax.ppermute(x, axis, [(i, (i - 1) % n) for i in range(n)])  32.3 us
    ppermute x12, waiting for transfers between devices, up(): return lax.ppermute(x, axis, [(i, (i + 1) % n) for i in range(n)])  13.2 us
    ppermute x7, waiting for transfers between devices, swap(): return lax.ppermute(x, axis, [(0, 1), (1, 0)])  11.8 us
    ppermute x12, waiting for transfers between devices, down(): return lax.ppermute(x, axis, [(i, (i - 1) % n) for i in range(n)])  8.12 us
    ppermute x12, starting transfers between devices, up(): return lax.ppermute(x, axis, [(i, (i + 1) % n) for i in range(n)])  7.31 us
    all_to_all x1, waiting for transfers between devices, local(): lax.all_to_all(conv.astype(BF16).reshape(groups, block, part), SEQ, 0, 0,...  7 us
    dynamic_update_slice x4, local copies, waits for them, and re-layouts, local(): lax.dynamic_update_slice(acts, early_other[k][None, None], (owner, 1 - yi...  6.52 us
  transfers between devices with their start and end apart: 34, of which 13 were waited for; matrix products, arithmetic and copies ran while one was open for 28% of the time, Pallas kernels for 0%

profile of v3, /device:TPU:0, one launch (start us, length us, event | category | flops | bytes accessed | tf_op | source)
XLA Modules:
  0.0 201.9 jit_solution(17316056863448232440)
XLA Ops:
  1.7 1.6 collective-permute-start.8
  3.3 1.7 collective-permute-start.7
  6.0 1.7 collective-permute-start.6
  7.7 1.3 fusion.18
  11.2 5.2 %all-to-all-start = ((bf16[8,152,256]{2,1,0:T(8,128)(2,1)}), bf16[8,152,256]{2,1,0:T(8,128)(2,1)S(1)}, u32[]{:S(2)}, u32[]{:S(2)}) async-start(bf16[8,152,256]{2,1,0:T(8,128)(2,1)} %copy.35), calls=%async_computation | async-start | bytes 1245184 | tf_op jit(solution)/shard_map/all_to_all | solution.py:113
  16.5 3.3 %collective-permute-start.10 = (bf16[64,768]{1,0:T(8,128)(2,1)S(1)}, bf16[64,768]{1,0:T(8,128)(2,1)S(1)}, u32[]{:S(2)}, u32[]{:S(2)}) collective-permute-start(bf16[64,768]{1,0:T(8,128)(2,1)S(1)} %slice.151), channel_id=1, source_target_pairs={{0,96},{32,0},{64,32},{96,64},{1,97},{33,1},{65,33},{97,65},{2,98}... | collective-permute-start | bytes 294920 | tf_op jit(solution)/shard_map/ppermute | solution.py:35
  19.8 6.7 %collective-permute-done.10 = bf16[64,768]{1,0:T(8,128)(2,1)S(1)} collective-permute-done((bf16[64,768]{1,0:T(8,128)(2,1)S(1)}, bf16[64,768]{1,0:T(8,128)(2,1)S(1)}, u32[]{:S(2)}, u32[]{:S(2)}) %collective-permute-start.10) | collective-permute-done | bytes 98336 | tf_op jit(solution)/shard_map/ppermute | solution.py:35
  27.6 1.4 collective-permute-start.11
  29.1 1.8 collective-permute-start.12
  31.2 2.5 %broadcast_in_dim.37 = bf16[4,2,128,2048]{3,2,1,0:T(8,128)(2,1)} broadcast(bf16[]{:T(256)} %constant.150.clone.1), dimensions={} | broadcast | bytes 4194306 | tf_op jit(solution)/shard_map/broadcast_in_dim | solution.py:101
  34.7 1.6 bitcast_dynamic-update-slice_fusion.3
  36.3 3.0 %collective-permute-start = (bf16[8,24,256]{2,1,0:T(8,128)(2,1)S(1)}, bf16[8,24,256]{2,1,0:T(8,128)(2,1)S(1)}, u32[]{:S(2)}, u32[]{:S(2)}) collective-permute-start(bf16[8,24,256]{2,1,0:T(8,128)(2,1)S(1)} %get-tuple-element.14), channel_id=1, source_target_pairs={{0,2},{2,0},{1,3},{3,1},{4,6},{6,4},{5,7},{7,5},{8,10},{10,8},{9,1... | collective-permute-start | bytes 294920 | tf_op jit(solution)/shard_map/ppermute | solution.py:39
  40.1 9.0 %collective-permute-done = bf16[8,24,256]{2,1,0:T(8,128)(2,1)S(1)} collective-permute-done((bf16[8,24,256]{2,1,0:T(8,128)(2,1)S(1)}, bf16[8,24,256]{2,1,0:T(8,128)(2,1)S(1)}, u32[]{:S(2)}, u32[]{:S(2)}) %collective-permute-start) | collective-permute-done | bytes 98336 | tf_op jit(solution)/shard_map/ppermute | solution.py:39
  49.1 4.1 %collective-permute-start.1 = (bf16[16,24,256]{2,1,0:T(8,128)(2,1)S(1)}, bf16[16,24,256]{2,1,0:T(8,128)(2,1)S(1)}, u32[]{:S(2)}, u32[]{:S(2)}) collective-permute-start(bf16[16,24,256]{2,1,0:T(8,128)(2,1)S(1)} %bitcast.247), channel_id=1, source_target_pairs={{0,12},{4,0},{8,4},{12,8},{1,13},{5,1},{9,5},{13,9},{2,14},{6,2},{... | collective-permute-start | bytes 589832 | tf_op jit(solution)/shard_map/ppermute | solution.py:35
  54.1 7.1 %collective-permute-done.2 = bf16[16,24,256]{2,1,0:T(8,128)(2,1)S(1)} collective-permute-done((bf16[16,24,256]{2,1,0:T(8,128)(2,1)S(1)}, bf16[16,24,256]{2,1,0:T(8,128)(2,1)S(1)}, u32[]{:S(2)}, u32[]{:S(2)}) %collective-permute-start.2) | collective-permute-done | bytes 196640 | tf_op jit(solution)/shard_map/ppermute | solution.py:30
  61.3 3.3 %collective-permute-start.4 = (bf16[8,24,256]{2,1,0:T(8,128)(2,1)S(1)}, bf16[8,24,256]{2,1,0:T(8,128)(2,1)S(1)}, u32[]{:S(2)}, u32[]{:S(2)}) collective-permute-start(bf16[8,24,256]{2,1,0:T(8,128)(2,1)S(1)} %slice.146), channel_id=1, source_target_pairs={{0,12},{4,0},{8,4},{12,8},{1,13},{5,1},{9,5},{13,9},{2,14},{6,2},{... | collective-permute-start | bytes 294920 | tf_op jit(solution)/shard_map/ppermute | solution.py:35
  64.6 2.5 %collective-permute-done.3 = bf16[8,24,256]{2,1,0:T(8,128)(2,1)S(1)} collective-permute-done((bf16[8,24,256]{2,1,0:T(8,128)(2,1)S(1)}, bf16[8,24,256]{2,1,0:T(8,128)(2,1)S(1)}, u32[]{:S(2)}, u32[]{:S(2)}) %collective-permute-start.3) | collective-permute-done | bytes 98336 | tf_op jit(solution)/shard_map/ppermute | solution.py:30
  68.2 1.3 collective-permute-start.14
  70.6 2.2 %collective-permute-start.15 = (bf16[128,1280]{1,0:T(8,128)(2,1)S(1)}, bf16[128,1280]{1,0:T(8,128)(2,1)S(1)}, u32[]{:S(2)}, u32[]{:S(2)}) collective-permute-start(bf16[128,1280]{1,0:T(8,128)(2,1)S(1)} %slice.155), channel_id=1, source_target_pairs={{0,96},{32,0},{64,32},{96,64},{1,97},{33,1},{65,33},{97,65},{2,98}... | collective-permute-start | bytes 983048 | tf_op jit(solution)/shard_map/ppermute | solution.py:35
  72.8 1.6 fusion.35
  74.4 2.0 %constant_dynamic-update-slice_fusion.2 = bf16[4,2,128,2048]{3,2,1,0:T(8,128)(2,1)} fusion(bf16[4,2,128,2048]{3,2,1,0:T(8,128)(2,1)} %fusion.35, bf16[1,2,128,1280]{3,2,1,0:T(8,128)(2,1)} %bitcast.21, s32[]{:T(128)S(6)} %select_n.206), kind=kLoop, calls=%fused_computation.116 | loop fusion | bytes 1310724 | tf_op jit(solution)/shard_map/dynamic_update_slice | solution.py:104
  77.2 1.6 fusion.34
  82.3 1.6 fusion.33
  84.0 2.0 constant_dynamic-update-slice_fusion
  86.7 1.6 fusion.32
  88.8 3.8 %convolution_convert_fusion.2 = bf16[1024,256]{1,0:T(8,128)(2,1)S(1)} fusion(bf16[1024,2048]{1,0:T(8,128)(2,1)} %bitcast.30, bf16[2048,256]{1,0:T(8,128)(2,1)S(1)} %bitcast.242), kind=kOutput, calls=%fused_computation.30 | convolution fusion | flops 1074003968 | bytes 5767168 | tf_op jit(solution)/shard_map/dot_general | solution.py:25
  92.6 1.8 fusion.54
  94.5 1.7 fusion.56
  100.5 5.1 %convolution_multiply_fusion = f32[2048,256]{1,0:T(8,128)} fusion(bf16[1024,2048]{1,0:T(8,128)(2,1)} %bitcast.30, bf16[256,1024]{1,0:T(8,128)(2,1)S(1)} %fusion.11), kind=kOutput, calls=%fused_computation.4 | convolution fusion | flops 1074266112 | bytes 6815744 | tf_op jit(solution)/shard_map/dot_general | solution.py:25
  105.6 2.2 %reshape.206 = bf16[4,2,128,256]{2,1,0,3:T(2,128)(2,1)} reshape(bf16[1024,256]{0,1:T(8,128)(2,1)} %bitcast.236) | data formatting | bytes 1048576 | tf_op jit(solution)/shard_map/reshape | solution.py:132
  107.8 2.3 %constant_dynamic-slice_fusion.4 = (bf16[1,2,128,256]{2,1,0,3:T(2,128)(2,1)}, bf16[1,2,128,256]{2,1,0,3:T(2,128)(2,1)}, bf16[1,2,128,256]{2,1,0,3:T(2,128)(2,1)}, bf16[1,2,128,256]{2,1,0,3:T(2,128)(2,1)}) fusion(bf16[4,2,128,256]{2,1,0,3:T(2,128)(2,1)} %reshape.206, s32[]{:T(128)S(6)} %select_n.206, s32[]{:T(128)S(6)} %select_n.210, s32[]{:T(128)S(6)} %select_n.208, ...), kind=kLoop, calls=%fused_computation.112 | loop fusion | bytes 1048592 | tf_op jit(solution)/shard_map/jit(dynamic_index_in_dim)/dynamic_slice | solution.py:43
  110.2 3.2 %constant_dynamic-slice_fusion = (bf16[4,1,128,256]{2,1,0,3:T(2,128)(2,1)}, bf16[4,1,128,256]{2,1,0,3:T(2,128)(2,1)}) fusion(bf16[4,2,128,256]{2,1,0,3:T(2,128)(2,1)} %reshape.206, s32[]{:T(128)S(6)} %select_n.204, s32[]{:T(128)S(6)} %select_n.203), kind=kLoop, calls=%fused_computation.108 | loop fusion | bytes 1048584 | tf_op jit(solution)/shard_map/jit(dynamic_index_in_dim)/dynamic_slice | solution.py:43
  113.4 1.0 slice.163
  114.5 2.2 %fusion.21 = f32[256,1024]{1,0:T(8,128)S(1)} fusion(bf16[1024,1024]{1,0:T(8,128)(2,1)S(1)} %copy-done.2, f32[256,1024]{1,0:T(8,128)} %fusion.56, f32[256,1024]{1,0:T(8,128)S(1)} %copy-done.12, f32[256,1024]{1,0:T(8,128)S(1)} %copy-done.13, f32[256,1024]{1,0:T(8,128)S(1)} %copy-done.10), kind=kOutput, calls=%fused_computation.54 | convolution fusion | flops 537919488 | bytes 7340032 | tf_op jit(solution)/shard_map/dot_general | solution.py:25
  116.8 1.8 fusion.19
  119.8 2.6 %fusion.16 = bf16[8,4,2,24,256]{4,3,2,1,0:T(8,128)(2,1)} fusion(s32[]{:T(128)S(6)} %select_n.212, f32[8,4,2,2,8,256]{5,4,3,2,1,0:T(8,128)S(1)} %bitcast.215, f32[8,4,2,2,16,256]{5,4,3,2,1,0:T(8,128)} %bitcast.217), kind=kLoop, calls=%fused_computation.41 | loop fusion | flops 1572864 | bytes 3932164 | tf_op jit(solution)/shard_map/convert_element_type | solution.py:165
  124.6 1.2 collective-permute-start.16
  125.8 2.0 %collective-permute-start.18 = (bf16[128,1280]{1,0:T(8,128)(2,1)}, bf16[128,1280]{1,0:T(8,128)(2,1)}, u32[]{:S(2)}, u32[]{:S(2)}) collective-permute-start(bf16[128,1280]{1,0:T(8,128)(2,1)} %get-tuple-element.12), channel_id=1, source_target_pairs={{0,96},{32,0},{64,32},{96,64},{1,97},{33,1},{65,33},{97,65},{2,98}... | collective-permute-start | bytes 983048 | tf_op jit(solution)/shard_map/ppermute | solution.py:35
  127.9 1.9 copy.49
  130.5 2.3 %convolution_convert_fusion.1 = bf16[512,768]{1,0:T(8,128)(2,1)} fusion(bf16[512,256]{1,0:T(8,128)(2,1)} %bitcast.243, bf16[768,256]{1,0:T(8,128)(2,1)S(1)} %bitcast.229), kind=kOutput, calls=%fused_computation.14 | convolution fusion | flops 201719808 | bytes 1441792 | tf_op jit(solution)/shard_map/dot_general | solution.py:25
  132.9 3.2 %fusion.12 = bf16[32,8,8,128]{3,2,1,0:T(8,128)(2,1)} fusion(f32[256,1024]{1,0:T(8,128)} %fusion.19, bf16[1024,1024]{1,0:T(8,128)(2,1)S(1)} %copy-done.5, f32[256,1024]{1,0:T(8,128)S(1)} %copy-done.8, f32[256,1024]{1,0:T(8,128)S(1)} %copy-done.14, f32[256,1024]{1,0:T(8,128)S(1)} %fusion.53, f32[256,1024]{1,0:T(8,128)} %fusion.56), kind=kOutput, calls=%fused_computation.31 | convolution fusion | flops 538705920 | bytes 7864320 | tf_op jit(solution)/shard_map/dot_general | solution.py:25
  137.2 1.1 copy.48
  139.1 4.6 %all-to-all-start.1 = ((bf16[8,128,256]{1,2,0:T(8,128)(2,1)}), bf16[8,128,256]{1,2,0:T(8,128)(2,1)}, u32[]{:S(2)}, u32[]{:S(2)}) async-start(bf16[8,128,256]{1,2,0:T(8,128)(2,1)} %bitcast.209), calls=%async_computation.1 | async-start | bytes 1048576 | tf_op jit(solution)/shard_map/all_to_all | solution.py:150
  143.8 2.2 %add_convert_fusion.1 = bf16[256,1280]{1,0:T(8,128)(2,1)} fusion(bf16[128,1280]{1,0:T(8,128)(2,1)} %collective-permute-done.16, bf16[1280,256]{1,0:T(8,128)(2,1)S(1)} %bitcast.213, bf16[32,8,2,128]{3,2,1,0:T(2,128)(2,1)S(1)} %bitcast.254), kind=kOutput, calls=%fused_computation.27 | convolution fusion | flops 168755200 | bytes 1769472 | tf_op jit(solution)/shard_map/dot_general | solution.py:25
  146.0 2.0 collective-permute-start.17
  148.0 2.2 %add_convert_fusion = bf16[256,1280]{1,0:T(8,128)(2,1)} fusion(bf16[128,1280]{1,0:T(8,128)(2,1)} %collective-permute-done.18, bf16[1280,256]{1,0:T(8,128)(2,1)S(1)} %bitcast.214, bf16[32,8,2,128]{3,2,1,0:T(2,128)(2,1)S(1)} %bitcast.253), kind=kOutput, calls=%fused_computation.26 | convolution fusion | flops 168755200 | bytes 1769472 | tf_op jit(solution)/shard_map/dot_general | solution.py:25
  150.2 1.2 collective-permute-start.19
  151.4 7.0 %all-to-all-done.1 = bf16[8,128,256]{1,2,0:T(8,128)(2,1)} async-done(((bf16[8,128,256]{1,2,0:T(8,128)(2,1)}), bf16[8,128,256]{1,2,0:T(8,128)(2,1)}, u32[]{:S(2)}, u32[]{:S(2)}) %all-to-all-start.1) | async-done | bytes 524320 | tf_op jit(solution)/shard_map/all_to_all | solution.py:150
  158.4 1.1 convert_element_type.217
  159.9 2.6 %fusion.15 = (bf16[1,128,2048]{2,1,0:T(8,128)(2,1)}, bf16[1,128,2048]{2,1,0:T(8,128)(2,1)}) fusion(f32[1,128,2048]{2,1,0:T(8,128)S(1)} %copy.39, bf16[1,128,2048]{2,1,0:T(8,128)(2,1)} %param.11, bf16[1,128,2048]{2,1,0:T(8,128)(2,1)} %param.8), kind=kLoop, calls=%fused_computation.34 | loop fusion | flops 1572864 | bytes 3145728 | tf_op jit(solution)/shard_map/convert_element_type | solution.py:153
  162.5 1.5 fusion.4
  164.0 3.4 %collective-permute-start.29 = (bf16[4,2,24,256]{3,2,1,0:T(8,128)(2,1)S(1)}, bf16[4,2,24,256]{3,2,1,0:T(8,128)(2,1)S(1)}, u32[]{:S(2)}, u32[]{:S(2)}) collective-permute-start(bf16[4,2,24,256]{3,2,1,0:T(8,128)(2,1)S(1)} %slice_bitcast_fusion.5), channel_id=1, source_target_pairs={{0,12},{4,0},{8,4},{12,8},{1,13},{5,1},{9,5},{13,9},{2,14},{6,2},{... | collective-permute-start | bytes 294920 | tf_op jit(solution)/shard_map/ppermute | solution.py:35
  167.6 1.5 convert_add_fusion
  169.6 2.9 %collective-permute-start.24 = (bf16[64,768]{1,0:T(8,128)(2,1)S(1)}, bf16[64,768]{1,0:T(8,128)(2,1)S(1)}, u32[]{:S(2)}, u32[]{:S(2)}) collective-permute-start(bf16[64,768]{1,0:T(8,128)(2,1)S(1)} %get-tuple-element.24), channel_id=1, source_target_pairs={{0,96},{32,0},{64,32},{96,64},{1,97},{33,1},{65,33},{97,65},{2,98}... | collective-permute-start | bytes 294920 | tf_op jit(solution)/shard_map/ppermute | solution.py:35
  173.5 1.5 collective-permute-done.22
  175.1 3.2 %collective-permute-start.30 = (bf16[8,2,24,256]{3,2,1,0:T(8,128)(2,1)S(1)}, bf16[8,2,24,256]{3,2,1,0:T(8,128)(2,1)S(1)}, u32[]{:S(2)}, u32[]{:S(2)}) collective-permute-start(bf16[8,2,24,256]{3,2,1,0:T(8,128)(2,1)S(1)} %get-tuple-element.6), channel_id=1, source_target_pairs={{0,12},{4,0},{8,4},{12,8},{1,13},{5,1},{9,5},{13,9},{2,14},{6,2},{... | collective-permute-start | bytes 589832 | tf_op jit(solution)/shard_map/ppermute | solution.py:35
  179.1 3.2 %collective-permute-start.25 = (bf16[128,768]{1,0:T(8,128)(2,1)}, bf16[128,768]{1,0:T(8,128)(2,1)}, u32[]{:S(2)}, u32[]{:S(2)}) collective-permute-start(bf16[128,768]{1,0:T(8,128)(2,1)} %get-tuple-element.8), channel_id=1, source_target_pairs={{0,96},{32,0},{64,32},{96,64},{1,97},{33,1},{65,33},{97,65},{2,98}... | collective-permute-start | bytes 589832 | tf_op jit(solution)/shard_map/ppermute | solution.py:35
  182.3 1.5 convert_add_fusion.1
  185.8 4.4 %all-to-all-start.2 = ((f32[16,24,256]{2,1,0:T(8,128)}), f32[16,24,256]{2,1,0:T(8,128)}, u32[]{:S(2)}, u32[]{:S(2)}) async-start(f32[16,24,256]{2,1,0:T(8,128)} %bitcast.237), calls=%async_computation.2 | async-start | bytes 786432 | tf_op jit(solution)/shard_map/all_to_all | solution.py:168
  190.2 1.1 fusion.31
  191.3 2.9 %collective-permute-done.20 = bf16[128,1280]{1,0:T(8,128)(2,1)} collective-permute-done((bf16[128,1280]{1,0:T(8,128)(2,1)}, bf16[128,1280]{1,0:T(8,128)(2,1)}, u32[]{:S(2)}, u32[]{:S(2)}) %collective-permute-start.20) | collective-permute-done | bytes 327712 | tf_op jit(solution)/shard_map/ppermute | solution.py:39
  194.2 1.0 fusion.30
  196.0 3.5 %all-to-all-done.2 = f32[16,24,256]{2,1,0:T(8,128)} async-done(((f32[16,24,256]{2,1,0:T(8,128)}), f32[16,24,256]{2,1,0:T(8,128)}, u32[]{:S(2)}, u32[]{:S(2)}) %all-to-all-start.2) | async-done | bytes 393248 | tf_op jit(solution)/shard_map/all_to_all | solution.py:168
  199.5 1.0 bitcast_reduce_fusion
  (189 shorter events, 33.2 us)
Async XLA Ops:
  0.6 8.4 %copy-start = (bf16[128,2048]{1,0:T(8,128)(2,1)S(1)}, bf16[128,2048]{1,0:T(8,128)(2,1)}, u32[]{:S(2)}) copy-start(bf16[128,2048]{1,0:T(8,128)(2,1)} %param.10) | copy-start | bytes 1572868
  0.6 9.4 %copy-start.42 = (bf16[16,2048]{1,0:T(8,128)(2,1)S(1)}, bf16[16,2048]{1,0:T(8,128)(2,1)}, u32[]{:S(2)}) copy-start(bf16[16,2048]{1,0:T(8,128)(2,1)} %param.9) | copy-start | bytes 196612
  1.7 7.8 %collective-permute-start.8 = (bf16[128,768]{1,0:T(8,128)(2,1)S(1)}, bf16[128,768]{1,0:T(8,128)(2,1)S(1)}, u32[]{:S(2)}, u32[]{:S(2)}) collective-permute-start(bf16[128,768]{1,0:T(8,128)(2,1)S(1)} %get-tuple-element.22), channel_id=1, source_target_pairs={{0,32},{32,64},{64,96},{96,0},{1,33},{33,65},{65,97},{97,1},{2,34}... | collective-permute-start | bytes 589832 | tf_op jit(solution)/shard_map/ppermute | solution.py:30
  3.3 13.2 %collective-permute-start.7 = (bf16[128,768]{1,0:T(8,128)(2,1)S(1)}, bf16[128,768]{1,0:T(8,128)(2,1)S(1)}, u32[]{:S(2)}, u32[]{:S(2)}) collective-permute-start(bf16[128,768]{1,0:T(8,128)(2,1)S(1)} %get-tuple-element.22), channel_id=1, source_target_pairs={{0,96},{32,0},{64,32},{96,64},{1,97},{33,1},{65,33},{97,65},{2,98}... | collective-permute-start | bytes 589832 | tf_op jit(solution)/shard_map/ppermute | solution.py:35
  6.0 23.0 %collective-permute-start.6 = (bf16[128,1280]{1,0:T(8,128)(2,1)S(1)}, bf16[128,1280]{1,0:T(8,128)(2,1)S(1)}, u32[]{:S(2)}, u32[]{:S(2)}) collective-permute-start(bf16[128,1280]{1,0:T(8,128)(2,1)S(1)} %slice.148), channel_id=1, source_target_pairs={{0,16},{16,0},{1,17},{17,1},{2,18},{18,2},{3,19},{19,3},{4,20},{20... | collective-permute-start | bytes 983048 | tf_op jit(solution)/shard_map/ppermute | solution.py:39
  9.5 17.1 %copy-start.31 = (bf16[128,768]{1,0:T(8,128)(2,1)}, bf16[128,768]{1,0:T(8,128)(2,1)S(1)}, u32[]{:S(2)}) copy-start(bf16[128,768]{1,0:T(8,128)(2,1)S(1)} %collective-permute-done.8) | copy-start | bytes 589828
  9.5 10.3 %collective-permute-start.9 = (bf16[64,768]{1,0:T(8,128)(2,1)S(1)}, bf16[64,768]{1,0:T(8,128)(2,1)S(1)}, u32[]{:S(2)}, u32[]{:S(2)}) collective-permute-start(bf16[64,768]{1,0:T(8,128)(2,1)S(1)} %slice.150), channel_id=1, source_target_pairs={{0,32},{32,64},{64,96},{96,0},{1,33},{33,65},{65,97},{97,1},{2,34}... | collective-permute-start | bytes 294920 | tf_op jit(solution)/shard_map/ppermute | solution.py:30
  11.2 25.1 %all-to-all-start = ((bf16[8,152,256]{2,1,0:T(8,128)(2,1)}), bf16[8,152,256]{2,1,0:T(8,128)(2,1)S(1)}, u32[]{:S(2)}, u32[]{:S(2)}) async-start(bf16[8,152,256]{2,1,0:T(8,128)(2,1)} %copy.35), calls=%async_computation | async-start | bytes 1245184 | tf_op jit(solution)/shard_map/all_to_all | solution.py:113
  16.5 14.7 %copy-start.33 = (bf16[128,768]{1,0:T(8,128)(2,1)}, bf16[128,768]{1,0:T(8,128)(2,1)S(1)}, u32[]{:S(2)}) copy-start(bf16[128,768]{1,0:T(8,128)(2,1)S(1)} %collective-permute-done.7) | copy-start | bytes 589828
  16.5 10.0 %collective-permute-start.10 = (bf16[64,768]{1,0:T(8,128)(2,1)S(1)}, bf16[64,768]{1,0:T(8,128)(2,1)S(1)}, u32[]{:S(2)}, u32[]{:S(2)}) collective-permute-start(bf16[64,768]{1,0:T(8,128)(2,1)S(1)} %slice.151), channel_id=1, source_target_pairs={{0,96},{32,0},{64,32},{96,64},{1,97},{33,1},{65,33},{97,65},{2,98}... | collective-permute-start | bytes 294920 | tf_op jit(solution)/shard_map/ppermute | solution.py:35
  26.6 4.7 %copy-start.35 = (bf16[128,768]{1,0:T(8,128)(2,1)}, bf16[128,768]{1,0:T(8,128)(2,1)S(1)}, u32[]{:S(2)}) copy-start(bf16[128,768]{1,0:T(8,128)(2,1)S(1)} %constant_dynamic-update-slice_fusion.4) | copy-start | bytes 589828
  27.6 45.2 %collective-permute-start.11 = (bf16[4,128,768]{2,1,0:T(8,128)(2,1)}, bf16[4,128,768]{2,1,0:T(8,128)(2,1)}, u32[]{:S(2)}, u32[]{:S(2)}) collective-permute-start(bf16[4,128,768]{2,1,0:T(8,128)(2,1)} %pad_maximum_fusion), channel_id=1, source_target_pairs={{0,16},{16,0},{1,17},{17,1},{2,18},{18,2},{3,19},{19,3},{4,20},{20... | collective-permute-start | bytes 2359304 | tf_op jit(solution)/shard_map/ppermute | solution.py:39
  29.1 40.4 %collective-permute-start.12 = (bf16[256,1280]{1,0:T(8,128)(2,1)S(1)}, bf16[256,1280]{1,0:T(8,128)(2,1)}, u32[]{:S(2)}, u32[]{:S(2)}) collective-permute-start(bf16[256,1280]{1,0:T(8,128)(2,1)S(1)} %maximum_select_fusion.1), channel_id=1, source_target_pairs={{0,96},{32,0},{64,32},{96,64},{1,97},{33,1},{65,33},{97,65},{2,98}... | collective-permute-start | bytes 1966088 | tf_op jit(solution)/shard_map/ppermute | solution.py:35
  30.9 36.3 %collective-permute-start.13 = (bf16[256,1280]{1,0:T(8,128)(2,1)S(1)}, bf16[256,1280]{1,0:T(8,128)(2,1)}, u32[]{:S(2)}, u32[]{:S(2)}) collective-permute-start(bf16[256,1280]{1,0:T(8,128)(2,1)S(1)} %maximum_select_fusion.1), channel_id=1, source_target_pairs={{0,32},{32,64},{64,96},{96,0},{1,33},{33,65},{65,97},{97,1},{2,34}... | collective-permute-start | bytes 1966088 | tf_op jit(solution)/shard_map/ppermute | solution.py:30
  33.8 5.6 %copy-start.2 = (bf16[1024,1024]{1,0:T(8,128)(2,1)S(1)}, bf16[1024,1024]{1,0:T(8,128)(2,1)}, u32[]{:S(2)}) copy-start(bf16[1024,1024]{1,0:T(8,128)(2,1)} %constant.184) | copy-start | bytes 6291460
  36.3 12.8 %collective-permute-start = (bf16[8,24,256]{2,1,0:T(8,128)(2,1)S(1)}, bf16[8,24,256]{2,1,0:T(8,128)(2,1)S(1)}, u32[]{:S(2)}, u32[]{:S(2)}) collective-permute-start(bf16[8,24,256]{2,1,0:T(8,128)(2,1)S(1)} %get-tuple-element.14), channel_id=1, source_target_pairs={{0,2},{2,0},{1,3},{3,1},{4,6},{6,4},{5,7},{7,5},{8,10},{10,8},{9,1... | collective-permute-start | bytes 294920 | tf_op jit(solution)/shard_map/ppermute | solution.py:39
  39.3 13.9 %copy-start.3 = (bf16[1024,1024]{1,0:T(8,128)(2,1)S(1)}, bf16[1024,1024]{1,0:T(8,128)(2,1)}, u32[]{:S(2)}) copy-start(bf16[1024,1024]{1,0:T(8,128)(2,1)} %constant.185) | copy-start | bytes 6291460
  40.1 59.5 %copy-start.9 = (f32[256,1024]{1,0:T(8,128)}, f32[256,1024]{1,0:T(8,128)S(1)}, u32[]{:S(2)}) copy-start(f32[256,1024]{1,0:T(8,128)S(1)} %fusion.57) | copy-start | bytes 3145732
  49.1 12.1 %collective-permute-start.1 = (bf16[16,24,256]{2,1,0:T(8,128)(2,1)S(1)}, bf16[16,24,256]{2,1,0:T(8,128)(2,1)S(1)}, u32[]{:S(2)}, u32[]{:S(2)}) collective-permute-start(bf16[16,24,256]{2,1,0:T(8,128)(2,1)S(1)} %bitcast.247), channel_id=1, source_target_pairs={{0,12},{4,0},{8,4},{12,8},{1,13},{5,1},{9,5},{13,9},{2,14},{6,2},{... | collective-permute-start | bytes 589832 | tf_op jit(solution)/shard_map/ppermute | solution.py:35
  53.2 7.9 %collective-permute-start.2 = (bf16[16,24,256]{2,1,0:T(8,128)(2,1)S(1)}, bf16[16,24,256]{2,1,0:T(8,128)(2,1)S(1)}, u32[]{:S(2)}, u32[]{:S(2)}) collective-permute-start(bf16[16,24,256]{2,1,0:T(8,128)(2,1)S(1)} %bitcast.248), channel_id=1, source_target_pairs={{0,4},{4,8},{8,12},{12,0},{1,5},{5,9},{9,13},{13,1},{2,6},{6,10},{... | collective-permute-start | bytes 589832 | tf_op jit(solution)/shard_map/ppermute | solution.py:30
  54.0 45.7 %copy-start.11 = (f32[256,1024]{1,0:T(8,128)}, f32[256,1024]{1,0:T(8,128)S(1)}, u32[]{:S(2)}) copy-start(f32[256,1024]{1,0:T(8,128)S(1)} %fusion.58) | copy-start | bytes 3145732
  61.2 5.9 %collective-permute-start.3 = (bf16[8,24,256]{2,1,0:T(8,128)(2,1)S(1)}, bf16[8,24,256]{2,1,0:T(8,128)(2,1)S(1)}, u32[]{:S(2)}, u32[]{:S(2)}) collective-permute-start(bf16[8,24,256]{2,1,0:T(8,128)(2,1)S(1)} %slice.145), channel_id=1, source_target_pairs={{0,4},{4,8},{8,12},{12,0},{1,5},{5,9},{9,13},{13,1},{2,6},{6,10},{... | collective-permute-start | bytes 294920 | tf_op jit(solution)/shard_map/ppermute | solution.py:30
  61.3 15.2 %copy-start.34 = (bf16[128,768]{1,0:T(8,128)(2,1)S(1)}, bf16[128,768]{1,0:T(8,128)(2,1)}, u32[]{:S(2)}) copy-start(bf16[128,768]{1,0:T(8,128)(2,1)} %copy-done.33) | copy-start | bytes 589828
  61.3 5.8 %collective-permute-start.4 = (bf16[8,24,256]{2,1,0:T(8,128)(2,1)S(1)}, bf16[8,24,256]{2,1,0:T(8,128)(2,1)S(1)}, u32[]{:S(2)}, u32[]{:S(2)}) collective-permute-start(bf16[8,24,256]{2,1,0:T(8,128)(2,1)S(1)} %slice.146), channel_id=1, source_target_pairs={{0,12},{4,0},{8,4},{12,8},{1,13},{5,1},{9,5},{13,9},{2,14},{6,2},{... | collective-permute-start | bytes 294920 | tf_op jit(solution)/shard_map/ppermute | solution.py:35
  67.1 21.2 %collective-permute-start.5 = (bf16[4,16,24,256]{3,2,1,0:T(8,128)(2,1)S(1)}, bf16[4,16,24,256]{3,2,1,0:T(8,128)(2,1)S(1)}, u32[]{:S(2)}, u32[]{:S(2)}) collective-permute-start(bf16[4,16,24,256]{3,2,1,0:T(8,128)(2,1)S(1)} %bitcast_dynamic-update-slice_fusion.4), channel_id=1, source_target_pairs={{0,1},{1,0},{2,3},{3,2},{4,5},{5,4},{6,7},{7,6},{8,9},{9,8},{10,11... | collective-permute-start | bytes 2359304 | tf_op jit(solution)/shard_map/ppermute | solution.py:39
  68.2 11.4 %collective-permute-start.14 = (bf16[128,1280]{1,0:T(8,128)(2,1)S(1)}, bf16[128,1280]{1,0:T(8,128)(2,1)S(1)}, u32[]{:S(2)}, u32[]{:S(2)}) collective-permute-start(bf16[128,1280]{1,0:T(8,128)(2,1)S(1)} %slice.154), channel_id=1, source_target_pairs={{0,32},{32,64},{64,96},{96,0},{1,33},{33,65},{65,97},{97,1},{2,34}... | collective-permute-start | bytes 983048 | tf_op jit(solution)/shard_map/ppermute | solution.py:30
  70.6 10.1 %collective-permute-start.15 = (bf16[128,1280]{1,0:T(8,128)(2,1)S(1)}, bf16[128,1280]{1,0:T(8,128)(2,1)S(1)}, u32[]{:S(2)}, u32[]{:S(2)}) collective-permute-start(bf16[128,1280]{1,0:T(8,128)(2,1)S(1)} %slice.155), channel_id=1, source_target_pairs={{0,96},{32,0},{64,32},{96,64},{1,97},{33,1},{65,33},{97,65},{2,98}... | collective-permute-start | bytes 983048 | tf_op jit(solution)/shard_map/ppermute | solution.py:35
  74.4 7.2 %copy-start.36 = (bf16[128,768]{1,0:T(8,128)(2,1)S(1)}, bf16[128,768]{1,0:T(8,128)(2,1)}, u32[]{:S(2)}) copy-start(bf16[128,768]{1,0:T(8,128)(2,1)} %copy-done.35) | copy-start | bytes 589828
  78.8 7.2 %copy-start.32 = (bf16[128,768]{1,0:T(8,128)(2,1)S(1)}, bf16[128,768]{1,0:T(8,128)(2,1)}, u32[]{:S(2)}) copy-start(bf16[128,768]{1,0:T(8,128)(2,1)} %copy-done.31) | copy-start | bytes 589828
  88.6 9.2 %copy-start.19 = (bf16[8,4,2,2,24,256]{5,4,0,2,1,3:T(8,128)(2,1)}, bf16[8,4,2,2,24,256]{5,4,0,2,1,3:T(8,128)(2,1)S(1)}, u32[]{:S(2)}) copy-start(bf16[8,4,2,2,24,256]{5,4,0,2,1,3:T(8,128)(2,1)S(1)} %fusion.5) | copy-start | bytes 4718596
  100.5 5.1 %copy-start.30 = (bf16[256,1024]{1,0:T(8,128)(2,1)}, bf16[256,1024]{1,0:T(8,128)(2,1)S(1)}, u32[]{:S(2)}) copy-start(bf16[256,1024]{1,0:T(8,128)(2,1)S(1)} %fusion.11) | copy-start | bytes 1572868
  107.8 6.6 %copy-start.10 = (f32[256,1024]{1,0:T(8,128)S(1)}, f32[256,1024]{1,0:T(8,128)}, u32[]{:S(2)}) copy-start(f32[256,1024]{1,0:T(8,128)} %copy-done.9) | copy-start | bytes 3145732
  107.8 6.6 %copy-start.12 = (f32[256,1024]{1,0:T(8,128)S(1)}, f32[256,1024]{1,0:T(8,128)}, u32[]{:S(2)}) copy-start(f32[256,1024]{1,0:T(8,128)} %copy-done.11) | copy-start | bytes 3145732
  107.8 6.6 %copy-start.13 = (f32[256,1024]{1,0:T(8,128)S(1)}, f32[256,1024]{1,0:T(8,128)}, u32[]{:S(2)}) copy-start(f32[256,1024]{1,0:T(8,128)} %fusion.54) | copy-start | bytes 3145732
  119.8 3.6 %copy-start.41 = (bf16[1,2,128,256]{2,1,0,3:T(2,128)(2,1)S(1)}, bf16[1,2,128,256]{2,1,0,3:T(2,128)(2,1)}, u32[]{:S(2)}) copy-start(bf16[1,2,128,256]{2,1,0,3:T(2,128)(2,1)} %get-tuple-element.17) | copy-start | bytes 393220
  122.4 40.1 %collective-permute-start.26 = (bf16[8,4,2,24,256]{4,3,2,1,0:T(8,128)(2,1)}, bf16[8,4,2,24,256]{4,3,2,1,0:T(8,128)(2,1)}, u32[]{:S(2)}, u32[]{:S(2)}) collective-permute-start(bf16[8,4,2,24,256]{4,3,2,1,0:T(8,128)(2,1)} %fusion.16), channel_id=1, source_target_pairs={{0,1},{1,0},{2,3},{3,2},{4,5},{5,4},{6,7},{7,6},{8,9},{9,8},{10,11... | collective-permute-start | bytes 2359304 | tf_op jit(solution)/shard_map/ppermute | solution.py:39
  123.7 9.1 %copy-start.5 = (bf16[1024,1024]{1,0:T(8,128)(2,1)S(1)}, bf16[1024,1024]{1,0:T(8,128)(2,1)}, u32[]{:S(2)}) copy-start(bf16[1024,1024]{1,0:T(8,128)(2,1)} %constant.185) | copy-start | bytes 6291460
  124.6 19.1 %collective-permute-start.16 = (bf16[128,1280]{1,0:T(8,128)(2,1)}, bf16[128,1280]{1,0:T(8,128)(2,1)}, u32[]{:S(2)}, u32[]{:S(2)}) collective-permute-start(bf16[128,1280]{1,0:T(8,128)(2,1)} %get-tuple-element.11), channel_id=1, source_target_pairs={{0,32},{32,64},{64,96},{96,0},{1,33},{33,65},{65,97},{97,1},{2,34}... | collective-permute-start | bytes 983048 | tf_op jit(solution)/shard_map/ppermute | solution.py:30
  125.8 22.1 %collective-permute-start.18 = (bf16[128,1280]{1,0:T(8,128)(2,1)}, bf16[128,1280]{1,0:T(8,128)(2,1)}, u32[]{:S(2)}, u32[]{:S(2)}) collective-permute-start(bf16[128,1280]{1,0:T(8,128)(2,1)} %get-tuple-element.12), channel_id=1, source_target_pairs={{0,96},{32,0},{64,32},{96,64},{1,97},{33,1},{65,33},{97,65},{2,98}... | collective-permute-start | bytes 983048 | tf_op jit(solution)/shard_map/ppermute | solution.py:35
  129.7 3.1 %copy-start.8 = (f32[256,1024]{1,0:T(8,128)S(1)}, f32[256,1024]{1,0:T(8,128)}, u32[]{:S(2)}) copy-start(f32[256,1024]{1,0:T(8,128)} %copy-done.6) | copy-start | bytes 3145732
  129.7 3.1 %copy-start.14 = (f32[256,1024]{1,0:T(8,128)S(1)}, f32[256,1024]{1,0:T(8,128)}, u32[]{:S(2)}) copy-start(f32[256,1024]{1,0:T(8,128)} %fusion.54) | copy-start | bytes 3145732
  132.8 3.3 %copy-start.17 = (bf16[5,4,2,2,16,256]{5,4,3,2,1,0:T(8,128)(2,1)S(1)}, bf16[5,4,2,2,16,256]{5,4,3,2,1,0:T(8,128)(2,1)}, u32[]{:S(2)}) copy-start(bf16[5,4,2,2,16,256]{5,4,3,2,1,0:T(8,128)(2,1)} %copy-done.16) | copy-start | bytes 1966084
  132.8 3.3 %copy-start.40 = (bf16[1,2,128,256]{2,1,0,3:T(2,128)(2,1)S(1)}, bf16[1,2,128,256]{2,1,0,3:T(2,128)(2,1)}, u32[]{:S(2)}) copy-start(bf16[1,2,128,256]{2,1,0,3:T(2,128)(2,1)} %get-tuple-element.18) | copy-start | bytes 393220
  132.8 34.7 %collective-permute-start.21 = (bf16[512,768]{1,0:T(8,128)(2,1)}, bf16[512,768]{1,0:T(8,128)(2,1)}, u32[]{:S(2)}, u32[]{:S(2)}) collective-permute-start(bf16[512,768]{1,0:T(8,128)(2,1)} %convolution_convert_fusion.1), channel_id=1, source_target_pairs={{0,16},{16,0},{1,17},{17,1},{2,18},{18,2},{3,19},{19,3},{4,20},{20... | collective-permute-start | bytes 2359304 | tf_op jit(solution)/shard_map/ppermute | solution.py:39
  136.1 7.6 %copy-start.18 = (bf16[5,4,2,2,16,256]{5,4,3,2,1,0:T(8,128)(2,1)S(1)}, bf16[5,4,2,2,16,256]{5,4,3,2,1,0:T(8,128)(2,1)}, u32[]{:S(2)}) copy-start(bf16[5,4,2,2,16,256]{5,4,3,2,1,0:T(8,128)(2,1)} %copy-done.16) | copy-start | bytes 1966084
  136.1 7.6 %copy-start.39 = (bf16[1,2,128,256]{2,1,0,3:T(2,128)(2,1)S(1)}, bf16[1,2,128,256]{2,1,0,3:T(2,128)(2,1)}, u32[]{:S(2)}) copy-start(bf16[1,2,128,256]{2,1,0,3:T(2,128)(2,1)} %get-tuple-element.15) | copy-start | bytes 393220
  138.3 9.7 %copy-start.38 = (bf16[1,2,128,256]{2,1,0,3:T(2,128)(2,1)S(1)}, bf16[1,2,128,256]{2,1,0,3:T(2,128)(2,1)}, u32[]{:S(2)}) copy-start(bf16[1,2,128,256]{2,1,0,3:T(2,128)(2,1)} %get-tuple-element.16) | copy-start | bytes 393220
  139.1 19.2 %all-to-all-start.1 = ((bf16[8,128,256]{1,2,0:T(8,128)(2,1)}), bf16[8,128,256]{1,2,0:T(8,128)(2,1)}, u32[]{:S(2)}, u32[]{:S(2)}) async-start(bf16[8,128,256]{1,2,0:T(8,128)(2,1)} %bitcast.209), calls=%async_computation.1 | async-start | bytes 1048576 | tf_op jit(solution)/shard_map/all_to_all | solution.py:150
  146.0 33.1 %collective-permute-start.17 = (bf16[256,1280]{1,0:T(8,128)(2,1)}, bf16[256,1280]{1,0:T(8,128)(2,1)}, u32[]{:S(2)}, u32[]{:S(2)}) collective-permute-start(bf16[256,1280]{1,0:T(8,128)(2,1)} %add_convert_fusion.1), channel_id=1, source_target_pairs={{0,32},{32,64},{64,96},{96,0},{1,33},{33,65},{65,97},{97,1},{2,34}... | collective-permute-start | bytes 1966088 | tf_op jit(solution)/shard_map/ppermute | solution.py:30
  150.2 32.2 %collective-permute-start.19 = (bf16[256,1280]{1,0:T(8,128)(2,1)}, bf16[256,1280]{1,0:T(8,128)(2,1)}, u32[]{:S(2)}, u32[]{:S(2)}) collective-permute-start(bf16[256,1280]{1,0:T(8,128)(2,1)} %add_convert_fusion), channel_id=1, source_target_pairs={{0,96},{32,0},{64,32},{96,64},{1,97},{33,1},{65,33},{97,65},{2,98}... | collective-permute-start | bytes 1966088 | tf_op jit(solution)/shard_map/ppermute | solution.py:35
  162.5 5.1 %copy-start.26 = (bf16[3,4,2,2,16,256]{5,4,3,2,1,0:T(8,128)(2,1)S(1)}, bf16[3,4,2,2,16,256]{5,4,3,2,1,0:T(8,128)(2,1)}, u32[]{:S(2)}) copy-start(bf16[3,4,2,2,16,256]{5,4,3,2,1,0:T(8,128)(2,1)} %copy-done.25) | copy-start | bytes 1179652
  162.5 5.1 %copy-start.37 = (bf16[4,1,128,256]{3,2,0,1:T(8,128)(2,1)S(1)}, bf16[4,1,128,256]{3,2,0,1:T(8,128)(2,1)}, u32[]{:S(2)}) copy-start(bf16[4,1,128,256]{3,2,0,1:T(8,128)(2,1)} %copy.48) | copy-start | bytes 786436
  164.0 5.6 %collective-permute-start.29 = (bf16[4,2,24,256]{3,2,1,0:T(8,128)(2,1)S(1)}, bf16[4,2,24,256]{3,2,1,0:T(8,128)(2,1)S(1)}, u32[]{:S(2)}, u32[]{:S(2)}) collective-permute-start(bf16[4,2,24,256]{3,2,1,0:T(8,128)(2,1)S(1)} %slice_bitcast_fusion.5), channel_id=1, source_target_pairs={{0,12},{4,0},{8,4},{12,8},{1,13},{5,1},{9,5},{13,9},{2,14},{6,2},{... | collective-permute-start | bytes 294920 | tf_op jit(solution)/shard_map/ppermute | solution.py:35
  167.5 5.9 %collective-permute-start.27 = (bf16[4,2,24,256]{3,2,1,0:T(8,128)(2,1)S(1)}, bf16[4,2,24,256]{3,2,1,0:T(8,128)(2,1)S(1)}, u32[]{:S(2)}, u32[]{:S(2)}) collective-permute-start(bf16[4,2,24,256]{3,2,1,0:T(8,128)(2,1)S(1)} %slice_bitcast_fusion.6), channel_id=1, source_target_pairs={{0,4},{4,8},{8,12},{12,0},{1,5},{5,9},{9,13},{13,1},{2,6},{6,10},{... | collective-permute-start | bytes 294920 | tf_op jit(solution)/shard_map/ppermute | solution.py:30
  169.2 5.9 %collective-permute-start.22 = (bf16[64,768]{1,0:T(8,128)(2,1)S(1)}, bf16[64,768]{1,0:T(8,128)(2,1)S(1)}, u32[]{:S(2)}, u32[]{:S(2)}) collective-permute-start(bf16[64,768]{1,0:T(8,128)(2,1)S(1)} %get-tuple-element.23), channel_id=1, source_target_pairs={{0,32},{32,64},{64,96},{96,0},{1,33},{33,65},{65,97},{97,1},{2,34}... | collective-permute-start | bytes 294920 | tf_op jit(solution)/shard_map/ppermute | solution.py:30
  169.6 8.6 %collective-permute-start.24 = (bf16[64,768]{1,0:T(8,128)(2,1)S(1)}, bf16[64,768]{1,0:T(8,128)(2,1)S(1)}, u32[]{:S(2)}, u32[]{:S(2)}) collective-permute-start(bf16[64,768]{1,0:T(8,128)(2,1)S(1)} %get-tuple-element.24), channel_id=1, source_target_pairs={{0,96},{32,0},{64,32},{96,64},{1,97},{33,1},{65,33},{97,65},{2,98}... | collective-permute-start | bytes 294920 | tf_op jit(solution)/shard_map/ppermute | solution.py:35
  173.5 11.5 %collective-permute-start.28 = (bf16[8,2,24,256]{3,2,1,0:T(8,128)(2,1)S(1)}, bf16[8,2,24,256]{3,2,1,0:T(8,128)(2,1)S(1)}, u32[]{:S(2)}, u32[]{:S(2)}) collective-permute-start(bf16[8,2,24,256]{3,2,1,0:T(8,128)(2,1)S(1)} %get-tuple-element.5), channel_id=1, source_target_pairs={{0,4},{4,8},{8,12},{12,0},{1,5},{5,9},{9,13},{13,1},{2,6},{6,10},{... | collective-permute-start | bytes 589832 | tf_op jit(solution)/shard_map/ppermute | solution.py:30
  175.1 9.9 %collective-permute-start.30 = (bf16[8,2,24,256]{3,2,1,0:T(8,128)(2,1)S(1)}, bf16[8,2,24,256]{3,2,1,0:T(8,128)(2,1)S(1)}, u32[]{:S(2)}, u32[]{:S(2)}) collective-permute-start(bf16[8,2,24,256]{3,2,1,0:T(8,128)(2,1)S(1)} %get-tuple-element.6), channel_id=1, source_target_pairs={{0,12},{4,0},{8,4},{12,8},{1,13},{5,1},{9,5},{13,9},{2,14},{6,2},{... | collective-permute-start | bytes 589832 | tf_op jit(solution)/shard_map/ppermute | solution.py:35
  179.1 11.0 %collective-permute-start.23 = (bf16[128,768]{1,0:T(8,128)(2,1)}, bf16[128,768]{1,0:T(8,128)(2,1)}, u32[]{:S(2)}, u32[]{:S(2)}) collective-permute-start(bf16[128,768]{1,0:T(8,128)(2,1)} %get-tuple-element.7), channel_id=1, source_target_pairs={{0,32},{32,64},{64,96},{96,0},{1,33},{33,65},{65,97},{97,1},{2,34}... | collective-permute-start | bytes 589832 | tf_op jit(solution)/shard_map/ppermute | solution.py:30
  179.1 11.0 %collective-permute-start.25 = (bf16[128,768]{1,0:T(8,128)(2,1)}, bf16[128,768]{1,0:T(8,128)(2,1)}, u32[]{:S(2)}, u32[]{:S(2)}) collective-permute-start(bf16[128,768]{1,0:T(8,128)(2,1)} %get-tuple-element.8), channel_id=1, source_target_pairs={{0,96},{32,0},{64,32},{96,64},{1,97},{33,1},{65,33},{97,65},{2,98}... | collective-permute-start | bytes 589832 | tf_op jit(solution)/shard_map/ppermute | solution.py:35
  184.7 9.5 %collective-permute-start.20 = (bf16[128,1280]{1,0:T(8,128)(2,1)}, bf16[128,1280]{1,0:T(8,128)(2,1)}, u32[]{:S(2)}, u32[]{:S(2)}) collective-permute-start(bf16[128,1280]{1,0:T(8,128)(2,1)} %fusion.29), channel_id=1, source_target_pairs={{0,16},{16,0},{1,17},{17,1},{2,18},{18,2},{3,19},{19,3},{4,20},{20... | collective-permute-start | bytes 983048 | tf_op jit(solution)/shard_map/ppermute | solution.py:39
  185.8 8.4 %copy-start.24 = (f32[256,1280]{1,0:T(8,128)S(1)}, f32[256,1280]{1,0:T(8,128)}, u32[]{:S(2)}) copy-start(f32[256,1280]{1,0:T(8,128)} %copy-done.23) | copy-start | bytes 3932164
  185.8 13.8 %all-to-all-start.2 = ((f32[16,24,256]{2,1,0:T(8,128)}), f32[16,24,256]{2,1,0:T(8,128)}, u32[]{:S(2)}, u32[]{:S(2)}) async-start(f32[16,24,256]{2,1,0:T(8,128)} %bitcast.237), calls=%async_computation.2 | async-start | bytes 786432 | tf_op jit(solution)/shard_map/all_to_all | solution.py:168
  190.1 11.8 %copy-start.1 = (bf16[128,2048]{1,0:T(8,128)(2,1)S(1)}, bf16[128,2048]{1,0:T(8,128)(2,1)}, u32[]{:S(2)}) copy-start(bf16[128,2048]{1,0:T(8,128)(2,1)} %param.10) | copy-start | bytes 1572868
  (13 other events, 25.6 us)

commit v4 on v1

v4 whole, which is shorter than its diff:
```python
import math

import jax
import jax.numpy as jnp
import numpy as np
from jax import lax
from jax.experimental import pallas as pl
from jax.experimental.pallas import tpu as pltpu
from jax.sharding import Mesh
from jax.sharding import PartitionSpec as P

F32 = jnp.float32
BF16 = jnp.bfloat16
SEQ = ("x", "yl")
REP = ("z", "yh", "core")
X, YL, Z, YH, CORE = 4, 2, 4, 2, 2
ROWS = 256


def tables(length):
    odd = 2 * np.arange(length, dtype=np.int64)[:, None] + 1
    phase = odd * np.arange(length, dtype=np.int64)[None, :] % (4 * length)
    angle = phase.astype(np.float64) * (math.pi / (2 * length))
    return (np.cos(angle), np.sin(angle))


def dot(a, b):
    return jnp.dot(a, b, preferred_element_type=F32)


def up(x, axis):
    n = lax.axis_size(axis)
    return lax.ppermute(x, axis, [(i, (i + 1) % n) for i in range(n)])


def down(x, axis):
    n = lax.axis_size(axis)
    return lax.ppermute(x, axis, [(i, (i - 1) % n) for i in range(n)])


def swap(x, axis):
    return lax.ppermute(x, axis, [(0, 1), (1, 0)])


def pick(x, index, axis=0):
    return lax.dynamic_index_in_dim(x, index, axis, keepdims=False)


def halves_round(block, axis):
    lower = up(block, axis)
    upper = down(block, axis)
    half = block.shape[0] // 2
    return block, upper, lower, up(lower[:half], axis), down(upper[half:], axis)


def in_order(own, other, index):
    return jnp.where(index == 0, jnp.stack([own, other]), jnp.stack([other, own]))


def ring_gather(block, axis):
    own, upper, lower, far_a, far_b = halves_round(block, axis)
    me = lax.axis_index(axis)
    out = jnp.zeros((4,) + block.shape, block.dtype)
    for k, piece in ((0, own), (1, upper), (3, lower), (2, jnp.concatenate([far_a, far_b]))):
        out = lax.dynamic_update_index_in_dim(out, piece, (me + k) % 4, 0)
    return out


def transforms_body(
    core, got, weight, taps, cos, sin, cos_t, sin_t, pair_o, w_mine, w_send, f_mine, f_send,
    acts_v, inner_v, w_v, taps_v, c_v, s_v, ct_v, st_v, fc, fs, ic, js, vc, vs, p, q, vals, sem,
):
    groups, block, features = acts_v.shape
    length, part = vals.shape
    scale = 1.0 / math.sqrt(length * Z * YH * CORE)
    moves = (
        (taps, taps_v),
        (cos, c_v),
        (sin, s_v),
        (got.at[:, :, features:], inner_v),
        (cos_t, ct_v),
        (sin_t, st_v),
        (weight, w_v),
        (got.at[:, :, :features], acts_v),
    )
    copies = [pltpu.make_async_copy(a, b, sem.at[i]) for i, (a, b) in enumerate(moves)]
    for copy in copies:
        copy.start()
    acts = acts_v.reshape(length, features)
    inner = inner_v.reshape(length, part)
    per = ROWS // block

    def each(count, step):
        @pl.loop(0, count // ROWS)
        def _(i):
            step(i, pl.ds(pl.multiple_of(i * ROWS, ROWS), ROWS))

    def spectrum(x, cos_sum, sin_sum):
        def step(i, r):
            cos_sum[r, :] = dot(c_v[r, :], x[...])
            sin_sum[r, :] = dot(s_v[r, :], x[...])

        each(length, step)

    def product(fn):
        def step(i, r):
            a, b = fn(r)
            p[r, :] = a.astype(BF16)
            q[r, :] = b.astype(BF16)

        each(length, step)

    def inverse(r):
        return (dot(ct_v[r, :], p[...]) + dot(st_v[r, :], q[...])) * (1.0 / length)

    def by_core(x, rows):
        x = x.reshape(-1, CORE, rows, part)
        own = core[0] == 0
        return jnp.where(own, x[:, 0], x[:, 1]), jnp.where(own, x[:, 1], x[:, 0])

    for copy in copies[:3]:
        copy.wait()
    spectrum(taps_v, fc, fs)
    copies[3].wait()
    spectrum(inner, ic, js)
    product(lambda r: (fc[r, :] * ic[r, :] + fs[r, :] * js[r, :], fc[r, :] * js[r, :] - fs[r, :] * ic[r, :]))
    copies[4].wait()
    copies[5].wait()

    def grad_step(i, r):
        g = inverse(r).astype(BF16)
        vals[r, :] = g
        pair_o[pl.ds(i * per, per), :, part:] = g.reshape(per, block, part)

    each(length, grad_step)
    copies[6].wait()
    copies[7].wait()

    def weight_step(i, r):
        g = lax.dot_general(acts[:, r], vals[...], (((0,), (0,)), ((), ())), preferred_element_type=F32) * scale
        own, other = by_core(g, 16)
        n = ROWS // (CORE * 16)
        w_mine[pl.ds(i * n, n)] = own
        w_send[pl.ds(i * n, n)] = other.astype(BF16)

    each(features, weight_step)

    def value_step(i, r):
        vals[r, :] = dot(acts[r, :], w_v[...]).astype(BF16)

    each(length, value_step)
    spectrum(vals, vc, vs)
    product(lambda r: (fc[r, :] * vc[r, :] - fs[r, :] * vs[r, :], fc[r, :] * vs[r, :] + fs[r, :] * vc[r, :]))

    def conv_step(i, r):
        pair_o[pl.ds(i * per, per), :, :part] = inverse(r).astype(BF16).reshape(per, block, part)

    each(length, conv_step)
    product(lambda r: (vc[r, :] * ic[r, :] + vs[r, :] * js[r, :], vc[r, :] * js[r, :] - vs[r, :] * ic[r, :]))

    def filter_step(i, r):
        own, other = by_core(inverse(r) * scale, 8)
        n = ROWS // (CORE * 8)
        f_mine[pl.ds(i * n, n)] = own
        f_send[pl.ds(i * n, n)] = other

    each(length, filter_step)


def transforms(core, got, weight, taps, tables_v):
    groups, block, width = got.shape
    features, part = weight.shape
    length = groups * block
    away = pl.BlockSpec(memory_space=pl.ANY)
    near = pl.BlockSpec(memory_space=pltpu.VMEM)
    shape = jax.ShapeDtypeStruct
    own = features // (CORE * 16)
    wave = pltpu.VMEM((length, part), F32)
    narrow = pltpu.VMEM((length, part), BF16)
    table = pltpu.VMEM((length, length), BF16)
    return pl.pallas_call(
        transforms_body,
        out_shape=[
            shape((groups, block, 2 * part), BF16),
            shape((own, 16, part), F32),
            shape((own, 16, part), BF16),
            shape((own, 8, part), F32),
            shape((own, 8, part), F32),
        ],
        in_specs=[pl.BlockSpec(memory_space=pltpu.SMEM)] + [away] * 7,
        out_specs=[near] * 5,
        scratch_shapes=[
            pltpu.VMEM((groups, block, features), BF16),
            pltpu.VMEM((groups, block, part), BF16),
            pltpu.VMEM((features, part), BF16),
            narrow,
            table,
            table,
            table,
            table,
            wave,
            wave,
            wave,
            wave,
            wave,
            wave,
            narrow,
            narrow,
            narrow,
            pltpu.SemaphoreType.DMA((8,)),
        ],
        compiler_params=pltpu.CompilerParams(vmem_limit_bytes=48 * 2**20),
        name="transforms",
    )(core, got, weight, taps, *tables_v)


def outputs_body(place, back, gates, upstream, *refs):
    pieces, (mixed_o, gate_o, input_o, w_v, grad_v, sem) = refs[:10], refs[10:]
    groups, block, _ = back.shape
    part = back.shape[2] // 2
    z, core = place[0], place[1]
    copies = []
    for side, which in ((0, core), (1, 1 - core)):
        own, upper, lower, far_a, far_b = pieces[5 * side : 5 * side + 5]
        for k, ref, yh in ((0, own, None), (1, upper, None), (3, lower, None), (2, far_a, 0), (2, far_b, 1)):
            to = lax.rem(z + k, Z)
            for h in (0, 1) if yh is None else (yh,):
                src = ref.at[h if yh is None else 0]
                copies.append(pltpu.make_async_copy(src, w_v.at[:, to, h, which], sem.at[len(copies)]))
    for copy in copies:
        copy.start()
    for g in range(groups):
        c = pl.ds(g * part, part)
        conv = back[g, :, :part].astype(F32)
        mixed_o[:, c] = (gates[:, c].astype(F32) * conv).astype(BF16)
        gate_o[:, c] = (upstream[:, c].astype(F32) * conv).astype(BF16)
        grad_v[:, c] = back[g, :, part:]
    for copy in copies:
        copy.wait()
    rows = w_v.shape[4]
    for g in range(groups):
        w = w_v[g].reshape(Z * YH * CORE * rows, w_v.shape[5])
        n = w.shape[0]
        y = lax.dot_general(grad_v[...], w, (((1,), (1,)), ((), ())), preferred_element_type=F32)
        input_o[:, pl.ds(g * n, n)] = y.astype(BF16)


def outputs(place, back, gates, upstream, pieces):
    groups, block, _ = back.shape
    channels = gates.shape[1]
    rows = pieces[0].shape[2]
    features = groups * Z * YH * CORE * rows
    away = pl.BlockSpec(memory_space=pl.ANY)
    near = pl.BlockSpec(memory_space=pltpu.VMEM)
    shape = jax.ShapeDtypeStruct
    return pl.pallas_call(
        outputs_body,
        out_shape=[shape((block, channels), BF16)] * 2 + [shape((block, features), BF16)],
        in_specs=[pl.BlockSpec(memory_space=pltpu.SMEM)] + [near] * 3 + [away] * 10,
        out_specs=[near] * 3,
        scratch_shapes=[
            pltpu.VMEM((groups, Z, YH, CORE, rows, channels), BF16),
            pltpu.VMEM((block, channels), BF16),
            pltpu.SemaphoreType.DMA((16,)),
        ],
        compiler_params=pltpu.CompilerParams(vmem_limit_bytes=32 * 2**20),
        name="outputs",
    )(place, back, gates, upstream, *pieces)


def local(activations, gate_values, in_weight, long_filter, out_cotangent):
    tokens = activations[0]
    gates = gate_values[0]
    upstream = out_cotangent[0]
    groups = X * YL
    replicas = Z * YH * CORE
    block, channels = gates.shape
    features = tokens.shape[1]
    length = block * groups
    part = channels // groups
    rows = in_weight.shape[0]
    taps_rows = block // replicas
    own_rows = rows + taps_rows
    xi, yi, zi, hi, ci = (lax.axis_index(a) for a in SEQ + REP)

    cosine, sine = (jnp.asarray(t.astype(np.float32)).astype(BF16) for t in tables(length))
    cosine_t, sine_t = (jnp.asarray(t.T.astype(np.float32)).astype(BF16) for t in tables(length))

    inner = (upstream.astype(F32) * gates.astype(F32)).astype(BF16)
    inner = inner.reshape(block, groups, part).transpose(1, 0, 2)
    sent = jnp.concatenate([jnp.broadcast_to(tokens, (groups, block, features)), inner], axis=2)
    got = lax.all_to_all(sent, SEQ, 0, 0, tiled=True)

    own_taps = lax.dynamic_slice_in_dim(long_filter, ((zi * YH + hi) * CORE + ci) * taps_rows, taps_rows, 0)
    piece = jnp.concatenate([in_weight, own_taps], axis=0)
    piece = ring_gather(in_order(piece, swap(piece, "yl"), yi), "x").reshape(groups, own_rows, channels)
    thin = lax.dynamic_slice_in_dim(piece, (xi * YL + yi) * part, part, 2)
    thin = ring_gather(in_order(thin, swap(thin, "yh"), hi), "z")
    thin = in_order(thin, swap(thin, "core"), ci).transpose(3, 1, 2, 0, 4, 5)
    weight = thin[..., :rows, :].reshape(features, part)
    taps = thin[..., rows:, :].reshape(length, part)
    wide = piece[:, :rows]
    wide = halves_round(in_order(wide, swap(wide, "yh"), hi), "z")
    wide = wide + tuple(swap(w, "core") for w in wide)

    pair, w_mine, w_send, f_mine, f_send = transforms(
        ci.reshape(1), got, weight, taps, (cosine, sine, cosine_t, sine_t)
    )

    back = lax.all_to_all(pair, SEQ, 0, 0, tiled=True)
    other = swap(jnp.concatenate([w_send, f_send.astype(BF16)], axis=1), "core")
    owned = (jnp.concatenate([w_mine, f_mine], axis=1) + other.astype(F32)).astype(BF16)
    owned = lax.all_to_all(owned, SEQ + ("z", "yh"), 0, 0, tiled=True)
    owned = jnp.sum(owned.reshape(groups, Z * YH, own_rows, part).astype(F32), axis=1)
    owned = owned.transpose(1, 0, 2).reshape(own_rows, channels)

    mixed_out, gate_grad, input_grad = outputs(jnp.stack([zi, ci]), back, gates, upstream, wide)
    return (mixed_out[None], gate_grad[None], input_grad[None], owned[:rows], owned[rows:])


def solution(mesh):
    mesh = Mesh(mesh.devices.reshape(X, YL, Z, YH, CORE), SEQ + REP)
    split = P(REP, SEQ, None)
    in_specs = (split, split, P(SEQ + REP, None), P(SEQ, None), split)
    out_specs = (split, split, split, P(SEQ + REP, None), P(SEQ + REP, None))
    return jax.shard_map(local, mesh=mesh, in_specs=in_specs, out_specs=out_specs, check_vma=False)
```

time: 454 us -> 203 us (0.45)
  waiting for transfers between devices: 322 us -> 107 us
  blocking collectives: 46.2 us -> 0 us
  starting transfers between devices: 10.6 us -> 46.4 us
  Pallas kernels: 0 us -> 25.8 us
  matrix products: 25.2 us -> 0 us
  local copies, waits for them, and re-layouts: 30.6 us -> 13 us
  between operations: 14 us -> 1.18 us
  other arithmetic: 3.68 us -> 9.29 us
    reduce_scatter x3 -> x0, waiting for transfers between devices: 194 us -> none  [the longest x2 114 us: reduce_rows(): x = lax.psum_scatter(x, 'rep', scatter_dimension=0, tiled=True)]
    all_gather x2 -> x0, waiting for transfers between devices: 117 us -> none  [the longest x1 88.7 us: local(): acts = lax.all_gather(tokens, 'seq', axis=0, tiled=True)]
    ppermute x0 -> x22, waiting for transfers between devices: none -> 95.4 us  [the longest x6 73.7 us: up(): return lax.ppermute(x, axis, [(i, (i + 1) % n) for i in range(n)])]
    all_to_all x4 -> x0, blocking collectives: 46.2 us -> none  [the longest x3 35.4 us: to_channels(): return lax.all_to_all(x, 'seq', 1, 0, tiled=True)]
    ppermute x0 -> x22, starting transfers between devices: none -> 30.5 us  [the longest x6 18.8 us: down(): return lax.ppermute(x, axis, [(i, (i - 1) % n) for i in range(n)])]
    pallas_call x0 -> x2, Pallas kernels: none -> 25.8 us  [the longest x1 18.6 us: transforms(): pl.pallas_call(transforms_body, out_shape=[shape((groups, block, 2 * part...]
    dot_general x15 -> x0, matrix products: 25.2 us -> none  [dot(): return lax.dot_general(a, b, (dims, ((), ())), preferred_element_type=F32)]
    unnamed x50 -> x23, local copies, waits for them, and re-layouts: 15.9 us -> 6.41 us
  transfers between devices with their start and end apart: 7 -> 25, of which waited for: 7 -> 12; matrix products, arithmetic and copies ran while one was open for 6% -> 7% of each run, Pallas kernels for 0% -> 13%
where the time goes in v4:
time: 203 us; the launch traced here: 202 us
  waiting for transfers between devices  107 us (53%)
  starting transfers between devices  46.4 us (23%)
  Pallas kernels  25.8 us (13%)
  local copies, waits for them, and re-layouts  13 us (6%)
  other arithmetic  9.29 us (5%)
    ppermute x6, waiting for transfers between devices, up(): return lax.ppermute(x, axis, [(i, (i + 1) % n) for i in range(n)])  73.7 us
    ppermute x6, starting transfers between devices, down(): return lax.ppermute(x, axis, [(i, (i - 1) % n) for i in range(n)])  18.8 us
    pallas_call x1, Pallas kernels, transforms(): pl.pallas_call(transforms_body, out_shape=[shape((groups, block, 2 * part...  18.6 us
    ppermute x10, waiting for transfers between devices, swap(): return lax.ppermute(x, axis, [(0, 1), (1, 0)])  18.4 us
    ppermute x10, starting transfers between devices, swap(): return lax.ppermute(x, axis, [(0, 1), (1, 0)])  8.96 us
    pallas_call x1, Pallas kernels, outputs(): pl.pallas_call(outputs_body, out_shape=[shape((block, channels), BF16)] *...  7.18 us
    all_to_all x1, starting transfers between devices, local(): owned = lax.all_to_all(owned, SEQ + ('z', 'yh'), 0, 0, tiled=True)  6.83 us
    all_to_all x1, waiting for transfers between devices, local(): back = lax.all_to_all(pair, SEQ, 0, 0, tiled=True)  6.44 us
  transfers between devices with their start and end apart: 25, of which 12 were waited for; matrix products, arithmetic and copies ran while one was open for 7% of the time, Pallas kernels for 13%

profile of v4, /device:TPU:0, one launch (start us, length us, event | category | flops | bytes accessed | tf_op | source)
XLA Modules:
  0.0 202.4 jit_solution(945885607609923124)
XLA Ops:
  0.6 0.0 copy-start
  0.7 1.0 copy-done
  1.7 0.9 fusion.6
  2.5 1.7 collective-permute-start
  4.3 1.3 copy.18
  5.6 0.3 copy.19
  5.9 0.1 multiply_convert_fusion
  6.0 0.2 copy.20
  6.3 0.7 copy-done.9
  6.9 0.5 broadcast_in_dim.40
  7.5 2.6 %pad_maximum_fusion = bf16[8,128,2304]{2,1,0:T(8,128)(2,1)} fusion(bf16[8,128,256]{2,1,0:T(8,128)(2,1)S(1)} %bitcast.66, bf16[8,128,2048]{2,1,0:T(8,128)(2,1)S(1)} %broadcast_in_dim.40), kind=kLoop, calls=%fused_computation | loop fusion | flops 9437184 | bytes 9437184 | tf_op jit(solution)/shard_map/concatenate | solution.py:291
  10.1 4.6 %all-to-all-start = ((bf16[8,128,2304]{2,1,0:T(8,128)(2,1)}), bf16[8,128,2304]{2,1,0:T(8,128)(2,1)}, u32[]{:S(2)}, u32[]{:S(2)}) async-start(bf16[8,128,2304]{2,1,0:T(8,128)(2,1)} %pad_maximum_fusion), calls=%async_computation | async-start | bytes 9437184 | tf_op jit(solution)/shard_map/all_to_all | solution.py:292
  14.8 3.1 %collective-permute-start.1 = (bf16[2,24,2048]{2,1,0:T(8,128)(2,1)S(1)}, bf16[2,24,2048]{2,1,0:T(8,128)(2,1)S(1)}, u32[]{:S(2)}, u32[]{:S(2)}) collective-permute-start(bf16[2,24,2048]{2,1,0:T(8,128)(2,1)S(1)} %maximum_select_fusion.3), channel_id=1, source_target_pairs={{0,96},{32,0},{64,32},{96,64},{1,97},{33,1},{65,33},{97,65},{2,98}... | collective-permute-start | bytes 589832 | tf_op jit(solution)/shard_map/ppermute | solution.py:38
  17.9 0.1 broadcast_in_dim.42
  18.0 61.0 %collective-permute-done.2 = bf16[2,24,2048]{2,1,0:T(8,128)(2,1)S(1)} collective-permute-done((bf16[2,24,2048]{2,1,0:T(8,128)(2,1)S(1)}, bf16[2,24,2048]{2,1,0:T(8,128)(2,1)S(1)}, u32[]{:S(2)}, u32[]{:S(2)}) %collective-permute-start.2) | collective-permute-done | bytes 196640 | tf_op jit(solution)/shard_map/ppermute | solution.py:33
  79.1 2.6 %collective-permute-start.3 = (bf16[1,24,2048]{2,1,0:T(8,128)(2,1)S(1)}, bf16[1,24,2048]{2,1,0:T(8,128)(2,1)S(1)}, u32[]{:S(2)}, u32[]{:S(2)}) collective-permute-start(bf16[1,24,2048]{2,1,0:T(8,128)(2,1)S(1)} %slice.52), channel_id=1, source_target_pairs={{0,32},{32,64},{64,96},{96,0},{1,33},{33,65},{65,97},{97,1},{2,34}... | collective-permute-start | bytes 294920 | tf_op jit(solution)/shard_map/ppermute | solution.py:33
  81.6 2.7 %collective-permute-done.1 = bf16[2,24,2048]{2,1,0:T(8,128)(2,1)S(1)} collective-permute-done((bf16[2,24,2048]{2,1,0:T(8,128)(2,1)S(1)}, bf16[2,24,2048]{2,1,0:T(8,128)(2,1)S(1)}, u32[]{:S(2)}, u32[]{:S(2)}) %collective-permute-start.1) | collective-permute-done | bytes 196640 | tf_op jit(solution)/shard_map/ppermute | solution.py:38
  84.4 1.7 collective-permute-start.4
  86.1 2.4 %collective-permute-done.3 = bf16[1,24,2048]{2,1,0:T(8,128)(2,1)S(1)} collective-permute-done((bf16[1,24,2048]{2,1,0:T(8,128)(2,1)S(1)}, bf16[1,24,2048]{2,1,0:T(8,128)(2,1)S(1)}, u32[]{:S(2)}, u32[]{:S(2)}) %collective-permute-start.3) | collective-permute-done | bytes 98336 | tf_op jit(solution)/shard_map/ppermute | solution.py:33
  88.6 0.5 collective-permute-done.4
  89.1 3.0 %collective-permute-start.5 = (bf16[8,24,256]{2,1,0:T(8,128)(2,1)S(1)}, bf16[8,24,256]{2,1,0:T(8,128)(2,1)S(1)}, u32[]{:S(2)}, u32[]{:S(2)}) collective-permute-start(bf16[8,24,256]{2,1,0:T(8,128)(2,1)S(1)} %constant_dynamic-slice_fusion), channel_id=1, source_target_pairs={{0,2},{2,0},{1,3},{3,1},{4,6},{6,4},{5,7},{7,5},{8,10},{10,8},{9,1... | collective-permute-start | bytes 294920 | tf_op jit(solution)/shard_map/ppermute | solution.py:42
  92.1 3.2 %collective-permute-done.5 = bf16[8,24,256]{2,1,0:T(8,128)(2,1)S(1)} collective-permute-done((bf16[8,24,256]{2,1,0:T(8,128)(2,1)S(1)}, bf16[8,24,256]{2,1,0:T(8,128)(2,1)S(1)}, u32[]{:S(2)}, u32[]{:S(2)}) %collective-permute-start.5) | collective-permute-done | bytes 98336 | tf_op jit(solution)/shard_map/ppermute | solution.py:42
  95.3 4.1 %collective-permute-start.6 = (bf16[2,8,24,256]{3,2,1,0:T(8,128)(2,1)S(1)}, bf16[2,8,24,256]{3,2,1,0:T(8,128)(2,1)S(1)}, u32[]{:S(2)}, u32[]{:S(2)}) collective-permute-start(bf16[2,8,24,256]{3,2,1,0:T(8,128)(2,1)S(1)} %maximum_select_fusion.5), channel_id=1, source_target_pairs={{0,12},{4,0},{8,4},{12,8},{1,13},{5,1},{9,5},{13,9},{2,14},{6,2},{... | collective-permute-start | bytes 589832 | tf_op jit(solution)/shard_map/ppermute | solution.py:38
  99.5 0.1 broadcast_in_dim.41
  99.6 7.8 %collective-permute-done.7 = bf16[2,8,24,256]{3,2,1,0:T(8,128)(2,1)S(1)} collective-permute-done((bf16[2,8,24,256]{3,2,1,0:T(8,128)(2,1)S(1)}, bf16[2,8,24,256]{3,2,1,0:T(8,128)(2,1)S(1)}, u32[]{:S(2)}, u32[]{:S(2)}) %collective-permute-start.7) | collective-permute-done | bytes 196640 | tf_op jit(solution)/shard_map/ppermute | solution.py:33
  107.4 0.1 collective-permute-start.8
  107.5 3.3 %collective-permute-start.9 = (bf16[1,8,24,256]{3,2,1,0:T(8,128)(2,1)S(1)}, bf16[1,8,24,256]{3,2,1,0:T(8,128)(2,1)S(1)}, u32[]{:S(2)}, u32[]{:S(2)}) collective-permute-start(bf16[1,8,24,256]{3,2,1,0:T(8,128)(2,1)S(1)} %slice.55), channel_id=1, source_target_pairs={{0,12},{4,0},{8,4},{12,8},{1,13},{5,1},{9,5},{13,9},{2,14},{6,2},{... | collective-permute-start | bytes 294920 | tf_op jit(solution)/shard_map/ppermute | solution.py:38
  110.8 2.5 %collective-permute-done.8 = bf16[1,8,24,256]{3,2,1,0:T(8,128)(2,1)S(1)} collective-permute-done((bf16[1,8,24,256]{3,2,1,0:T(8,128)(2,1)S(1)}, bf16[1,8,24,256]{3,2,1,0:T(8,128)(2,1)S(1)}, u32[]{:S(2)}, u32[]{:S(2)}) %collective-permute-start.8) | collective-permute-done | bytes 98336 | tf_op jit(solution)/shard_map/ppermute | solution.py:33
  113.3 0.1 collective-permute-start.10
  113.4 0.1 slice_bitcast_fusion.1
  113.5 3.0 %collective-permute-start.11 = (bf16[8,16,2048]{2,1,0:T(8,128)(2,1)S(1)}, bf16[8,16,2048]{2,1,0:T(8,128)(2,1)S(1)}, u32[]{:S(2)}, u32[]{:S(2)}) collective-permute-start(bf16[8,16,2048]{2,1,0:T(8,128)(2,1)S(1)} %get-tuple-element.22), channel_id=1, source_target_pairs={{0,2},{2,0},{1,3},{3,1},{4,6},{6,4},{5,7},{7,5},{8,10},{10,8},{9,1... | collective-permute-start | bytes 1572872 | tf_op jit(solution)/shard_map/ppermute | solution.py:42
  116.5 12.9 %collective-permute-done.11 = bf16[8,16,2048]{2,1,0:T(8,128)(2,1)S(1)} collective-permute-done((bf16[8,16,2048]{2,1,0:T(8,128)(2,1)S(1)}, bf16[8,16,2048]{2,1,0:T(8,128)(2,1)S(1)}, u32[]{:S(2)}, u32[]{:S(2)}) %collective-permute-start.11) | collective-permute-done | bytes 524320 | tf_op jit(solution)/shard_map/ppermute | solution.py:42
  129.4 0.2 maximum_select_fusion.1.refs_0_
  129.6 0.1 collective-permute-start.13
  129.7 3.4 %collective-permute-start.12 = (bf16[2,8,16,2048]{3,2,1,0:T(8,128)(2,1)S(1)}, bf16[2,8,16,2048]{3,2,1,0:T(8,128)(2,1)}, u32[]{:S(2)}, u32[]{:S(2)}) collective-permute-start(bf16[2,8,16,2048]{3,2,1,0:T(8,128)(2,1)S(1)} %maximum_select_fusion.1.refs_0_), channel_id=1, source_target_pairs={{0,12},{4,0},{8,4},{12,8},{1,13},{5,1},{9,5},{13,9},{2,14},{6,2},{... | collective-permute-start | bytes 3145736 | tf_op jit(solution)/shard_map/ppermute | solution.py:38
  133.1 1.6 fusion
  134.7 0.1 slice.56
  134.9 0.1 copy.21
  135.0 0.1 copy.22
  135.1 18.6 %transforms.1 = (bf16[8,128,512]{2,1,0:T(8,128)(2,1)S(1)}, f32[64,16,256]{2,1,0:T(8,128)S(1)}, bf16[64,16,256]{2,1,0:T(8,128)(2,1)S(1)}, f32[64,8,256]{2,1,0:T(8,128)S(1)}, f32[64,8,256]{2,1,0:T(8,128)S(1)}) custom-call(s32[1]{0:T(128)} %bitcast.1.core, bf16[8,128,2304]{2,1,0:T(8,128)(2,1)} %all-to-all-done.got, bf16[2048,256]{1,0:T(8,128)(2,1)S(1)} %bitcast.56, ...), custom_call_target="tpu_custom_call" | custom-call | tf_op jit(solution)/shard_map/transforms/pallas_call | solution.py:181
  153.7 1.0 copy-done.4
  154.7 0.1 pad_maximum_fusion.1
  154.8 0.7 copy-done.7
  155.5 0.4 copy-done.6
  155.9 4.4 %all-to-all-start.1 = ((bf16[8,128,512]{2,1,0:T(8,128)(2,1)}), bf16[8,128,512]{2,1,0:T(8,128)(2,1)S(1)}, u32[]{:S(2)}, u32[]{:S(2)}) async-start(bf16[8,128,512]{2,1,0:T(8,128)(2,1)} %copy-done.6), calls=%async_computation.1 | async-start | bytes 2097152 | tf_op jit(solution)/shard_map/all_to_all | solution.py:310
  160.3 0.1 collective-permute-start.16
  160.4 2.0 slice.59
  162.4 1.9 slice.60
  164.3 3.3 %collective-permute-start.15 = (bf16[1,8,16,2048]{3,2,1,0:T(8,128)(2,1)}, bf16[1,8,16,2048]{3,2,1,0:T(8,128)(2,1)}, u32[]{:S(2)}, u32[]{:S(2)}) collective-permute-start(bf16[1,8,16,2048]{3,2,1,0:T(8,128)(2,1)} %slice.60), channel_id=1, source_target_pairs={{0,12},{4,0},{8,4},{12,8},{1,13},{5,1},{9,5},{13,9},{2,14},{6,2},{... | collective-permute-start | bytes 1572872 | tf_op jit(solution)/shard_map/ppermute | solution.py:38
  167.5 0.5 collective-permute-start.18
  168.1 2.3 %fusion.1 = bf16[64,24,256]{2,1,0:T(8,128)(2,1)} fusion(f32[64,8,256]{2,1,0:T(8,128)S(1)} %copy-done.8, f32[64,16,256]{2,1,0:T(8,128)S(1)} %copy-done.5, bf16[64,24,256]{2,1,0:T(8,128)(2,1)} %collective-permute-done.21), kind=kLoop, calls=%fused_computation.4 | loop fusion | flops 1572864 | bytes 3145728 | tf_op jit(solution)/shard_map/convert_element_type | solution.py:312
  170.4 6.4 %all-to-all-done.1.back = bf16[8,128,512]{2,1,0:T(8,128)(2,1)S(1)} async-done(((bf16[8,128,512]{2,1,0:T(8,128)(2,1)}), bf16[8,128,512]{2,1,0:T(8,128)(2,1)S(1)}, u32[]{:S(2)}, u32[]{:S(2)}) %all-to-all-start.1) | async-done | bytes 1048608 | tf_op jit(solution)/shard_map/all_to_all | solution.py:310
  176.8 6.8 %all-to-all-start.2 = ((bf16[64,24,256]{2,1,0:T(8,128)(2,1)}), bf16[64,24,256]{2,1,0:T(8,128)(2,1)}, u32[]{:S(2)}, u32[]{:S(2)}) async-start(bf16[64,24,256]{2,1,0:T(8,128)(2,1)} %fusion.1), calls=%async_computation.2 | async-start | bytes 1572864 | tf_op jit(solution)/shard_map/all_to_all | solution.py:313
  183.6 0.1 collective-permute-start.19
  183.8 0.5 collective-permute-start.20
  184.2 0.1 pad_add_fusion.place
  184.3 1.5 collective-permute-done.19.refs_8_
  185.8 0.7 collective-permute-done.20.refs_9_
  186.6 1.0 copy-done.3
  187.7 7.2 %outputs.1 = (bf16[128,2048]{1,0:T(8,128)(2,1)}, bf16[128,2048]{1,0:T(8,128)(2,1)}, bf16[128,2048]{1,0:T(8,128)(2,1)}) custom-call(s32[2]{0:T(128)S(1)} %pad_add_fusion.place, bf16[8,128,512]{2,1,0:T(8,128)(2,1)S(1)} %all-to-all-done.1.back, bf16[128,2048]{1,0:T(8,128)(2,1)S(1)} %bitcast.58, bf16[128,2048]{1,0:T(8,128)(2,1)S(1)} %bitcast.59, ...), custom_call_target="tpu_custom_call" | custom-call | tf_op jit(solution)/shard_map/outputs/pallas_call | solution.py:256
  194.8 5.0 %all-to-all-done.2 = bf16[64,24,256]{2,1,0:T(8,128)(2,1)} async-done(((bf16[64,24,256]{2,1,0:T(8,128)(2,1)}), bf16[64,24,256]{2,1,0:T(8,128)(2,1)}, u32[]{:S(2)}, u32[]{:S(2)}) %all-to-all-start.2) | async-done | bytes 786464 | tf_op jit(solution)/shard_map/all_to_all | solution.py:313
  199.9 1.3 convert_reduce_fusion
  201.1 0.6 slice.62
  201.8 0.7 copy.24
  (52 shorter events, 0.5 us)
Async XLA Ops:
  0.6 1.0 copy-start
  0.6 5.0 %copy-start.1 = (bf16[1,128,2048]{2,1,0:T(8,128)(2,1)S(1)}, bf16[1,128,2048]{2,1,0:T(8,128)(2,1)}, u32[]{:S(2)}) copy-start(bf16[1,128,2048]{2,1,0:T(8,128)(2,1)} %param.10) | copy-start | bytes 1572868
  2.5 12.2 %collective-permute-start = (bf16[24,2048]{1,0:T(8,128)(2,1)S(1)}, bf16[24,2048]{1,0:T(8,128)(2,1)S(1)}, u32[]{:S(2)}, u32[]{:S(2)}) collective-permute-start(bf16[24,2048]{1,0:T(8,128)(2,1)S(1)} %get-tuple-element.25), channel_id=1, source_target_pairs={{0,16},{16,0},{1,17},{17,1},{2,18},{18,2},{3,19},{19,3},{4,20},{20... | collective-permute-start | bytes 294920 | tf_op jit(solution)/shard_map/ppermute | solution.py:42
  5.9 1.0 copy-start.9
  10.1 125.0 %all-to-all-start = ((bf16[8,128,2304]{2,1,0:T(8,128)(2,1)}), bf16[8,128,2304]{2,1,0:T(8,128)(2,1)}, u32[]{:S(2)}, u32[]{:S(2)}) async-start(bf16[8,128,2304]{2,1,0:T(8,128)(2,1)} %pad_maximum_fusion), calls=%async_computation | async-start | bytes 9437184 | tf_op jit(solution)/shard_map/all_to_all | solution.py:292
  14.8 69.5 %collective-permute-start.1 = (bf16[2,24,2048]{2,1,0:T(8,128)(2,1)S(1)}, bf16[2,24,2048]{2,1,0:T(8,128)(2,1)S(1)}, u32[]{:S(2)}, u32[]{:S(2)}) collective-permute-start(bf16[2,24,2048]{2,1,0:T(8,128)(2,1)S(1)} %maximum_select_fusion.3), channel_id=1, source_target_pairs={{0,96},{32,0},{64,32},{96,64},{1,97},{33,1},{65,33},{97,65},{2,98}... | collective-permute-start | bytes 589832 | tf_op jit(solution)/shard_map/ppermute | solution.py:38
  17.9 61.2 %collective-permute-start.2 = (bf16[2,24,2048]{2,1,0:T(8,128)(2,1)S(1)}, bf16[2,24,2048]{2,1,0:T(8,128)(2,1)S(1)}, u32[]{:S(2)}, u32[]{:S(2)}) collective-permute-start(bf16[2,24,2048]{2,1,0:T(8,128)(2,1)S(1)} %maximum_select_fusion.3), channel_id=1, source_target_pairs={{0,32},{32,64},{64,96},{96,0},{1,33},{33,65},{65,97},{97,1},{2,34}... | collective-permute-start | bytes 589832 | tf_op jit(solution)/shard_map/ppermute | solution.py:33
  79.1 9.5 %collective-permute-start.3 = (bf16[1,24,2048]{2,1,0:T(8,128)(2,1)S(1)}, bf16[1,24,2048]{2,1,0:T(8,128)(2,1)S(1)}, u32[]{:S(2)}, u32[]{:S(2)}) collective-permute-start(bf16[1,24,2048]{2,1,0:T(8,128)(2,1)S(1)} %slice.52), channel_id=1, source_target_pairs={{0,32},{32,64},{64,96},{96,0},{1,33},{33,65},{65,97},{97,1},{2,34}... | collective-permute-start | bytes 294920 | tf_op jit(solution)/shard_map/ppermute | solution.py:33
  84.4 4.7 %collective-permute-start.4 = (bf16[1,24,2048]{2,1,0:T(8,128)(2,1)S(1)}, bf16[1,24,2048]{2,1,0:T(8,128)(2,1)S(1)}, u32[]{:S(2)}, u32[]{:S(2)}) collective-permute-start(bf16[1,24,2048]{2,1,0:T(8,128)(2,1)S(1)} %slice.53), channel_id=1, source_target_pairs={{0,96},{32,0},{64,32},{96,64},{1,97},{33,1},{65,33},{97,65},{2,98}... | collective-permute-start | bytes 294920 | tf_op jit(solution)/shard_map/ppermute | solution.py:38
  89.1 6.2 %collective-permute-start.5 = (bf16[8,24,256]{2,1,0:T(8,128)(2,1)S(1)}, bf16[8,24,256]{2,1,0:T(8,128)(2,1)S(1)}, u32[]{:S(2)}, u32[]{:S(2)}) collective-permute-start(bf16[8,24,256]{2,1,0:T(8,128)(2,1)S(1)} %constant_dynamic-slice_fusion), channel_id=1, source_target_pairs={{0,2},{2,0},{1,3},{3,1},{4,6},{6,4},{5,7},{7,5},{8,10},{10,8},{9,1... | collective-permute-start | bytes 294920 | tf_op jit(solution)/shard_map/ppermute | solution.py:42
  95.3 12.1 %collective-permute-start.6 = (bf16[2,8,24,256]{3,2,1,0:T(8,128)(2,1)S(1)}, bf16[2,8,24,256]{3,2,1,0:T(8,128)(2,1)S(1)}, u32[]{:S(2)}, u32[]{:S(2)}) collective-permute-start(bf16[2,8,24,256]{3,2,1,0:T(8,128)(2,1)S(1)} %maximum_select_fusion.5), channel_id=1, source_target_pairs={{0,12},{4,0},{8,4},{12,8},{1,13},{5,1},{9,5},{13,9},{2,14},{6,2},{... | collective-permute-start | bytes 589832 | tf_op jit(solution)/shard_map/ppermute | solution.py:38
  99.4 7.9 %collective-permute-start.7 = (bf16[2,8,24,256]{3,2,1,0:T(8,128)(2,1)S(1)}, bf16[2,8,24,256]{3,2,1,0:T(8,128)(2,1)S(1)}, u32[]{:S(2)}, u32[]{:S(2)}) collective-permute-start(bf16[2,8,24,256]{3,2,1,0:T(8,128)(2,1)S(1)} %maximum_select_fusion.5), channel_id=1, source_target_pairs={{0,4},{4,8},{8,12},{12,0},{1,5},{5,9},{9,13},{13,1},{2,6},{6,10},{... | collective-permute-start | bytes 589832 | tf_op jit(solution)/shard_map/ppermute | solution.py:33
  107.4 5.9 %collective-permute-start.8 = (bf16[1,8,24,256]{3,2,1,0:T(8,128)(2,1)S(1)}, bf16[1,8,24,256]{3,2,1,0:T(8,128)(2,1)S(1)}, u32[]{:S(2)}, u32[]{:S(2)}) collective-permute-start(bf16[1,8,24,256]{3,2,1,0:T(8,128)(2,1)S(1)} %slice.54), channel_id=1, source_target_pairs={{0,4},{4,8},{8,12},{12,0},{1,5},{5,9},{9,13},{13,1},{2,6},{6,10},{... | collective-permute-start | bytes 294920 | tf_op jit(solution)/shard_map/ppermute | solution.py:33
  107.5 5.8 %collective-permute-start.9 = (bf16[1,8,24,256]{3,2,1,0:T(8,128)(2,1)S(1)}, bf16[1,8,24,256]{3,2,1,0:T(8,128)(2,1)S(1)}, u32[]{:S(2)}, u32[]{:S(2)}) collective-permute-start(bf16[1,8,24,256]{3,2,1,0:T(8,128)(2,1)S(1)} %slice.55), channel_id=1, source_target_pairs={{0,12},{4,0},{8,4},{12,8},{1,13},{5,1},{9,5},{13,9},{2,14},{6,2},{... | collective-permute-start | bytes 294920 | tf_op jit(solution)/shard_map/ppermute | solution.py:38
  113.3 19.8 %collective-permute-start.10 = (bf16[4,2,8,24,256]{4,3,2,1,0:T(8,128)(2,1)S(1)}, bf16[4,2,8,24,256]{4,3,2,1,0:T(8,128)(2,1)}, u32[]{:S(2)}, u32[]{:S(2)}) collective-permute-start(bf16[4,2,8,24,256]{4,3,2,1,0:T(8,128)(2,1)S(1)} %fusion.5), channel_id=1, source_target_pairs={{0,1},{1,0},{2,3},{3,2},{4,5},{5,4},{6,7},{7,6},{8,9},{9,8},{10,11... | collective-permute-start | bytes 2359304 | tf_op jit(solution)/shard_map/ppermute | solution.py:42
  113.5 15.9 %collective-permute-start.11 = (bf16[8,16,2048]{2,1,0:T(8,128)(2,1)S(1)}, bf16[8,16,2048]{2,1,0:T(8,128)(2,1)S(1)}, u32[]{:S(2)}, u32[]{:S(2)}) collective-permute-start(bf16[8,16,2048]{2,1,0:T(8,128)(2,1)S(1)} %get-tuple-element.22), channel_id=1, source_target_pairs={{0,2},{2,0},{1,3},{3,1},{4,6},{6,4},{5,7},{7,5},{8,10},{10,8},{9,1... | collective-permute-start | bytes 1572872 | tf_op jit(solution)/shard_map/ppermute | solution.py:42
  129.6 30.8 %collective-permute-start.13 = (bf16[2,8,16,2048]{3,2,1,0:T(8,128)(2,1)S(1)}, bf16[2,8,16,2048]{3,2,1,0:T(8,128)(2,1)}, u32[]{:S(2)}, u32[]{:S(2)}) collective-permute-start(bf16[2,8,16,2048]{3,2,1,0:T(8,128)(2,1)S(1)} %maximum_select_fusion.1.refs_0_), channel_id=1, source_target_pairs={{0,4},{4,8},{8,12},{12,0},{1,5},{5,9},{9,13},{13,1},{2,6},{6,10},{... | collective-permute-start | bytes 3145736 | tf_op jit(solution)/shard_map/ppermute | solution.py:33
  129.7 32.7 %collective-permute-start.12 = (bf16[2,8,16,2048]{3,2,1,0:T(8,128)(2,1)S(1)}, bf16[2,8,16,2048]{3,2,1,0:T(8,128)(2,1)}, u32[]{:S(2)}, u32[]{:S(2)}) collective-permute-start(bf16[2,8,16,2048]{3,2,1,0:T(8,128)(2,1)S(1)} %maximum_select_fusion.1.refs_0_), channel_id=1, source_target_pairs={{0,12},{4,0},{8,4},{12,8},{1,13},{5,1},{9,5},{13,9},{2,14},{6,2},{... | collective-permute-start | bytes 3145736 | tf_op jit(solution)/shard_map/ppermute | solution.py:38
  153.7 1.0 copy-start.4
  154.7 0.8 copy-start.7
  154.7 1.2 copy-start.6
  155.5 12.1 %collective-permute-start.21 = (bf16[64,24,256]{2,1,0:T(8,128)(2,1)S(1)}, bf16[64,24,256]{2,1,0:T(8,128)(2,1)}, u32[]{:S(2)}, u32[]{:S(2)}) collective-permute-start(bf16[64,24,256]{2,1,0:T(8,128)(2,1)S(1)} %pad_maximum_fusion.1), channel_id=1, source_target_pairs={{0,1},{1,0},{2,3},{3,2},{4,5},{5,4},{6,7},{7,6},{8,9},{9,8},{10,11... | collective-permute-start | bytes 2359304 | tf_op jit(solution)/shard_map/ppermute | solution.py:42
  155.9 20.9 %all-to-all-start.1 = ((bf16[8,128,512]{2,1,0:T(8,128)(2,1)}), bf16[8,128,512]{2,1,0:T(8,128)(2,1)S(1)}, u32[]{:S(2)}, u32[]{:S(2)}) async-start(bf16[8,128,512]{2,1,0:T(8,128)(2,1)} %copy-done.6), calls=%async_computation.1 | async-start | bytes 2097152 | tf_op jit(solution)/shard_map/all_to_all | solution.py:310
  160.3 7.8 %copy-start.5 = (f32[64,16,256]{2,1,0:T(8,128)S(1)}, f32[64,16,256]{2,1,0:T(8,128)}, u32[]{:S(2)}) copy-start(f32[64,16,256]{2,1,0:T(8,128)} %copy-done.4) | copy-start | bytes 3145732
  160.3 7.8 %copy-start.8 = (f32[64,8,256]{2,1,0:T(8,128)S(1)}, f32[64,8,256]{2,1,0:T(8,128)}, u32[]{:S(2)}) copy-start(f32[64,8,256]{2,1,0:T(8,128)} %copy-done.7) | copy-start | bytes 1572868
  160.3 24.0 %collective-permute-start.16 = (bf16[2,8,16,2048]{3,2,1,0:T(8,128)(2,1)S(1)}, bf16[2,8,16,2048]{3,2,1,0:T(8,128)(2,1)}, u32[]{:S(2)}, u32[]{:S(2)}) collective-permute-start(bf16[2,8,16,2048]{3,2,1,0:T(8,128)(2,1)S(1)} %maximum_select_fusion.1.refs_0_), channel_id=1, source_target_pairs={{0,1},{1,0},{2,3},{3,2},{4,5},{5,4},{6,7},{7,6},{8,9},{9,8},{10,11... | collective-permute-start | bytes 3145736 | tf_op jit(solution)/shard_map/ppermute | solution.py:42
  162.4 21.3 %collective-permute-start.14 = (bf16[1,8,16,2048]{3,2,1,0:T(8,128)(2,1)}, bf16[1,8,16,2048]{3,2,1,0:T(8,128)(2,1)}, u32[]{:S(2)}, u32[]{:S(2)}) collective-permute-start(bf16[1,8,16,2048]{3,2,1,0:T(8,128)(2,1)} %slice.59), channel_id=1, source_target_pairs={{0,4},{4,8},{8,12},{12,0},{1,5},{5,9},{9,13},{13,1},{2,6},{6,10},{... | collective-permute-start | bytes 1572872 | tf_op jit(solution)/shard_map/ppermute | solution.py:33
  164.3 19.5 %collective-permute-start.15 = (bf16[1,8,16,2048]{3,2,1,0:T(8,128)(2,1)}, bf16[1,8,16,2048]{3,2,1,0:T(8,128)(2,1)}, u32[]{:S(2)}, u32[]{:S(2)}) collective-permute-start(bf16[1,8,16,2048]{3,2,1,0:T(8,128)(2,1)} %slice.60), channel_id=1, source_target_pairs={{0,12},{4,0},{8,4},{12,8},{1,13},{5,1},{9,5},{13,9},{2,14},{6,2},{... | collective-permute-start | bytes 1572872 | tf_op jit(solution)/shard_map/ppermute | solution.py:38
  167.5 19.1 %collective-permute-start.17 = (bf16[2,8,16,2048]{3,2,1,0:T(8,128)(2,1)}, bf16[2,8,16,2048]{3,2,1,0:T(8,128)(2,1)}, u32[]{:S(2)}, u32[]{:S(2)}) collective-permute-start(bf16[2,8,16,2048]{3,2,1,0:T(8,128)(2,1)} %collective-permute-done.12.refs_1_), channel_id=1, source_target_pairs={{0,1},{1,0},{2,3},{3,2},{4,5},{5,4},{6,7},{7,6},{8,9},{9,8},{10,11... | collective-permute-start | bytes 3145736 | tf_op jit(solution)/shard_map/ppermute | solution.py:42
  167.5 19.1 %collective-permute-start.18 = (bf16[2,8,16,2048]{3,2,1,0:T(8,128)(2,1)}, bf16[2,8,16,2048]{3,2,1,0:T(8,128)(2,1)}, u32[]{:S(2)}, u32[]{:S(2)}) collective-permute-start(bf16[2,8,16,2048]{3,2,1,0:T(8,128)(2,1)} %collective-permute-done.13.refs_2_), channel_id=1, source_target_pairs={{0,1},{1,0},{2,3},{3,2},{4,5},{5,4},{6,7},{7,6},{8,9},{9,8},{10,11... | collective-permute-start | bytes 3145736 | tf_op jit(solution)/shard_map/ppermute | solution.py:42
  170.4 16.3 %copy-start.2 = (bf16[1,128,2048]{2,1,0:T(8,128)(2,1)S(1)}, bf16[1,128,2048]{2,1,0:T(8,128)(2,1)}, u32[]{:S(2)}) copy-start(bf16[1,128,2048]{2,1,0:T(8,128)(2,1)} %param.10) | copy-start | bytes 1572868
  176.8 23.1 %all-to-all-start.2 = ((bf16[64,24,256]{2,1,0:T(8,128)(2,1)}), bf16[64,24,256]{2,1,0:T(8,128)(2,1)}, u32[]{:S(2)}, u32[]{:S(2)}) async-start(bf16[64,24,256]{2,1,0:T(8,128)(2,1)} %fusion.1), calls=%async_computation.2 | async-start | bytes 1572864 | tf_op jit(solution)/shard_map/all_to_all | solution.py:313
  183.6 2.2 %collective-permute-start.19 = (bf16[1,8,16,2048]{3,2,1,0:T(8,128)(2,1)}, bf16[1,8,16,2048]{3,2,1,0:T(8,128)(2,1)S(1)}, u32[]{:S(2)}, u32[]{:S(2)}) collective-permute-start(bf16[1,8,16,2048]{3,2,1,0:T(8,128)(2,1)} %collective-permute-done.14.refs_3_), channel_id=1, source_target_pairs={{0,1},{1,0},{2,3},{3,2},{4,5},{5,4},{6,7},{7,6},{8,9},{9,8},{10,11... | collective-permute-start | bytes 1572872 | tf_op jit(solution)/shard_map/ppermute | solution.py:42
  183.8 2.8 %collective-permute-start.20 = (bf16[1,8,16,2048]{3,2,1,0:T(8,128)(2,1)}, bf16[1,8,16,2048]{3,2,1,0:T(8,128)(2,1)S(1)}, u32[]{:S(2)}, u32[]{:S(2)}) collective-permute-start(bf16[1,8,16,2048]{3,2,1,0:T(8,128)(2,1)} %collective-permute-done.15.refs_4_), channel_id=1, source_target_pairs={{0,1},{1,0},{2,3},{3,2},{4,5},{5,4},{6,7},{7,6},{8,9},{9,8},{10,11... | collective-permute-start | bytes 1572872 | tf_op jit(solution)/shard_map/ppermute | solution.py:42
  186.6 1.0 copy-start.3

commit v5 on v4

v5 whole, which is shorter than its diff:
```python
import math

import jax
import jax.numpy as jnp
import numpy as np
from jax import lax
from jax.experimental import pallas as pl
from jax.experimental.pallas import tpu as pltpu
from jax.sharding import Mesh
from jax.sharding import PartitionSpec as P

F32 = jnp.float32
BF16 = jnp.bfloat16
SEQ = ("x", "yl")
REP = ("z", "yh", "core")
X, YL, Z, YH, CORE = 4, 2, 4, 2, 2
ROWS = 256


def tables(length):
    odd = 2 * np.arange(length, dtype=np.int64)[:, None] + 1
    phase = odd * np.arange(length, dtype=np.int64)[None, :] % (4 * length)
    angle = phase.astype(np.float64) * (math.pi / (2 * length))
    return (np.cos(angle), np.sin(angle))


def dot(a, b):
    return jnp.dot(a, b, preferred_element_type=F32)


def up(x, axis):
    n = lax.axis_size(axis)
    return lax.ppermute(x, axis, [(i, (i + 1) % n) for i in range(n)])


def down(x, axis):
    n = lax.axis_size(axis)
    return lax.ppermute(x, axis, [(i, (i - 1) % n) for i in range(n)])


def swap(x, axis):
    return lax.ppermute(x, axis, [(0, 1), (1, 0)])


def pick(x, index, axis=0):
    return lax.dynamic_index_in_dim(x, index, axis, keepdims=False)


def halves_round(block, axis):
    lower = up(block, axis)
    upper = down(block, axis)
    half = block.shape[0] // 2
    return block, upper, lower, up(lower[:half], axis), down(upper[half:], axis)


def in_order(own, other, index):
    return jnp.where(index == 0, jnp.stack([own, other]), jnp.stack([other, own]))


def places(position, size):
    far = lax.rem(position + 2, size)
    return (
        (position, None),
        (lax.rem(position + 1, size), None),
        (lax.rem(position + size - 1, size), None),
        (far, 0),
        (far, 1),
    )


def transforms_body(place, *refs):
    slices, (cos, sin, cos_t, sin_t), thin, late, early, early_own, early_far, rest = (
        refs[0], refs[1:5], refs[5:10], refs[10:15], refs[15:20], refs[20], refs[21], refs[22:]
    )
    (
        pair_o, mine_o, send_o, acts_v, inner_v, w_v, taps_v, c_v, s_v, ct_v, st_v, fc, fs, ic, js, vc, vs, p, q,
        vals, sem,
    ) = rest
    xs, yls, block, features = acts_v.shape
    groups = xs * yls
    length, part = vals.shape
    scale = 1.0 / math.sqrt(length * Z * YH * CORE)
    x, yl, z, core = (place[i] for i in range(4))
    cut = late[0].shape[2]
    half = taps_v.shape[4] // CORE
    copies = []

    def move(src, dst):
        copies.append(pltpu.make_async_copy(src, dst, sem.at[len(copies)]))
        copies[-1].start()

    def waiter(first, last):
        def wait():
            for copy in copies[first:last]:
                copy.wait()

        return wait

    for ref, (to, side) in zip(thin, places(z, Z)):
        for n in (0, 1) if side is None else (side,):
            c = core if n == 0 else 1 - core
            src = ref.at[n if side is None else 0]
            move(src.at[:, :, :, part:], taps_v.at[:, to, :, :, pl.ds(pl.multiple_of(c * half, half), half)])
    move(cos, c_v)
    move(sin, s_v)
    wait_taps = waiter(0, len(copies))
    mark = len(copies)
    lines = slices.shape[1]
    for n in range(block // lines):
        left = slices.shape[2] - part * (block // lines - n)
        move(slices.at[:, :, left : left + part], inner_v.at[:, n * lines : (n + 1) * lines, :])
    wait_inner = waiter(mark, len(copies))
    mark = len(copies)
    move(cos_t, ct_v)
    move(sin_t, st_v)
    wait_inverse = waiter(mark, len(copies))
    mark = len(copies)
    for ref, (to, side) in zip(late, places(x, X)):
        if side is None:
            move(ref, acts_v.at[to, :, :, :cut])
        else:
            move(ref.at[0], acts_v.at[to, side, :, :cut])
    n = block // 2
    for i, (ref, (to, side)) in enumerate(zip(early, places(x, X))):
        across = early_own.at[i] if side is None else early_far.at[side]
        for src, y in ((ref, yl), (across, 1 - yl)):
            dst = acts_v.at[to, y]
            if side is None:
                move(src, dst.at[:, cut:])
            else:
                move(src, dst.at[side * n : (side + 1) * n, cut:])
    wait_acts = waiter(mark, len(copies))
    mark = len(copies)
    for ref, (to, side) in zip(thin, places(z, Z)):
        for n in (0, 1) if side is None else (side,):
            c = core if n == 0 else 1 - core
            src = ref.at[n if side is None else 0]
            move(src.at[:, :, :, :part], w_v.at[:, to, :, c])
    wait_weight = waiter(mark, len(copies))
    weight = w_v.reshape(features, part)
    taps = taps_v.reshape(length, part)
    acts = acts_v.reshape(length, features)
    inner = inner_v.reshape(length, part)
    per = ROWS // block

    def each(count, step):
        @pl.loop(0, count // ROWS)
        def _(i):
            step(i, pl.ds(pl.multiple_of(i * ROWS, ROWS), ROWS))

    def spectrum(x, cos_sum, sin_sum):
        def step(i, r):
            cos_sum[r, :] = dot(c_v[r, :], x[...])
            sin_sum[r, :] = dot(s_v[r, :], x[...])

        each(length, step)

    def product(fn):
        def step(i, r):
            a, b = fn(r)
            p[r, :] = a.astype(BF16)
            q[r, :] = b.astype(BF16)

        each(length, step)

    def inverse(r):
        return (dot(ct_v[r, :], p[...]) + dot(st_v[r, :], q[...])) * (1.0 / length)

    def by_core(x, rows):
        x = x.reshape(-1, CORE, rows, part)
        own = core == 0
        return jnp.where(own, x[:, 0], x[:, 1]), jnp.where(own, x[:, 1], x[:, 0])

    wait_taps()
    spectrum(taps, fc, fs)
    wait_inner()
    spectrum(inner, ic, js)
    product(lambda r: (fc[r, :] * ic[r, :] + fs[r, :] * js[r, :], fc[r, :] * js[r, :] - fs[r, :] * ic[r, :]))
    wait_inverse()

    def grad_step(i, r):
        g = inverse(r).astype(BF16)
        vals[r, :] = g
        pair_o[pl.ds(i * per, per), :, part:] = g.reshape(per, block, part)

    each(length, grad_step)
    wait_acts()

    def weight_step(i, r):
        g = lax.dot_general(acts[:, r], vals[...], (((0,), (0,)), ((), ())), preferred_element_type=F32) * scale
        own, other = by_core(g, 16)
        n = ROWS // (CORE * 16)
        mine_o[pl.ds(i * n, n), :16] = own
        send_o[pl.ds(i * n, n), :16] = other

    each(features, weight_step)
    wait_weight()

    def value_step(i, r):
        vals[r, :] = dot(acts[r, :], weight[...]).astype(BF16)

    each(length, value_step)
    spectrum(vals, vc, vs)
    product(lambda r: (fc[r, :] * vc[r, :] - fs[r, :] * vs[r, :], fc[r, :] * vs[r, :] + fs[r, :] * vc[r, :]))

    def conv_step(i, r):
        pair_o[pl.ds(i * per, per), :, :part] = inverse(r).astype(BF16).reshape(per, block, part)

    each(length, conv_step)
    product(lambda r: (vc[r, :] * ic[r, :] + vs[r, :] * js[r, :], vc[r, :] * js[r, :] - vs[r, :] * ic[r, :]))

    def filter_step(i, r):
        own, other = by_core(inverse(r) * scale, 8)
        n = ROWS // (CORE * 8)
        mine_o[pl.ds(i * n, n), 16:] = own
        send_o[pl.ds(i * n, n), 16:] = other

    each(length, filter_step)


def transforms(place, slices, tables_v, thin, late, early, early_own, early_far):
    length = tables_v[0].shape[0]
    block = length // (X * YL)
    part = thin[0].shape[4] * 2 // 3
    features = late[0].shape[2] + early[0].shape[1]
    away = pl.BlockSpec(memory_space=pl.ANY)
    near = pl.BlockSpec(memory_space=pltpu.VMEM)
    shape = jax.ShapeDtypeStruct
    own = features // (CORE * 16)
    wave = pltpu.VMEM((length, part), F32)
    narrow = pltpu.VMEM((length, part), BF16)
    table = pltpu.VMEM((length, length), BF16)
    operands = (slices, *tables_v, *thin, *late, *early, early_own, early_far)
    return pl.pallas_call(
        transforms_body,
        out_shape=[shape((X * YL, block, 2 * part), BF16)] + [shape((own, 24, part), F32)] * 2,
        in_specs=[pl.BlockSpec(memory_space=pltpu.SMEM)] + [away] * len(operands),
        out_specs=[near] * 3,
        scratch_shapes=[
            pltpu.VMEM((X, YL, block, features), BF16),
            pltpu.VMEM((X * YL, block, part), BF16),
            pltpu.VMEM((X * YL, Z, YH, CORE, 16, part), BF16),
            pltpu.VMEM((X * YL, Z, YH, 16, part), BF16),
            *[table] * 4,
            *[wave] * 6,
            *[narrow] * 3,
            pltpu.SemaphoreType.DMA((48,)),
        ],
        compiler_params=pltpu.CompilerParams(vmem_limit_bytes=48 * 2**20),
        name="transforms",
    )(place, *operands)


def outputs_body(place, back, gates, upstream, *refs):
    pieces, (mixed_o, gate_o, input_o, w_v, grad_v, sem) = refs[:10], refs[10:]
    groups, block, _ = back.shape
    part = back.shape[2] // 2
    z, core = place[2], place[3]
    copies = []
    for n, c in ((0, core), (1, 1 - core)):
        for ref, (to, side) in zip(pieces[5 * n : 5 * n + 5], places(z, Z)):
            some = pl.ds(0, groups) if side is None else pl.ds(side * groups // 2, groups // 2)
            copies.append(pltpu.make_async_copy(ref, w_v.at[some, to, :, c], sem.at[len(copies)]))
    for copy in copies:
        copy.start()
    for g in range(groups):
        c = pl.ds(g * part, part)
        conv = back[g, :, :part].astype(F32)
        mixed_o[:, c] = (gates[:, c].astype(F32) * conv).astype(BF16)
        gate_o[:, c] = (upstream[:, c].astype(F32) * conv).astype(BF16)
        grad_v[:, c] = back[g, :, part:]
    for copy in copies:
        copy.wait()
    rows = w_v.shape[4]
    for g in range(groups):
        w = w_v[g].reshape(Z * YH * CORE * rows, w_v.shape[5])
        n = w.shape[0]
        y = lax.dot_general(grad_v[...], w, (((1,), (1,)), ((), ())), preferred_element_type=F32)
        input_o[:, pl.ds(g * n, n)] = y.astype(BF16)


def outputs(place, back, gates, upstream, pieces):
    groups, block, _ = back.shape
    channels = gates.shape[1]
    rows = pieces[0].shape[2]
    features = groups * Z * YH * CORE * rows
    away = pl.BlockSpec(memory_space=pl.ANY)
    near = pl.BlockSpec(memory_space=pltpu.VMEM)
    shape = jax.ShapeDtypeStruct
    return pl.pallas_call(
        outputs_body,
        out_shape=[shape((block, channels), BF16)] * 2 + [shape((block, features), BF16)],
        in_specs=[pl.BlockSpec(memory_space=pltpu.SMEM)] + [near] * 3 + [away] * 10,
        out_specs=[near] * 3,
        scratch_shapes=[
            pltpu.VMEM((groups, Z, YH, CORE, rows, channels), BF16),
            pltpu.VMEM((block, channels), BF16),
            pltpu.SemaphoreType.DMA((10,)),
        ],
        compiler_params=pltpu.CompilerParams(vmem_limit_bytes=32 * 2**20),
        name="outputs",
    )(place, back, gates, upstream, *pieces)


def local(activations, gate_values, in_weight, long_filter, out_cotangent):
    tokens = activations[0]
    gates = gate_values[0]
    upstream = out_cotangent[0]
    groups = X * YL
    replicas = Z * YH * CORE
    block, channels = gates.shape
    features = tokens.shape[1]
    length = block * groups
    part = channels // groups
    rows = in_weight.shape[0]
    shared = rows
    half = part // CORE
    cut = features * 5 // 8
    xi, yi, zi, hi, ci = (lax.axis_index(a) for a in SEQ + REP)
    place = jnp.stack([xi, yi, zi, ci])

    cosine, sine = (jnp.asarray(t.astype(np.float32)).astype(BF16) for t in tables(length))
    cosine_t, sine_t = (jnp.asarray(t.T.astype(np.float32)).astype(BF16) for t in tables(length))

    own_taps = lax.dynamic_slice_in_dim(long_filter, (zi * YH + hi) * shared, shared, 0)
    own_taps = pick(own_taps.reshape(shared, groups, CORE, half), ci, 2).reshape(shared, groups * half)
    piece = jnp.concatenate([in_weight, own_taps], axis=1)
    piece = in_order(piece, swap(piece, "yh"), hi).reshape(YH * rows, channels + groups * half)
    inner = (upstream.astype(F32) * gates.astype(F32)).astype(BF16)
    inner = inner.reshape(block // (YH * rows), YH * rows, groups, part).transpose(2, 1, 0, 3)
    sent = jnp.concatenate(
        [
            jnp.broadcast_to(piece[:, :channels], (groups, YH * rows, channels)),
            piece[:, channels:].reshape(YH * rows, groups, half).transpose(1, 0, 2),
            inner.reshape(groups, YH * rows, -1),
        ],
        axis=2,
    )
    slices = lax.all_to_all(sent, SEQ, 0, 0, tiled=True)

    thin = jnp.concatenate(
        [
            lax.dynamic_slice_in_dim(slices, (xi * YL + yi) * part, part, 2),
            slices[:, :, channels : channels + half],
        ],
        axis=2,
    ).reshape(groups, YH, rows, part + half)
    thin = halves_round(jnp.stack([thin, swap(thin, "core")]), "z")
    wide = halves_round(slices[:, :, :channels].reshape(groups, YH, rows, channels), "z")
    wide = wide + tuple(swap(w, "core") for w in wide)

    early = halves_round(tokens[:, cut:], "x")
    late = halves_round(in_order(tokens[:, :cut], swap(tokens[:, :cut], "yl"), yi), "x")
    early_own = swap(jnp.stack(early[:3]), "yl")
    early_far = swap(jnp.stack(early[3:]), "yl")

    pair, mine, other = transforms(
        place, slices, (cosine, sine, cosine_t, sine_t), thin, late, early, early_own, early_far
    )

    back = lax.all_to_all(pair, SEQ, 0, 0, tiled=True)
    owned = (mine + swap(other, "core")).astype(BF16)
    owned = lax.all_to_all(owned, SEQ + ("z", "yh"), 0, 0, tiled=True)
    owned = jnp.sum(owned.reshape(groups, Z * YH, -1, part).astype(F32), axis=1)
    owned = owned.transpose(1, 0, 2).reshape(-1, channels)

    mixed_out, gate_grad, input_grad = outputs(place, back, gates, upstream, wide)
    return (mixed_out[None], gate_grad[None], input_grad[None], owned[:rows], owned[rows:])


def solution(mesh):
    mesh = Mesh(mesh.devices.reshape(X, YL, Z, YH, CORE), SEQ + REP)
    split = P(REP, SEQ, None)
    in_specs = (split, split, P(SEQ + REP, None), P(SEQ, None), split)
    out_specs = (split, split, split, P(SEQ + REP, None), P(SEQ + REP, None))
    return jax.shard_map(local, mesh=mesh, in_specs=in_specs, out_specs=out_specs, check_vma=False)
```

time: 203 us -> 186 us (0.916); the launches traced: 202 us -> 183 us
  waiting for transfers between devices: 107 us -> 84.4 us
  starting transfers between devices: 46.4 us -> 49.8 us
  Pallas kernels: 25.8 us -> 28.4 us
  other arithmetic: 9.29 us -> 6.75 us
    ppermute x6 -> x8, waiting for transfers between devices: 73.7 us -> 35.7 us  [up(): return lax.ppermute(x, axis, [(i, (i + 1) % n) for i in range(n)])]
    ppermute x10 -> x11, waiting for transfers between devices: 18.4 us -> 37 us  [swap(): return lax.ppermute(x, axis, [(0, 1), (1, 0)])]
    all_to_all x1, waiting for transfers between devices: 6.44 us -> 0.01 us  [local(): back = lax.all_to_all(pair, SEQ, 0, 0, tiled=True)]
    ppermute x6 -> x8, waiting for transfers between devices: 3.22 us -> 7.61 us  [down(): return lax.ppermute(x, axis, [(i, (i - 1) % n) for i in range(n)])]
    unnamed x23 -> x13, local copies, waits for them, and re-layouts: 6.41 us -> 3.05 us
    ppermute x6 -> x8, starting transfers between devices: 2.71 us -> 5.71 us  [up(): return lax.ppermute(x, axis, [(i, (i + 1) % n) for i in range(n)])]
    pallas_call x1, Pallas kernels: 18.6 us -> 21.2 us  [transforms(): pl.pallas_call(transforms_body, out_shape=[shape((X * YL, block, 2 * part...]
    ppermute x6 -> x8, starting transfers between devices: 18.8 us -> 19.5 us  [down(): return lax.ppermute(x, axis, [(i, (i - 1) % n) for i in range(n)])]
  transfers between devices with their start and end apart: 25 -> 30, of which waited for: 12 -> 13; matrix products, arithmetic and copies ran while one was open for 7% -> 7% of each run, Pallas kernels for 13% -> 4%
where the time goes in v5:
time: 186 us; the launch traced here: 183 us
  waiting for transfers between devices  84.4 us (45%)
  starting transfers between devices  49.8 us (27%)
  Pallas kernels  28.4 us (15%)
  local copies, waits for them, and re-layouts  12.5 us (7%)
  other arithmetic  6.75 us (4%)
    ppermute x11, waiting for transfers between devices, swap(): return lax.ppermute(x, axis, [(0, 1), (1, 0)])  37 us
    ppermute x8, waiting for transfers between devices, up(): return lax.ppermute(x, axis, [(i, (i + 1) % n) for i in range(n)])  35.7 us
    pallas_call x1, Pallas kernels, transforms(): pl.pallas_call(transforms_body, out_shape=[shape((X * YL, block, 2 * part...  21.2 us
    ppermute x8, starting transfers between devices, down(): return lax.ppermute(x, axis, [(i, (i - 1) % n) for i in range(n)])  19.5 us
    ppermute x11, starting transfers between devices, swap(): return lax.ppermute(x, axis, [(0, 1), (1, 0)])  8.36 us
    ppermute x8, waiting for transfers between devices, down(): return lax.ppermute(x, axis, [(i, (i - 1) % n) for i in range(n)])  7.61 us
    pallas_call x1, Pallas kernels, outputs(): pl.pallas_call(outputs_body, out_shape=[shape((block, channels), BF16)] *...  7.16 us
    all_to_all x1, starting transfers between devices, local(): owned = lax.all_to_all(owned, SEQ + ('z', 'yh'), 0, 0, tiled=True)  6.84 us
  transfers between devices with their start and end apart: 30, of which 13 were waited for; matrix products, arithmetic and copies ran while one was open for 7% of the time, Pallas kernels for 4%

profile of v5, /device:TPU:0, one launch (start us, length us, event | category | flops | bytes accessed | tf_op | source)
XLA Modules:
  0.0 182.8 jit_solution(5326019394842520364)
XLA Ops:
  0.6 0.0 copy-start
  0.7 1.0 copy-done
  1.7 0.8 constant_dynamic-update-slice_fusion
  2.6 0.2 dynamic-slice_reduce_fusion
  2.8 3.4 %collective-permute-start = (bf16[16,3072]{1,0:T(8,128)(2,1)S(1)}, bf16[16,3072]{1,0:T(8,128)(2,1)S(1)}, u32[]{:S(2)}, u32[]{:S(2)}) collective-permute-start(bf16[16,3072]{1,0:T(8,128)(2,1)S(1)} %bitcast_dynamic-update-slice_fusion), channel_id=1, source_target_pairs={{0,2},{2,0},{1,3},{3,1},{4,6},{6,4},{5,7},{7,5},{8,10},{10,8},{9,1... | collective-permute-start | bytes 294920 | tf_op jit(solution)/shard_map/ppermute | solution.py:42
  6.1 1.3 multiply_convert_fusion
  7.5 0.1 copy.25
  7.6 0.4 copy.29
  8.0 0.4 reshape.50
  8.4 0.6 collective-permute-done
  9.0 0.1 broadcast_in_dim.12
  9.2 1.3 pad_maximum_fusion
  10.5 5.5 %all-to-all-start = ((bf16[8,32,3200]{2,1,0:T(8,128)(2,1)}), bf16[8,32,3200]{2,1,0:T(8,128)(2,1)}, u32[]{:S(2)}, u32[]{:S(2)}) async-start(bf16[8,32,3200]{2,1,0:T(8,128)(2,1)} %pad_maximum_fusion), calls=%async_computation | async-start | bytes 3276800 | tf_op jit(solution)/shard_map/all_to_all | solution.py:339
  16.1 2.1 %collective-permute-start.6 = (bf16[128,1280]{1,0:T(8,128)(2,1)S(1)}, bf16[128,1280]{1,0:T(8,128)(2,1)S(1)}, u32[]{:S(2)}, u32[]{:S(2)}) collective-permute-start(bf16[128,1280]{1,0:T(8,128)(2,1)S(1)} %get-tuple-element.20), channel_id=1, source_target_pairs={{0,16},{16,0},{1,17},{17,1},{2,18},{18,2},{3,19},{19,3},{4,20},{20... | collective-permute-start | bytes 983048 | tf_op jit(solution)/shard_map/ppermute | solution.py:42
  18.1 23.6 %collective-permute-done.6 = bf16[128,1280]{1,0:T(8,128)(2,1)S(1)} collective-permute-done((bf16[128,1280]{1,0:T(8,128)(2,1)S(1)}, bf16[128,1280]{1,0:T(8,128)(2,1)S(1)}, u32[]{:S(2)}, u32[]{:S(2)}) %collective-permute-start.6) | collective-permute-done | bytes 327712 | tf_op jit(solution)/shard_map/ppermute | solution.py:42
  41.8 0.1 maximum_select_fusion.refs_10_
  41.9 2.7 %collective-permute-start.7 = (bf16[2,128,1280]{2,1,0:T(8,128)(2,1)S(1)}, bf16[2,128,1280]{2,1,0:T(8,128)(2,1)S(1)}, u32[]{:S(2)}, u32[]{:S(2)}) collective-permute-start(bf16[2,128,1280]{2,1,0:T(8,128)(2,1)S(1)} %maximum_select_fusion.refs_10_), channel_id=1, source_target_pairs={{0,96},{32,0},{64,32},{96,64},{1,97},{33,1},{65,33},{97,65},{2,98}... | collective-permute-start | bytes 1966088 | tf_op jit(solution)/shard_map/ppermute | solution.py:38
  44.6 0.8 slice.75
  45.5 0.9 constant_dynamic-slice_fusion
  46.4 0.1 collective-permute-start.1
  46.6 0.9 collective-permute-start.12
  47.4 2.5 %collective-permute-start.11 = (bf16[128,768]{1,0:T(8,128)(2,1)S(1)}, bf16[128,768]{1,0:T(8,128)(2,1)S(1)}, u32[]{:S(2)}, u32[]{:S(2)}) collective-permute-start(bf16[128,768]{1,0:T(8,128)(2,1)S(1)} %get-tuple-element.18.refs_15_), channel_id=1, source_target_pairs={{0,96},{32,0},{64,32},{96,64},{1,97},{33,1},{65,33},{97,65},{2,98}... | collective-permute-start | bytes 589832 | tf_op jit(solution)/shard_map/ppermute | solution.py:38
  50.0 2.0 %collective-permute-start.3 = (bf16[2,8,2,16,384]{4,3,2,1,0:T(8,128)(2,1)S(1)}, bf16[2,8,2,16,384]{4,3,2,1,0:T(8,128)(2,1)S(1)}, u32[]{:S(2)}, u32[]{:S(2)}) collective-permute-start(bf16[2,8,2,16,384]{4,3,2,1,0:T(8,128)(2,1)S(1)} %pad_maximum_fusion.2.refs_5_), channel_id=1, source_target_pairs={{0,4},{4,8},{8,12},{12,0},{1,5},{5,9},{9,13},{13,1},{2,6},{6,10},{... | collective-permute-start | bytes 1179656 | tf_op jit(solution)/shard_map/ppermute | solution.py:33
  52.0 13.4 %collective-permute-done.12.refs_17_ = bf16[128,768]{1,0:T(8,128)(2,1)S(1)} collective-permute-done((bf16[128,768]{1,0:T(8,128)(2,1)S(1)}, bf16[128,768]{1,0:T(8,128)(2,1)S(1)}, u32[]{:S(2)}, u32[]{:S(2)}) %collective-permute-start.12) | collective-permute-done | bytes 196640 | tf_op jit(solution)/shard_map/ppermute | solution.py:33
  65.4 0.1 collective-permute-start.13
  65.5 3.3 %collective-permute-start.14 = (bf16[64,768]{1,0:T(8,128)(2,1)S(1)}, bf16[64,768]{1,0:T(8,128)(2,1)S(1)}, u32[]{:S(2)}, u32[]{:S(2)}) collective-permute-start(bf16[64,768]{1,0:T(8,128)(2,1)S(1)} %slice.83), channel_id=1, source_target_pairs={{0,96},{32,0},{64,32},{96,64},{1,97},{33,1},{65,33},{97,65},{2,98}... | collective-permute-start | bytes 294920 | tf_op jit(solution)/shard_map/ppermute | solution.py:38
  68.8 0.1 pad_maximum_fusion.1
  68.9 2.4 %collective-permute-done.13.refs_18_ = bf16[64,768]{1,0:T(8,128)(2,1)S(1)} collective-permute-done((bf16[64,768]{1,0:T(8,128)(2,1)S(1)}, bf16[64,768]{1,0:T(8,128)(2,1)S(1)}, u32[]{:S(2)}, u32[]{:S(2)}) %collective-permute-start.13) | collective-permute-done | bytes 98336 | tf_op jit(solution)/shard_map/ppermute | solution.py:33
  71.3 4.0 %collective-permute-start.2 = (bf16[2,8,2,16,384]{4,3,2,1,0:T(8,128)(2,1)S(1)}, bf16[2,8,2,16,384]{4,3,2,1,0:T(8,128)(2,1)S(1)}, u32[]{:S(2)}, u32[]{:S(2)}) collective-permute-start(bf16[2,8,2,16,384]{4,3,2,1,0:T(8,128)(2,1)S(1)} %pad_maximum_fusion.2.refs_5_), channel_id=1, source_target_pairs={{0,12},{4,0},{8,4},{12,8},{1,13},{5,1},{9,5},{13,9},{2,14},{6,2},{... | collective-permute-start | bytes 1179656 | tf_op jit(solution)/shard_map/ppermute | solution.py:38
  75.4 1.3 collective-permute-start.15
  76.7 0.8 collective-permute-start.16
  77.5 0.1 collective-permute-start.10
  77.7 2.1 %collective-permute-start.9 = (bf16[1,128,1280]{2,1,0:T(8,128)(2,1)S(1)}, bf16[1,128,1280]{2,1,0:T(8,128)(2,1)S(1)}, u32[]{:S(2)}, u32[]{:S(2)}) collective-permute-start(bf16[1,128,1280]{2,1,0:T(8,128)(2,1)S(1)} %slice.79), channel_id=1, source_target_pairs={{0,32},{32,64},{64,96},{96,0},{1,33},{33,65},{65,97},{97,1},{2,34}... | collective-permute-start | bytes 983048 | tf_op jit(solution)/shard_map/ppermute | solution.py:33
  79.8 0.9 collective-permute-done.2.refs_6_
  80.7 0.4 collective-permute-start.4
  81.1 10.7 %collective-permute-done.16.refs_21_ = bf16[2,64,768]{2,1,0:T(8,128)(2,1)S(1)} collective-permute-done((bf16[2,64,768]{2,1,0:T(8,128)(2,1)S(1)}, bf16[2,64,768]{2,1,0:T(8,128)(2,1)S(1)}, u32[]{:S(2)}, u32[]{:S(2)}) %collective-permute-start.16) | collective-permute-done | bytes 196640 | tf_op jit(solution)/shard_map/ppermute | solution.py:42
  91.8 0.4 collective-permute-start.5
  92.2 0.1 pad_add_fusion.place
  92.3 5.2 %collective-permute-done.5.refs_9_ = bf16[1,8,2,16,384]{4,3,2,1,0:T(8,128)(2,1)S(1)} collective-permute-done((bf16[1,8,2,16,384]{4,3,2,1,0:T(8,128)(2,1)S(1)}, bf16[1,8,2,16,384]{4,3,2,1,0:T(8,128)(2,1)S(1)}, u32[]{:S(2)}, u32[]{:S(2)}) %collective-permute-start.5) | collective-permute-done | bytes 196640 | tf_op jit(solution)/shard_map/ppermute | solution.py:38
  97.5 21.2 %transforms.1 = (bf16[8,128,512]{2,1,0:T(8,128)(2,1)}, f32[64,24,256]{2,1,0:T(8,128)}, f32[64,24,256]{2,1,0:T(8,128)}) custom-call(s32[4]{0:T(128)S(1)} %pad_add_fusion.place, bf16[8,32,3200]{2,1,0:T(8,128)(2,1)} %all-to-all-done.refs_0_, bf16[1024,1024]{1,0:T(8,128)(2,1)} %constant.53.refs_1_, bf16[1024,1024]{1,0:T(8,128)(2,1)} %constant.54.refs_2_, ...), custom_call_target="tpu_custom_call" | custom-call | tf_op jit(solution)/shard_map/transforms/pallas_call | solution.py:234
  118.7 0.1 collective-permute-start.26
  118.8 1.3 slice.84
  120.1 0.3 collective-permute-start.18
  120.4 3.2 %collective-permute-start.17 = (bf16[8,2,16,2048]{3,2,1,0:T(8,128)(2,1)S(1)}, bf16[8,2,16,2048]{3,2,1,0:T(8,128)(2,1)}, u32[]{:S(2)}, u32[]{:S(2)}) collective-permute-start(bf16[8,2,16,2048]{3,2,1,0:T(8,128)(2,1)S(1)} %bitcast.52), channel_id=1, source_target_pairs={{0,12},{4,0},{8,4},{12,8},{1,13},{5,1},{9,5},{13,9},{2,14},{6,2},{... | collective-permute-start | bytes 3145736 | tf_op jit(solution)/shard_map/ppermute | solution.py:38
  123.6 3.8 %all-to-all-start.1 = ((bf16[8,128,512]{2,1,0:T(8,128)(2,1)}), bf16[8,128,512]{2,1,0:T(8,128)(2,1)S(1)}, u32[]{:S(2)}, u32[]{:S(2)}) async-start(bf16[8,128,512]{2,1,0:T(8,128)(2,1)} %get-tuple-element.11), calls=%async_computation.1 | async-start | bytes 2097152 | tf_op jit(solution)/shard_map/all_to_all | solution.py:361
  127.4 0.1 collective-permute-start.21
  127.5 19.7 %collective-permute-done.18.refs_2_ = bf16[8,2,16,2048]{3,2,1,0:T(8,128)(2,1)} collective-permute-done((bf16[8,2,16,2048]{3,2,1,0:T(8,128)(2,1)S(1)}, bf16[8,2,16,2048]{3,2,1,0:T(8,128)(2,1)}, u32[]{:S(2)}, u32[]{:S(2)}) %collective-permute-start.18) | collective-permute-done | bytes 1048608 | tf_op jit(solution)/shard_map/ppermute | solution.py:33
  147.2 1.9 %slice.85 = bf16[4,2,16,2048]{3,2,1,0:T(8,128)(2,1)} slice(bf16[8,2,16,2048]{3,2,1,0:T(8,128)(2,1)} %collective-permute-done.18.refs_2_), slice={[0:4], [0:2], [0:16], [0:2048]} | slice | bytes 1048576 | tf_op jit(solution)/shard_map/slice | solution.py:53
  149.1 1.9 %slice.86 = bf16[4,2,16,2048]{3,2,1,0:T(8,128)(2,1)} slice(bf16[8,2,16,2048]{3,2,1,0:T(8,128)(2,1)} %collective-permute-done.17.refs_1_), slice={[4:8], [0:2], [0:16], [0:2048]} | slice | bytes 1048576 | tf_op jit(solution)/shard_map/slice | solution.py:53
  151.0 3.2 %collective-permute-start.20 = (bf16[4,2,16,2048]{3,2,1,0:T(8,128)(2,1)}, bf16[4,2,16,2048]{3,2,1,0:T(8,128)(2,1)}, u32[]{:S(2)}, u32[]{:S(2)}) collective-permute-start(bf16[4,2,16,2048]{3,2,1,0:T(8,128)(2,1)} %slice.86), channel_id=1, source_target_pairs={{0,12},{4,0},{8,4},{12,8},{1,13},{5,1},{9,5},{13,9},{2,14},{6,2},{... | collective-permute-start | bytes 1572872 | tf_op jit(solution)/shard_map/ppermute | solution.py:38
  154.2 0.5 collective-permute-start.23
  154.7 2.5 %add_convert_fusion = bf16[64,24,256]{2,1,0:T(8,128)(2,1)} fusion(f32[64,24,256]{2,1,0:T(8,128)S(1)} %copy-done.3, f32[64,24,256]{2,1,0:T(8,128)} %collective-permute-done.26), kind=kLoop, calls=%fused_computation.2 | loop fusion | flops 786432 | bytes 3932160 | tf_op jit(solution)/shard_map/convert_element_type | solution.py:362
  157.3 6.8 %all-to-all-start.2 = ((bf16[64,24,256]{2,1,0:T(8,128)(2,1)}), bf16[64,24,256]{2,1,0:T(8,128)(2,1)}, u32[]{:S(2)}, u32[]{:S(2)}) async-start(bf16[64,24,256]{2,1,0:T(8,128)(2,1)} %add_convert_fusion), calls=%async_computation.2 | async-start | bytes 1572864 | tf_op jit(solution)/shard_map/all_to_all | solution.py:363
  164.1 0.1 collective-permute-done.19.refs_3_
  164.2 0.0 collective-permute-start.24
  164.2 1.5 collective-permute-done.20.refs_4_
  165.8 0.6 collective-permute-done.24.refs_8_
  166.3 1.6 collective-permute-done.25.refs_9_
  167.9 1.0 copy-done.2
  168.9 7.2 %outputs.1 = (bf16[128,2048]{1,0:T(8,128)(2,1)}, bf16[128,2048]{1,0:T(8,128)(2,1)}, bf16[128,2048]{1,0:T(8,128)(2,1)}) custom-call(s32[4]{0:T(128)S(1)} %pad_add_fusion.place, bf16[8,128,512]{2,1,0:T(8,128)(2,1)S(1)} %all-to-all-done.1.back, bf16[128,2048]{1,0:T(8,128)(2,1)S(1)} %bitcast.55, bf16[128,2048]{1,0:T(8,128)(2,1)S(1)} %bitcast.56, ...), custom_call_target="tpu_custom_call" | custom-call | tf_op jit(solution)/shard_map/outputs/pallas_call | solution.py:290
  176.1 4.1 %all-to-all-done.2 = bf16[64,24,256]{2,1,0:T(8,128)(2,1)} async-done(((bf16[64,24,256]{2,1,0:T(8,128)(2,1)}), bf16[64,24,256]{2,1,0:T(8,128)(2,1)}, u32[]{:S(2)}, u32[]{:S(2)}) %all-to-all-start.2) | async-done | bytes 786464 | tf_op jit(solution)/shard_map/all_to_all | solution.py:363
  180.2 1.3 convert_reduce_fusion
  181.5 0.6 slice.88
  182.1 0.7 copy.23
  (46 shorter events, 0.4 us)
Async XLA Ops:
  0.6 1.0 copy-start
  2.8 6.2 %collective-permute-start = (bf16[16,3072]{1,0:T(8,128)(2,1)S(1)}, bf16[16,3072]{1,0:T(8,128)(2,1)S(1)}, u32[]{:S(2)}, u32[]{:S(2)}) collective-permute-start(bf16[16,3072]{1,0:T(8,128)(2,1)S(1)} %bitcast_dynamic-update-slice_fusion), channel_id=1, source_target_pairs={{0,2},{2,0},{1,3},{3,1},{4,6},{6,4},{5,7},{7,5},{8,10},{10,8},{9,1... | collective-permute-start | bytes 294920 | tf_op jit(solution)/shard_map/ppermute | solution.py:42
  10.5 5.5 %copy-start.4 = (bf16[1,128,2048]{2,1,0:T(8,128)(2,1)S(1)}, bf16[1,128,2048]{2,1,0:T(8,128)(2,1)}, u32[]{:S(2)}) copy-start(bf16[1,128,2048]{2,1,0:T(8,128)(2,1)} %param.9) | copy-start | bytes 1572868
  10.5 34.2 %all-to-all-start = ((bf16[8,32,3200]{2,1,0:T(8,128)(2,1)}), bf16[8,32,3200]{2,1,0:T(8,128)(2,1)}, u32[]{:S(2)}, u32[]{:S(2)}) async-start(bf16[8,32,3200]{2,1,0:T(8,128)(2,1)} %pad_maximum_fusion), calls=%async_computation | async-start | bytes 3276800 | tf_op jit(solution)/shard_map/all_to_all | solution.py:339
  16.1 25.7 %collective-permute-start.6 = (bf16[128,1280]{1,0:T(8,128)(2,1)S(1)}, bf16[128,1280]{1,0:T(8,128)(2,1)S(1)}, u32[]{:S(2)}, u32[]{:S(2)}) collective-permute-start(bf16[128,1280]{1,0:T(8,128)(2,1)S(1)} %get-tuple-element.20), channel_id=1, source_target_pairs={{0,16},{16,0},{1,17},{17,1},{2,18},{18,2},{3,19},{19,3},{4,20},{20... | collective-permute-start | bytes 983048 | tf_op jit(solution)/shard_map/ppermute | solution.py:42
  41.9 34.8 %collective-permute-start.7 = (bf16[2,128,1280]{2,1,0:T(8,128)(2,1)S(1)}, bf16[2,128,1280]{2,1,0:T(8,128)(2,1)S(1)}, u32[]{:S(2)}, u32[]{:S(2)}) collective-permute-start(bf16[2,128,1280]{2,1,0:T(8,128)(2,1)S(1)} %maximum_select_fusion.refs_10_), channel_id=1, source_target_pairs={{0,96},{32,0},{64,32},{96,64},{1,97},{33,1},{65,33},{97,65},{2,98}... | collective-permute-start | bytes 1966088 | tf_op jit(solution)/shard_map/ppermute | solution.py:38
  44.6 32.9 %collective-permute-start.8 = (bf16[2,128,1280]{2,1,0:T(8,128)(2,1)S(1)}, bf16[2,128,1280]{2,1,0:T(8,128)(2,1)S(1)}, u32[]{:S(2)}, u32[]{:S(2)}) collective-permute-start(bf16[2,128,1280]{2,1,0:T(8,128)(2,1)S(1)} %maximum_select_fusion.refs_10_), channel_id=1, source_target_pairs={{0,32},{32,64},{64,96},{96,0},{1,33},{33,65},{65,97},{97,1},{2,34}... | collective-permute-start | bytes 1966088 | tf_op jit(solution)/shard_map/ppermute | solution.py:33
  46.4 3.5 %collective-permute-start.1 = (bf16[8,2,16,384]{3,2,1,0:T(8,128)(2,1)S(1)}, bf16[8,2,16,384]{3,2,1,0:T(8,128)(2,1)S(1)}, u32[]{:S(2)}, u32[]{:S(2)}) collective-permute-start(bf16[8,2,16,384]{3,2,1,0:T(8,128)(2,1)S(1)} %bitcast.66), channel_id=1, source_target_pairs={{0,1},{1,0},{2,3},{3,2},{4,5},{5,4},{6,7},{7,6},{8,9},{9,8},{10,11... | collective-permute-start | bytes 589832 | tf_op jit(solution)/shard_map/ppermute | solution.py:42
  46.6 18.9 %collective-permute-start.12 = (bf16[128,768]{1,0:T(8,128)(2,1)S(1)}, bf16[128,768]{1,0:T(8,128)(2,1)S(1)}, u32[]{:S(2)}, u32[]{:S(2)}) collective-permute-start(bf16[128,768]{1,0:T(8,128)(2,1)S(1)} %get-tuple-element.18.refs_15_), channel_id=1, source_target_pairs={{0,32},{32,64},{64,96},{96,0},{1,33},{33,65},{65,97},{97,1},{2,34}... | collective-permute-start | bytes 589832 | tf_op jit(solution)/shard_map/ppermute | solution.py:33
  47.4 18.1 %collective-permute-start.11 = (bf16[128,768]{1,0:T(8,128)(2,1)S(1)}, bf16[128,768]{1,0:T(8,128)(2,1)S(1)}, u32[]{:S(2)}, u32[]{:S(2)}) collective-permute-start(bf16[128,768]{1,0:T(8,128)(2,1)S(1)} %get-tuple-element.18.refs_15_), channel_id=1, source_target_pairs={{0,96},{32,0},{64,32},{96,64},{1,97},{33,1},{65,33},{97,65},{2,98}... | collective-permute-start | bytes 589832 | tf_op jit(solution)/shard_map/ppermute | solution.py:38
  50.0 27.7 %collective-permute-start.3 = (bf16[2,8,2,16,384]{4,3,2,1,0:T(8,128)(2,1)S(1)}, bf16[2,8,2,16,384]{4,3,2,1,0:T(8,128)(2,1)S(1)}, u32[]{:S(2)}, u32[]{:S(2)}) collective-permute-start(bf16[2,8,2,16,384]{4,3,2,1,0:T(8,128)(2,1)S(1)} %pad_maximum_fusion.2.refs_5_), channel_id=1, source_target_pairs={{0,4},{4,8},{8,12},{12,0},{1,5},{5,9},{9,13},{13,1},{2,6},{6,10},{... | collective-permute-start | bytes 1179656 | tf_op jit(solution)/shard_map/ppermute | solution.py:33
  65.4 5.9 %collective-permute-start.13 = (bf16[64,768]{1,0:T(8,128)(2,1)S(1)}, bf16[64,768]{1,0:T(8,128)(2,1)S(1)}, u32[]{:S(2)}, u32[]{:S(2)}) collective-permute-start(bf16[64,768]{1,0:T(8,128)(2,1)S(1)} %slice.82), channel_id=1, source_target_pairs={{0,32},{32,64},{64,96},{96,0},{1,33},{33,65},{65,97},{97,1},{2,34}... | collective-permute-start | bytes 294920 | tf_op jit(solution)/shard_map/ppermute | solution.py:33
  65.5 9.8 %collective-permute-start.14 = (bf16[64,768]{1,0:T(8,128)(2,1)S(1)}, bf16[64,768]{1,0:T(8,128)(2,1)S(1)}, u32[]{:S(2)}, u32[]{:S(2)}) collective-permute-start(bf16[64,768]{1,0:T(8,128)(2,1)S(1)} %slice.83), channel_id=1, source_target_pairs={{0,96},{32,0},{64,32},{96,64},{1,97},{33,1},{65,33},{97,65},{2,98}... | collective-permute-start | bytes 294920 | tf_op jit(solution)/shard_map/ppermute | solution.py:38
  71.3 9.3 %collective-permute-start.2 = (bf16[2,8,2,16,384]{4,3,2,1,0:T(8,128)(2,1)S(1)}, bf16[2,8,2,16,384]{4,3,2,1,0:T(8,128)(2,1)S(1)}, u32[]{:S(2)}, u32[]{:S(2)}) collective-permute-start(bf16[2,8,2,16,384]{4,3,2,1,0:T(8,128)(2,1)S(1)} %pad_maximum_fusion.2.refs_5_), channel_id=1, source_target_pairs={{0,12},{4,0},{8,4},{12,8},{1,13},{5,1},{9,5},{13,9},{2,14},{6,2},{... | collective-permute-start | bytes 1179656 | tf_op jit(solution)/shard_map/ppermute | solution.py:38
  75.4 16.9 %collective-permute-start.15 = (bf16[3,128,768]{2,1,0:T(8,128)(2,1)S(1)}, bf16[3,128,768]{2,1,0:T(8,128)(2,1)S(1)}, u32[]{:S(2)}, u32[]{:S(2)}) collective-permute-start(bf16[3,128,768]{2,1,0:T(8,128)(2,1)S(1)} %pad_maximum_fusion.1), channel_id=1, source_target_pairs={{0,16},{16,0},{1,17},{17,1},{2,18},{18,2},{3,19},{19,3},{4,20},{20... | collective-permute-start | bytes 1769480 | tf_op jit(solution)/shard_map/ppermute | solution.py:42
  76.7 15.1 %collective-permute-start.16 = (bf16[2,64,768]{2,1,0:T(8,128)(2,1)S(1)}, bf16[2,64,768]{2,1,0:T(8,128)(2,1)S(1)}, u32[]{:S(2)}, u32[]{:S(2)}) collective-permute-start(bf16[2,64,768]{2,1,0:T(8,128)(2,1)S(1)} %pad_maximum_fusion.4), channel_id=1, source_target_pairs={{0,16},{16,0},{1,17},{17,1},{2,18},{18,2},{3,19},{19,3},{4,20},{20... | collective-permute-start | bytes 589832 | tf_op jit(solution)/shard_map/ppermute | solution.py:42
  77.5 14.7 %collective-permute-start.10 = (bf16[1,128,1280]{2,1,0:T(8,128)(2,1)S(1)}, bf16[1,128,1280]{2,1,0:T(8,128)(2,1)S(1)}, u32[]{:S(2)}, u32[]{:S(2)}) collective-permute-start(bf16[1,128,1280]{2,1,0:T(8,128)(2,1)S(1)} %slice.80), channel_id=1, source_target_pairs={{0,96},{32,0},{64,32},{96,64},{1,97},{33,1},{65,33},{97,65},{2,98}... | collective-permute-start | bytes 983048 | tf_op jit(solution)/shard_map/ppermute | solution.py:38
  77.7 14.6 %collective-permute-start.9 = (bf16[1,128,1280]{2,1,0:T(8,128)(2,1)S(1)}, bf16[1,128,1280]{2,1,0:T(8,128)(2,1)S(1)}, u32[]{:S(2)}, u32[]{:S(2)}) collective-permute-start(bf16[1,128,1280]{2,1,0:T(8,128)(2,1)S(1)} %slice.79), channel_id=1, source_target_pairs={{0,32},{32,64},{64,96},{96,0},{1,33},{33,65},{65,97},{97,1},{2,34}... | collective-permute-start | bytes 983048 | tf_op jit(solution)/shard_map/ppermute | solution.py:33
  80.7 11.6 %collective-permute-start.4 = (bf16[1,8,2,16,384]{4,3,2,1,0:T(8,128)(2,1)S(1)}, bf16[1,8,2,16,384]{4,3,2,1,0:T(8,128)(2,1)S(1)}, u32[]{:S(2)}, u32[]{:S(2)}) collective-permute-start(bf16[1,8,2,16,384]{4,3,2,1,0:T(8,128)(2,1)S(1)} %slice.76), channel_id=1, source_target_pairs={{0,4},{4,8},{8,12},{12,0},{1,5},{5,9},{9,13},{13,1},{2,6},{6,10},{... | collective-permute-start | bytes 589832 | tf_op jit(solution)/shard_map/ppermute | solution.py:33
  91.8 5.7 %collective-permute-start.5 = (bf16[1,8,2,16,384]{4,3,2,1,0:T(8,128)(2,1)S(1)}, bf16[1,8,2,16,384]{4,3,2,1,0:T(8,128)(2,1)S(1)}, u32[]{:S(2)}, u32[]{:S(2)}) collective-permute-start(bf16[1,8,2,16,384]{4,3,2,1,0:T(8,128)(2,1)S(1)} %slice.77), channel_id=1, source_target_pairs={{0,12},{4,0},{8,4},{12,8},{1,13},{5,1},{9,5},{13,9},{2,14},{6,2},{... | collective-permute-start | bytes 589832 | tf_op jit(solution)/shard_map/ppermute | solution.py:38
  118.7 35.5 %collective-permute-start.26 = (f32[64,24,256]{2,1,0:T(8,128)}, f32[64,24,256]{2,1,0:T(8,128)}, u32[]{:S(2)}, u32[]{:S(2)}) collective-permute-start(f32[64,24,256]{2,1,0:T(8,128)} %get-tuple-element.16), channel_id=1, source_target_pairs={{0,1},{1,0},{2,3},{3,2},{4,5},{5,4},{6,7},{7,6},{8,9},{9,8},{10,11... | collective-permute-start | bytes 4718600 | tf_op jit(solution)/shard_map/ppermute | solution.py:42
  120.1 27.1 %collective-permute-start.18 = (bf16[8,2,16,2048]{3,2,1,0:T(8,128)(2,1)S(1)}, bf16[8,2,16,2048]{3,2,1,0:T(8,128)(2,1)}, u32[]{:S(2)}, u32[]{:S(2)}) collective-permute-start(bf16[8,2,16,2048]{3,2,1,0:T(8,128)(2,1)S(1)} %bitcast.51), channel_id=1, source_target_pairs={{0,4},{4,8},{8,12},{12,0},{1,5},{5,9},{9,13},{13,1},{2,6},{6,10},{... | collective-permute-start | bytes 3145736 | tf_op jit(solution)/shard_map/ppermute | solution.py:33
  120.4 28.7 %collective-permute-start.17 = (bf16[8,2,16,2048]{3,2,1,0:T(8,128)(2,1)S(1)}, bf16[8,2,16,2048]{3,2,1,0:T(8,128)(2,1)}, u32[]{:S(2)}, u32[]{:S(2)}) collective-permute-start(bf16[8,2,16,2048]{3,2,1,0:T(8,128)(2,1)S(1)} %bitcast.52), channel_id=1, source_target_pairs={{0,12},{4,0},{8,4},{12,8},{1,13},{5,1},{9,5},{13,9},{2,14},{6,2},{... | collective-permute-start | bytes 3145736 | tf_op jit(solution)/shard_map/ppermute | solution.py:38
  123.6 33.7 %all-to-all-start.1 = ((bf16[8,128,512]{2,1,0:T(8,128)(2,1)}), bf16[8,128,512]{2,1,0:T(8,128)(2,1)S(1)}, u32[]{:S(2)}, u32[]{:S(2)}) async-start(bf16[8,128,512]{2,1,0:T(8,128)(2,1)} %get-tuple-element.11), calls=%async_computation.1 | async-start | bytes 2097152 | tf_op jit(solution)/shard_map/all_to_all | solution.py:361
  127.4 27.3 %copy-start.3 = (f32[64,24,256]{2,1,0:T(8,128)S(1)}, f32[64,24,256]{2,1,0:T(8,128)}, u32[]{:S(2)}) copy-start(f32[64,24,256]{2,1,0:T(8,128)} %get-tuple-element.15) | copy-start | bytes 4718596
  127.4 38.3 %collective-permute-start.21 = (bf16[8,2,16,2048]{3,2,1,0:T(8,128)(2,1)S(1)}, bf16[8,2,16,2048]{3,2,1,0:T(8,128)(2,1)}, u32[]{:S(2)}, u32[]{:S(2)}) collective-permute-start(bf16[8,2,16,2048]{3,2,1,0:T(8,128)(2,1)S(1)} %bitcast.53), channel_id=1, source_target_pairs={{0,1},{1,0},{2,3},{3,2},{4,5},{5,4},{6,7},{7,6},{8,9},{9,8},{10,11... | collective-permute-start | bytes 3145736 | tf_op jit(solution)/shard_map/ppermute | solution.py:42
  149.1 15.1 %collective-permute-start.19 = (bf16[4,2,16,2048]{3,2,1,0:T(8,128)(2,1)}, bf16[4,2,16,2048]{3,2,1,0:T(8,128)(2,1)}, u32[]{:S(2)}, u32[]{:S(2)}) collective-permute-start(bf16[4,2,16,2048]{3,2,1,0:T(8,128)(2,1)} %slice.85), channel_id=1, source_target_pairs={{0,4},{4,8},{8,12},{12,0},{1,5},{5,9},{9,13},{13,1},{2,6},{6,10},{... | collective-permute-start | bytes 1572872 | tf_op jit(solution)/shard_map/ppermute | solution.py:33
  151.0 14.8 %collective-permute-start.20 = (bf16[4,2,16,2048]{3,2,1,0:T(8,128)(2,1)}, bf16[4,2,16,2048]{3,2,1,0:T(8,128)(2,1)}, u32[]{:S(2)}, u32[]{:S(2)}) collective-permute-start(bf16[4,2,16,2048]{3,2,1,0:T(8,128)(2,1)} %slice.86), channel_id=1, source_target_pairs={{0,12},{4,0},{8,4},{12,8},{1,13},{5,1},{9,5},{13,9},{2,14},{6,2},{... | collective-permute-start | bytes 1572872 | tf_op jit(solution)/shard_map/ppermute | solution.py:38
  154.2 13.7 %collective-permute-start.22 = (bf16[8,2,16,2048]{3,2,1,0:T(8,128)(2,1)}, bf16[8,2,16,2048]{3,2,1,0:T(8,128)(2,1)}, u32[]{:S(2)}, u32[]{:S(2)}) collective-permute-start(bf16[8,2,16,2048]{3,2,1,0:T(8,128)(2,1)} %collective-permute-done.17.refs_1_), channel_id=1, source_target_pairs={{0,1},{1,0},{2,3},{3,2},{4,5},{5,4},{6,7},{7,6},{8,9},{9,8},{10,11... | collective-permute-start | bytes 3145736 | tf_op jit(solution)/shard_map/ppermute | solution.py:42
  154.2 13.6 %collective-permute-start.23 = (bf16[8,2,16,2048]{3,2,1,0:T(8,128)(2,1)}, bf16[8,2,16,2048]{3,2,1,0:T(8,128)(2,1)}, u32[]{:S(2)}, u32[]{:S(2)}) collective-permute-start(bf16[8,2,16,2048]{3,2,1,0:T(8,128)(2,1)} %collective-permute-done.18.refs_2_), channel_id=1, source_target_pairs={{0,1},{1,0},{2,3},{3,2},{4,5},{5,4},{6,7},{7,6},{8,9},{9,8},{10,11... | collective-permute-start | bytes 3145736 | tf_op jit(solution)/shard_map/ppermute | solution.py:42
  157.2 10.6 %copy-start.1 = (bf16[1,128,2048]{2,1,0:T(8,128)(2,1)S(1)}, bf16[1,128,2048]{2,1,0:T(8,128)(2,1)}, u32[]{:S(2)}) copy-start(bf16[1,128,2048]{2,1,0:T(8,128)(2,1)} %param.10) | copy-start | bytes 1572868
  157.3 23.0 %all-to-all-start.2 = ((bf16[64,24,256]{2,1,0:T(8,128)(2,1)}), bf16[64,24,256]{2,1,0:T(8,128)(2,1)}, u32[]{:S(2)}, u32[]{:S(2)}) async-start(bf16[64,24,256]{2,1,0:T(8,128)(2,1)} %add_convert_fusion), calls=%async_computation.2 | async-start | bytes 1572864 | tf_op jit(solution)/shard_map/all_to_all | solution.py:363
  164.2 2.1 %collective-permute-start.24 = (bf16[4,2,16,2048]{3,2,1,0:T(8,128)(2,1)}, bf16[4,2,16,2048]{3,2,1,0:T(8,128)(2,1)S(1)}, u32[]{:S(2)}, u32[]{:S(2)}) collective-permute-start(bf16[4,2,16,2048]{3,2,1,0:T(8,128)(2,1)} %collective-permute-done.19.refs_3_), channel_id=1, source_target_pairs={{0,1},{1,0},{2,3},{3,2},{4,5},{5,4},{6,7},{7,6},{8,9},{9,8},{10,11... | collective-permute-start | bytes 1572872 | tf_op jit(solution)/shard_map/ppermute | solution.py:42
  165.7 2.1 %collective-permute-start.25 = (bf16[4,2,16,2048]{3,2,1,0:T(8,128)(2,1)}, bf16[4,2,16,2048]{3,2,1,0:T(8,128)(2,1)S(1)}, u32[]{:S(2)}, u32[]{:S(2)}) collective-permute-start(bf16[4,2,16,2048]{3,2,1,0:T(8,128)(2,1)} %collective-permute-done.20.refs_4_), channel_id=1, source_target_pairs={{0,1},{1,0},{2,3},{3,2},{4,5},{5,4},{6,7},{7,6},{8,9},{9,8},{10,11... | collective-permute-start | bytes 1572872 | tf_op jit(solution)/shard_map/ppermute | solution.py:42
  167.9 1.0 copy-start.2

commit v6 on v5

--- a/solution.py
+++ b/solution.py
@@ -15,6 +15,7 @@
 REP = ("z", "yh", "core")
 X, YL, Z, YH, CORE = 4, 2, 4, 2, 2
 ROWS = 256
+WIDE = ((0, None), (1, 0), (1, 1), (3, 0), (3, 1), (2, 0), (2, 1))
 
 
 def tables(length):
@@ -51,6 +52,10 @@
     upper = down(block, axis)
     half = block.shape[0] // 2
     return block, upper, lower, up(lower[:half], axis), down(upper[half:], axis)
+
+
+def after(x, *others):
+    return lax.optimization_barrier((x, *others))[0]
 
 
 def in_order(own, other, index):
@@ -252,14 +257,15 @@
 
 
 def outputs_body(place, back, gates, upstream, *refs):
-    pieces, (mixed_o, gate_o, input_o, w_v, grad_v, sem) = refs[:10], refs[10:]
+    pieces, (mixed_o, gate_o, input_o, w_v, grad_v, sem) = refs[:14], refs[14:]
     groups, block, _ = back.shape
     part = back.shape[2] // 2
     z, core = place[2], place[3]
     copies = []
     for n, c in ((0, core), (1, 1 - core)):
-        for ref, (to, side) in zip(pieces[5 * n : 5 * n + 5], places(z, Z)):
+        for ref, (k, side) in zip(pieces[7 * n : 7 * n + 7], WIDE):
             some = pl.ds(0, groups) if side is None else pl.ds(side * groups // 2, groups // 2)
+            to = lax.rem(z + k, Z)
             copies.append(pltpu.make_async_copy(ref, w_v.at[some, to, :, c], sem.at[len(copies)]))
     for copy in copies:
         copy.start()
@@ -290,12 +296,12 @@
     return pl.pallas_call(
         outputs_body,
         out_shape=[shape((block, channels), BF16)] * 2 + [shape((block, features), BF16)],
-        in_specs=[pl.BlockSpec(memory_space=pltpu.SMEM)] + [near] * 3 + [away] * 10,
+        in_specs=[pl.BlockSpec(memory_space=pltpu.SMEM)] + [near] * 3 + [away] * 14,
         out_specs=[near] * 3,
         scratch_shapes=[
             pltpu.VMEM((groups, Z, YH, CORE, rows, channels), BF16),
             pltpu.VMEM((block, channels), BF16),
-            pltpu.SemaphoreType.DMA((10,)),
+            pltpu.SemaphoreType.DMA((14,)),
         ],
         compiler_params=pltpu.CompilerParams(vmem_limit_bytes=32 * 2**20),
         name="outputs",
@@ -328,6 +334,9 @@
     piece = in_order(piece, swap(piece, "yh"), hi).reshape(YH * rows, channels + groups * half)
     inner = (upstream.astype(F32) * gates.astype(F32)).astype(BF16)
     inner = inner.reshape(block // (YH * rows), YH * rows, groups, part).transpose(2, 1, 0, 3)
+    early = tokens[:, cut:]
+    early_lower, early_upper = up(early, "x"), down(early, "x")
+    late_other = swap(tokens[:, :cut], "yl")
     sent = jnp.concatenate(
         [
             jnp.broadcast_to(piece[:, :channels], (groups, YH * rows, channels)),
@@ -336,7 +345,17 @@
         ],
         axis=2,
     )
+    sent = after(sent, early_lower, early_upper, late_other)
     slices = lax.all_to_all(sent, SEQ, 0, 0, tiled=True)
+    late = in_order(tokens[:, :cut], late_other, yi)
+    late_lower, late_upper = up(late, "x"), down(late, "x")
+    n = block // 2
+    early_far = (up(early_lower[:n], "x"), down(early_upper[n:], "x"))
+    early_own = swap(jnp.stack([early, early_upper, early_lower]), "yl")
+    early = (early, early_upper, early_lower, *early_far)
+    slices = after(slices, late_lower, late_upper, *early_far, early_own)
+    late = (late, late_upper, late_lower, up(late_lower[:1], "x"), down(late_upper[1:], "x"))
+    early_far = swap(jnp.stack(early_far), "yl")
 
     thin = jnp.concatenate(
         [
@@ -346,13 +365,13 @@
         axis=2,
     ).reshape(groups, YH, rows, part + half)
     thin = halves_round(jnp.stack([thin, swap(thin, "core")]), "z")
-    wide = halves_round(slices[:, :, :channels].reshape(groups, YH, rows, channels), "z")
+    wide = slices[:, :, :channels].reshape(groups, YH, rows, channels)
+    n = groups // 2
+    first = (up(wide[:n], "z"), down(wide[n:], "z"))
+    thin = (after(thin[0], *first), *thin[1:])
+    second = (up(wide[n:], "z"), down(wide[:n], "z"))
+    wide = (wide, second[1], first[1], first[0], second[0], up(first[0], "z"), down(first[1], "z"))
     wide = wide + tuple(swap(w, "core") for w in wide)
-
-    early = halves_round(tokens[:, cut:], "x")
-    late = halves_round(in_order(tokens[:, :cut], swap(tokens[:, :cut], "yl"), yi), "x")
-    early_own = swap(jnp.stack(early[:3]), "yl")
-    early_far = swap(jnp.stack(early[3:]), "yl")
 
     pair, mine, other = transforms(
         place, slices, (cosine, sine, cosine_t, sine_t), thin, late, early, early_own, early_far

time: 186 us -> 177 us (0.952); the launches traced: 183 us -> 176 us
  waiting for transfers between devices: 84.4 us -> 68.4 us
  starting transfers between devices: 49.8 us -> 54.8 us
  other arithmetic: 6.75 us -> 9.33 us
  local copies, waits for them, and re-layouts: 12.5 us -> 14.7 us
    ppermute x11 -> x13, waiting for transfers between devices: 37 us -> 12 us  [swap(): return lax.ppermute(x, axis, [(0, 1), (1, 0)])]
    ppermute x8 -> x9, waiting for transfers between devices: 35.7 us -> 42.2 us  [up(): return lax.ppermute(x, axis, [(i, (i + 1) % n) for i in range(n)])]
    ppermute x8 -> x9, starting transfers between devices: 5.71 us -> 9.94 us  [up(): return lax.ppermute(x, axis, [(i, (i + 1) % n) for i in range(n)])]
    slice x1 -> x6, local copies, waits for them, and re-layouts: 1.29 us -> 4.91 us  [the longest x1 2.28 us: local(): first = (up(wide[:n], 'z'), down(wide[n:], 'z'))]
    ppermute x8 -> x9, waiting for transfers between devices: 7.61 us -> 10.6 us  [down(): return lax.ppermute(x, axis, [(i, (i - 1) % n) for i in range(n)])]
    another operation x2, other arithmetic: 0.09 us -> 2.72 us  [the longest x1 1.81 us: local(): early_own = swap(jnp.stack([early, early_upper, early_lower]), 'yl')]
    all_to_all x1, starting transfers between devices: 6.84 us -> 8.87 us  [local(): owned = lax.all_to_all(owned, SEQ + ('z', 'yh'), 0, 0, tiled=True)]
    slice x4 -> x1, local copies, waits for them, and re-layouts: 1.93 us -> 0.02 us  [halves_round(): upper[half:]]
  transfers between devices with their start and end apart: 30 -> 34, of which waited for: 13 -> 13; matrix products, arithmetic and copies ran while one was open for 7% -> 10% of each run, Pallas kernels for 4% -> 4%
where the time goes in v6:
time: 177 us; the launch traced here: 176 us
  waiting for transfers between devices  68.4 us (39%)
  starting transfers between devices  54.8 us (31%)
  Pallas kernels  28 us (16%)
  local copies, waits for them, and re-layouts  14.7 us (8%)
  other arithmetic  9.33 us (5%)
    ppermute x9, waiting for transfers between devices, up(): return lax.ppermute(x, axis, [(i, (i + 1) % n) for i in range(n)])  42.2 us
    pallas_call x1, Pallas kernels, transforms(): pl.pallas_call(transforms_body, out_shape=[shape((X * YL, block, 2 * part...  21.3 us
    ppermute x9, starting transfers between devices, down(): return lax.ppermute(x, axis, [(i, (i - 1) % n) for i in range(n)])  20.5 us
    ppermute x13, waiting for transfers between devices, swap(): return lax.ppermute(x, axis, [(0, 1), (1, 0)])  12 us
    ppermute x9, waiting for transfers between devices, down(): return lax.ppermute(x, axis, [(i, (i - 1) % n) for i in range(n)])  10.6 us
    ppermute x9, starting transfers between devices, up(): return lax.ppermute(x, axis, [(i, (i + 1) % n) for i in range(n)])  9.94 us
    all_to_all x1, starting transfers between devices, local(): owned = lax.all_to_all(owned, SEQ + ('z', 'yh'), 0, 0, tiled=True)  8.87 us
    ppermute x13, starting transfers between devices, swap(): return lax.ppermute(x, axis, [(0, 1), (1, 0)])  7.65 us
  transfers between devices with their start and end apart: 34, of which 13 were waited for; matrix products, arithmetic and copies ran while one was open for 10% of the time, Pallas kernels for 4%

profile of v6, /device:TPU:0, one launch (start us, length us, event | category | flops | bytes accessed | tf_op | source)
XLA Modules:
  0.0 176.2 jit_solution(17911104515810010447)
XLA Ops:
  0.7 1.7 slice_bitcast_fusion.2
  2.4 1.6 collective-permute-start.1
  4.0 1.7 collective-permute-start.2
  5.7 0.8 constant_dynamic-update-slice_fusion
  6.6 0.2 dynamic-slice_reduce_fusion
  6.8 3.4 %collective-permute-start = (bf16[16,3072]{1,0:T(8,128)(2,1)S(1)}, bf16[16,3072]{1,0:T(8,128)(2,1)S(1)}, u32[]{:S(2)}, u32[]{:S(2)}) collective-permute-start(bf16[16,3072]{1,0:T(8,128)(2,1)S(1)} %bitcast_dynamic-update-slice_fusion), channel_id=1, source_target_pairs={{0,2},{2,0},{1,3},{3,1},{4,6},{6,4},{5,7},{7,5},{8,10},{10,8},{9,1... | collective-permute-start | bytes 294920 | tf_op jit(solution)/shard_map/ppermute | solution.py:43
  10.1 1.7 slice_bitcast_fusion.3
  11.9 0.7 collective-permute-start.3
  12.5 0.1 multiply_convert_fusion
  12.8 0.4 copy.29
  13.2 0.4 reshape.52
  13.7 0.1 broadcast_in_dim.12
  13.8 1.4 pad_maximum_fusion
  15.2 5.6 %collective-permute-done.3 = bf16[128,1280]{1,0:T(8,128)(2,1)} collective-permute-done((bf16[128,1280]{1,0:T(8,128)(2,1)}, bf16[128,1280]{1,0:T(8,128)(2,1)}, u32[]{:S(2)}, u32[]{:S(2)}) %collective-permute-start.3) | collective-permute-done | bytes 327712 | tf_op jit(solution)/shard_map/ppermute | solution.py:43
  20.8 4.3 %all-to-all-start = ((bf16[8,32,3200]{2,1,0:T(8,128)(2,1)}), bf16[8,32,3200]{2,1,0:T(8,128)(2,1)}, u32[]{:S(2)}, u32[]{:S(2)}) async-start(bf16[8,32,3200]{2,1,0:T(8,128)(2,1)} %pad_maximum_fusion), calls=%async_computation | async-start | bytes 3276800 | tf_op jit(solution)/shard_map/all_to_all | solution.py:349
  25.1 1.2 maximum_select_fusion.refs_10_
  26.3 2.0 %collective-permute-start.4 = (bf16[2,128,1280]{2,1,0:T(8,128)(2,1)S(1)}, bf16[2,128,1280]{2,1,0:T(8,128)(2,1)S(1)}, u32[]{:S(2)}, u32[]{:S(2)}) collective-permute-start(bf16[2,128,1280]{2,1,0:T(8,128)(2,1)S(1)} %maximum_select_fusion.refs_10_), channel_id=1, source_target_pairs={{0,32},{32,64},{64,96},{96,0},{1,33},{33,65},{65,97},{97,1},{2,34}... | collective-permute-start | bytes 1966088 | tf_op jit(solution)/shard_map/ppermute | solution.py:34
  28.2 1.3 collective-permute-start.5
  29.6 1.8 %pad_maximum_fusion.1 = bf16[3,128,768]{2,1,0:T(8,128)(2,1)} fusion(bf16[1,128,768]{2,1,0:T(8,128)(2,1)S(1)} %bitcast.57, bf16[1,128,768]{2,1,0:T(8,128)(2,1)S(1)} %bitcast.58, bf16[1,128,768]{2,1,0:T(8,128)(2,1)} %get-tuple-element.25), kind=kLoop, calls=%fused_computation.5 | loop fusion | flops 589824 | bytes 1179648 | tf_op jit(solution)/shard_map/stack | solution.py:354
  31.4 1.9 %collective-permute-start.8 = (bf16[3,128,768]{2,1,0:T(8,128)(2,1)}, bf16[3,128,768]{2,1,0:T(8,128)(2,1)}, u32[]{:S(2)}, u32[]{:S(2)}) collective-permute-start(bf16[3,128,768]{2,1,0:T(8,128)(2,1)} %pad_maximum_fusion.1), channel_id=1, source_target_pairs={{0,16},{16,0},{1,17},{17,1},{2,18},{18,2},{3,19},{19,3},{4,20},{20... | collective-permute-start | bytes 1769480 | tf_op jit(solution)/shard_map/ppermute | solution.py:43
  33.3 0.6 slice.89
  33.9 0.3 collective-permute-start.6
  34.2 0.6 slice.90
  34.8 3.0 %collective-permute-start.7 = (bf16[64,768]{1,0:T(8,128)(2,1)}, bf16[64,768]{1,0:T(8,128)(2,1)}, u32[]{:S(2)}, u32[]{:S(2)}) collective-permute-start(bf16[64,768]{1,0:T(8,128)(2,1)} %slice.90), channel_id=1, source_target_pairs={{0,96},{32,0},{64,32},{96,64},{1,97},{33,1},{65,33},{97,65},{2,98}... | collective-permute-start | bytes 294920 | tf_op jit(solution)/shard_map/ppermute | solution.py:39
  37.8 23.0 %collective-permute-done.6.refs_18_ = bf16[64,768]{1,0:T(8,128)(2,1)S(1)} collective-permute-done((bf16[64,768]{1,0:T(8,128)(2,1)}, bf16[64,768]{1,0:T(8,128)(2,1)S(1)}, u32[]{:S(2)}, u32[]{:S(2)}) %collective-permute-start.6) | collective-permute-done | bytes 98336 | tf_op jit(solution)/shard_map/ppermute | solution.py:34
  60.8 0.8 slice.71
  61.7 0.9 constant_dynamic-slice_fusion
  62.7 2.3 %fusion = (bf16[4,32,2048]{2,1,0:T(8,128)(2,1)}, bf16[4,32,2048]{2,1,0:T(8,128)(2,1)}) fusion(bf16[8,32,3200]{2,1,0:T(8,128)(2,1)} %all-to-all-done.refs_0_), kind=kLoop, calls=%fused_computation.22 | loop fusion | bytes 2097152 | tf_op jit(solution)/shard_map/slice | solution.py:370
  65.0 1.9 %collective-permute-start.10 = (bf16[4,2,16,2048]{3,2,1,0:T(8,128)(2,1)}, bf16[4,2,16,2048]{3,2,1,0:T(8,128)(2,1)}, u32[]{:S(2)}, u32[]{:S(2)}) collective-permute-start(bf16[4,2,16,2048]{3,2,1,0:T(8,128)(2,1)} %bitcast.18), channel_id=1, source_target_pairs={{0,4},{4,8},{8,12},{12,0},{1,5},{5,9},{9,13},{13,1},{2,6},{6,10},{... | collective-permute-start | bytes 1572872 | tf_op jit(solution)/shard_map/ppermute | solution.py:34
  67.0 2.0 %collective-permute-start.13 = (bf16[2,8,2,16,384]{4,3,2,1,0:T(8,128)(2,1)S(1)}, bf16[2,8,2,16,384]{4,3,2,1,0:T(8,128)(2,1)S(1)}, u32[]{:S(2)}, u32[]{:S(2)}) collective-permute-start(bf16[2,8,2,16,384]{4,3,2,1,0:T(8,128)(2,1)S(1)} %pad_maximum_fusion.2.refs_5_), channel_id=1, source_target_pairs={{0,4},{4,8},{8,12},{12,0},{1,5},{5,9},{9,13},{13,1},{2,6},{6,10},{... | collective-permute-start | bytes 1179656 | tf_op jit(solution)/shard_map/ppermute | solution.py:34
  69.0 1.3 collective-permute-start.11
  70.3 1.0 collective-permute-start.12
  71.3 1.7 collective-permute-start.16
  73.0 17.2 %collective-permute-done.13.refs_7_ = bf16[2,8,2,16,384]{4,3,2,1,0:T(8,128)(2,1)S(1)} collective-permute-done((bf16[2,8,2,16,384]{4,3,2,1,0:T(8,128)(2,1)S(1)}, bf16[2,8,2,16,384]{4,3,2,1,0:T(8,128)(2,1)S(1)}, u32[]{:S(2)}, u32[]{:S(2)}) %collective-permute-start.13) | collective-permute-done | bytes 393248 | tf_op jit(solution)/shard_map/ppermute | solution.py:34
  90.3 2.7 %collective-permute-start.17 = (bf16[1,128,1280]{2,1,0:T(8,128)(2,1)S(1)}, bf16[1,128,1280]{2,1,0:T(8,128)(2,1)S(1)}, u32[]{:S(2)}, u32[]{:S(2)}) collective-permute-start(bf16[1,128,1280]{2,1,0:T(8,128)(2,1)S(1)} %slice.94), channel_id=1, source_target_pairs={{0,96},{32,0},{64,32},{96,64},{1,97},{33,1},{65,33},{97,65},{2,98}... | collective-permute-start | bytes 983048 | tf_op jit(solution)/shard_map/ppermute | solution.py:39
  92.9 0.9 pad_maximum_fusion.4
  94.0 0.5 collective-permute-start.14
  94.5 2.8 %collective-permute-start.15 = (bf16[1,8,2,16,384]{4,3,2,1,0:T(8,128)(2,1)S(1)}, bf16[1,8,2,16,384]{4,3,2,1,0:T(8,128)(2,1)S(1)}, u32[]{:S(2)}, u32[]{:S(2)}) collective-permute-start(bf16[1,8,2,16,384]{4,3,2,1,0:T(8,128)(2,1)S(1)} %slice.92), channel_id=1, source_target_pairs={{0,12},{4,0},{8,4},{12,8},{1,13},{5,1},{9,5},{13,9},{2,14},{6,2},{... | collective-permute-start | bytes 589832 | tf_op jit(solution)/shard_map/ppermute | solution.py:39
  97.4 3.0 %collective-permute-done.18.refs_21_ = bf16[2,64,768]{2,1,0:T(8,128)(2,1)S(1)} collective-permute-done((bf16[2,64,768]{2,1,0:T(8,128)(2,1)S(1)}, bf16[2,64,768]{2,1,0:T(8,128)(2,1)S(1)}, u32[]{:S(2)}, u32[]{:S(2)}) %collective-permute-start.18) | collective-permute-done | bytes 196640 | tf_op jit(solution)/shard_map/ppermute | solution.py:43
  100.4 1.3 collective-permute-done.14.refs_8_
  101.8 21.3 %transforms.1 = (bf16[8,128,512]{2,1,0:T(8,128)(2,1)}, f32[64,24,256]{2,1,0:T(8,128)}, f32[64,24,256]{2,1,0:T(8,128)}) custom-call(s32[4]{0:T(128)S(1)} %pad_add_fusion.place, bf16[8,32,3200]{2,1,0:T(8,128)(2,1)} %all-to-all-done.refs_0_, bf16[1024,1024]{1,0:T(8,128)(2,1)} %constant.53.refs_1_, bf16[1024,1024]{1,0:T(8,128)(2,1)} %constant.54.refs_2_, ...), custom_call_target="tpu_custom_call" | custom-call | tf_op jit(solution)/shard_map/transforms/pallas_call | solution.py:239
  123.1 3.6 %all-to-all-start.1 = ((bf16[8,128,512]{2,1,0:T(8,128)(2,1)}), bf16[8,128,512]{2,1,0:T(8,128)(2,1)S(1)}, u32[]{:S(2)}, u32[]{:S(2)}) async-start(bf16[8,128,512]{2,1,0:T(8,128)(2,1)} %get-tuple-element.17), calls=%async_computation.1 | async-start | bytes 2097152 | tf_op jit(solution)/shard_map/all_to_all | solution.py:380
  126.7 3.0 %collective-permute-start.19 = (bf16[4,2,16,2048]{3,2,1,0:T(8,128)(2,1)}, bf16[4,2,16,2048]{3,2,1,0:T(8,128)(2,1)}, u32[]{:S(2)}, u32[]{:S(2)}) collective-permute-start(bf16[4,2,16,2048]{3,2,1,0:T(8,128)(2,1)} %bitcast.18), channel_id=1, source_target_pairs={{0,12},{4,0},{8,4},{12,8},{1,13},{5,1},{9,5},{13,9},{2,14},{6,2},{... | collective-permute-start | bytes 1572872 | tf_op jit(solution)/shard_map/ppermute | solution.py:39
  129.7 1.3 slice.80
  131.0 0.3 collective-permute-start.23
  131.3 10.6 %collective-permute-done.19.refs_1_ = bf16[4,2,16,2048]{3,2,1,0:T(8,128)(2,1)} collective-permute-done((bf16[4,2,16,2048]{3,2,1,0:T(8,128)(2,1)}, bf16[4,2,16,2048]{3,2,1,0:T(8,128)(2,1)}, u32[]{:S(2)}, u32[]{:S(2)}) %collective-permute-start.19) | collective-permute-done | bytes 524320 | tf_op jit(solution)/shard_map/ppermute | solution.py:39
  141.9 3.7 %collective-permute-start.22 = (bf16[4,2,16,2048]{3,2,1,0:T(8,128)(2,1)}, bf16[4,2,16,2048]{3,2,1,0:T(8,128)(2,1)}, u32[]{:S(2)}, u32[]{:S(2)}) collective-permute-start(bf16[4,2,16,2048]{3,2,1,0:T(8,128)(2,1)} %collective-permute-done.11.refs_2_), channel_id=1, source_target_pairs={{0,12},{4,0},{8,4},{12,8},{1,13},{5,1},{9,5},{13,9},{2,14},{6,2},{... | collective-permute-start | bytes 1572872 | tf_op jit(solution)/shard_map/ppermute | solution.py:39
  145.6 2.5 %add_convert_fusion = bf16[64,24,256]{2,1,0:T(8,128)(2,1)} fusion(f32[64,24,256]{2,1,0:T(8,128)S(1)} %copy-done.6, f32[64,24,256]{2,1,0:T(8,128)} %collective-permute-done.30), kind=kLoop, calls=%fused_computation.2 | loop fusion | flops 786432 | bytes 3932160 | tf_op jit(solution)/shard_map/convert_element_type | solution.py:381
  148.1 8.9 %all-to-all-start.2 = ((bf16[64,24,256]{2,1,0:T(8,128)(2,1)}), bf16[64,24,256]{2,1,0:T(8,128)(2,1)}, u32[]{:S(2)}, u32[]{:S(2)}) async-start(bf16[64,24,256]{2,1,0:T(8,128)(2,1)} %add_convert_fusion), calls=%async_computation.2 | async-start | bytes 1572864 | tf_op jit(solution)/shard_map/all_to_all | solution.py:382
  157.0 0.3 collective-permute-start.25
  157.3 0.3 collective-permute-start.26
  157.6 0.6 collective-permute-done.21.refs_5_
  158.2 0.5 collective-permute-start.28
  158.8 0.4 collective-permute-done.25.refs_9_
  159.2 0.7 collective-permute-done.26.refs_10_
  160.0 0.7 collective-permute-done.27.refs_11_
  160.7 0.7 collective-permute-done.28.refs_12_
  161.5 0.7 collective-permute-done.29.refs_13_
  162.2 1.0 copy-done.3
  163.3 6.7 %outputs.1 = (bf16[128,2048]{1,0:T(8,128)(2,1)}, bf16[128,2048]{1,0:T(8,128)(2,1)}, bf16[128,2048]{1,0:T(8,128)(2,1)}) custom-call(s32[4]{0:T(128)S(1)} %pad_add_fusion.place, bf16[8,128,512]{2,1,0:T(8,128)(2,1)S(1)} %all-to-all-done.1.back, bf16[128,2048]{1,0:T(8,128)(2,1)S(1)} %bitcast.55, bf16[128,2048]{1,0:T(8,128)(2,1)S(1)} %bitcast.56, ...), custom_call_target="tpu_custom_call" | custom-call | tf_op jit(solution)/shard_map/outputs/pallas_call | solution.py:296
  170.0 3.6 %all-to-all-done.2 = bf16[64,24,256]{2,1,0:T(8,128)(2,1)} async-done(((bf16[64,24,256]{2,1,0:T(8,128)(2,1)}), bf16[64,24,256]{2,1,0:T(8,128)(2,1)}, u32[]{:S(2)}, u32[]{:S(2)}) %all-to-all-start.2) | async-done | bytes 786464 | tf_op jit(solution)/shard_map/all_to_all | solution.py:382
  173.6 1.3 convert_reduce_fusion
  174.9 0.6 slice.96
  175.5 0.7 copy.23
  (57 shorter events, 0.9 us)
Async XLA Ops:
  0.6 5.0 %copy-start = (bf16[128,2048]{1,0:T(8,128)(2,1)S(1)}, bf16[128,2048]{1,0:T(8,128)(2,1)}, u32[]{:S(2)}) copy-start(bf16[128,2048]{1,0:T(8,128)(2,1)} %param.12) | copy-start | bytes 1572868
  0.6 11.9 %copy-start.1 = (bf16[1,128,2048]{2,1,0:T(8,128)(2,1)S(1)}, bf16[1,128,2048]{2,1,0:T(8,128)(2,1)}, u32[]{:S(2)}) copy-start(bf16[1,128,2048]{2,1,0:T(8,128)(2,1)} %param.10) | copy-start | bytes 1572868
  0.7 11.9 %copy-start.2 = (bf16[1,128,2048]{2,1,0:T(8,128)(2,1)S(1)}, bf16[1,128,2048]{2,1,0:T(8,128)(2,1)}, u32[]{:S(2)}) copy-start(bf16[1,128,2048]{2,1,0:T(8,128)(2,1)} %param.13) | copy-start | bytes 1572868
  2.4 10.4 %copy-start.4 = (bf16[128,768]{1,0:T(8,128)(2,1)}, bf16[128,768]{1,0:T(8,128)(2,1)S(1)}, u32[]{:S(2)}) copy-start(bf16[128,768]{1,0:T(8,128)(2,1)S(1)} %get-tuple-element.26.refs_15_) | copy-start | bytes 589828
  2.4 12.7 %collective-permute-start.1 = (bf16[128,768]{1,0:T(8,128)(2,1)S(1)}, bf16[128,768]{1,0:T(8,128)(2,1)S(1)}, u32[]{:S(2)}, u32[]{:S(2)}) collective-permute-start(bf16[128,768]{1,0:T(8,128)(2,1)S(1)} %get-tuple-element.26.refs_15_), channel_id=1, source_target_pairs={{0,32},{32,64},{64,96},{96,0},{1,33},{33,65},{65,97},{97,1},{2,34}... | collective-permute-start | bytes 589832 | tf_op jit(solution)/shard_map/ppermute | solution.py:34
  4.0 11.2 %collective-permute-start.2 = (bf16[128,768]{1,0:T(8,128)(2,1)S(1)}, bf16[128,768]{1,0:T(8,128)(2,1)S(1)}, u32[]{:S(2)}, u32[]{:S(2)}) collective-permute-start(bf16[128,768]{1,0:T(8,128)(2,1)S(1)} %get-tuple-element.26.refs_15_), channel_id=1, source_target_pairs={{0,96},{32,0},{64,32},{96,64},{1,97},{33,1},{65,33},{97,65},{2,98}... | collective-permute-start | bytes 589832 | tf_op jit(solution)/shard_map/ppermute | solution.py:39
  6.8 6.8 %collective-permute-start = (bf16[16,3072]{1,0:T(8,128)(2,1)S(1)}, bf16[16,3072]{1,0:T(8,128)(2,1)S(1)}, u32[]{:S(2)}, u32[]{:S(2)}) collective-permute-start(bf16[16,3072]{1,0:T(8,128)(2,1)S(1)} %bitcast_dynamic-update-slice_fusion), channel_id=1, source_target_pairs={{0,2},{2,0},{1,3},{3,1},{4,6},{6,4},{5,7},{7,5},{8,10},{10,8},{9,1... | collective-permute-start | bytes 294920 | tf_op jit(solution)/shard_map/ppermute | solution.py:43
  11.9 8.9 %collective-permute-start.3 = (bf16[128,1280]{1,0:T(8,128)(2,1)}, bf16[128,1280]{1,0:T(8,128)(2,1)}, u32[]{:S(2)}, u32[]{:S(2)}) collective-permute-start(bf16[128,1280]{1,0:T(8,128)(2,1)} %get-tuple-element.28), channel_id=1, source_target_pairs={{0,16},{16,0},{1,17},{17,1},{2,18},{18,2},{3,19},{19,3},{4,20},{20... | collective-permute-start | bytes 983048 | tf_op jit(solution)/shard_map/ppermute | solution.py:43
  20.8 40.0 %all-to-all-start = ((bf16[8,32,3200]{2,1,0:T(8,128)(2,1)}), bf16[8,32,3200]{2,1,0:T(8,128)(2,1)}, u32[]{:S(2)}, u32[]{:S(2)}) async-start(bf16[8,32,3200]{2,1,0:T(8,128)(2,1)} %pad_maximum_fusion), calls=%async_computation | async-start | bytes 3276800 | tf_op jit(solution)/shard_map/all_to_all | solution.py:349
  26.3 34.5 %collective-permute-start.4 = (bf16[2,128,1280]{2,1,0:T(8,128)(2,1)S(1)}, bf16[2,128,1280]{2,1,0:T(8,128)(2,1)S(1)}, u32[]{:S(2)}, u32[]{:S(2)}) collective-permute-start(bf16[2,128,1280]{2,1,0:T(8,128)(2,1)S(1)} %maximum_select_fusion.refs_10_), channel_id=1, source_target_pairs={{0,32},{32,64},{64,96},{96,0},{1,33},{33,65},{65,97},{97,1},{2,34}... | collective-permute-start | bytes 1966088 | tf_op jit(solution)/shard_map/ppermute | solution.py:34
  28.2 32.6 %collective-permute-start.5 = (bf16[2,128,1280]{2,1,0:T(8,128)(2,1)S(1)}, bf16[2,128,1280]{2,1,0:T(8,128)(2,1)S(1)}, u32[]{:S(2)}, u32[]{:S(2)}) collective-permute-start(bf16[2,128,1280]{2,1,0:T(8,128)(2,1)S(1)} %maximum_select_fusion.refs_10_), channel_id=1, source_target_pairs={{0,96},{32,0},{64,32},{96,64},{1,97},{33,1},{65,33},{97,65},{2,98}... | collective-permute-start | bytes 1966088 | tf_op jit(solution)/shard_map/ppermute | solution.py:39
  31.4 29.4 %collective-permute-start.8 = (bf16[3,128,768]{2,1,0:T(8,128)(2,1)}, bf16[3,128,768]{2,1,0:T(8,128)(2,1)}, u32[]{:S(2)}, u32[]{:S(2)}) collective-permute-start(bf16[3,128,768]{2,1,0:T(8,128)(2,1)} %pad_maximum_fusion.1), channel_id=1, source_target_pairs={{0,16},{16,0},{1,17},{17,1},{2,18},{18,2},{3,19},{19,3},{4,20},{20... | collective-permute-start | bytes 1769480 | tf_op jit(solution)/shard_map/ppermute | solution.py:43
  33.9 26.9 %collective-permute-start.6 = (bf16[64,768]{1,0:T(8,128)(2,1)}, bf16[64,768]{1,0:T(8,128)(2,1)S(1)}, u32[]{:S(2)}, u32[]{:S(2)}) collective-permute-start(bf16[64,768]{1,0:T(8,128)(2,1)} %slice.89), channel_id=1, source_target_pairs={{0,32},{32,64},{64,96},{96,0},{1,33},{33,65},{65,97},{97,1},{2,34}... | collective-permute-start | bytes 294920 | tf_op jit(solution)/shard_map/ppermute | solution.py:34
  34.8 26.0 %collective-permute-start.7 = (bf16[64,768]{1,0:T(8,128)(2,1)}, bf16[64,768]{1,0:T(8,128)(2,1)}, u32[]{:S(2)}, u32[]{:S(2)}) collective-permute-start(bf16[64,768]{1,0:T(8,128)(2,1)} %slice.90), channel_id=1, source_target_pairs={{0,96},{32,0},{64,32},{96,64},{1,97},{33,1},{65,33},{97,65},{2,98}... | collective-permute-start | bytes 294920 | tf_op jit(solution)/shard_map/ppermute | solution.py:39
  62.6 4.3 %collective-permute-start.9 = (bf16[8,2,16,384]{3,2,1,0:T(8,128)(2,1)S(1)}, bf16[8,2,16,384]{3,2,1,0:T(8,128)(2,1)S(1)}, u32[]{:S(2)}, u32[]{:S(2)}) collective-permute-start(bf16[8,2,16,384]{3,2,1,0:T(8,128)(2,1)S(1)} %bitcast.65), channel_id=1, source_target_pairs={{0,1},{1,0},{2,3},{3,2},{4,5},{5,4},{6,7},{7,6},{8,9},{9,8},{10,11... | collective-permute-start | bytes 589832 | tf_op jit(solution)/shard_map/ppermute | solution.py:43
  65.0 29.0 %collective-permute-start.10 = (bf16[4,2,16,2048]{3,2,1,0:T(8,128)(2,1)}, bf16[4,2,16,2048]{3,2,1,0:T(8,128)(2,1)}, u32[]{:S(2)}, u32[]{:S(2)}) collective-permute-start(bf16[4,2,16,2048]{3,2,1,0:T(8,128)(2,1)} %bitcast.18), channel_id=1, source_target_pairs={{0,4},{4,8},{8,12},{12,0},{1,5},{5,9},{9,13},{13,1},{2,6},{6,10},{... | collective-permute-start | bytes 1572872 | tf_op jit(solution)/shard_map/ppermute | solution.py:34
  66.9 34.8 %copy-start.5 = (bf16[128,768]{1,0:T(8,128)(2,1)S(1)}, bf16[128,768]{1,0:T(8,128)(2,1)}, u32[]{:S(2)}) copy-start(bf16[128,768]{1,0:T(8,128)(2,1)} %copy-done.4) | copy-start | bytes 589828
  67.0 23.3 %collective-permute-start.13 = (bf16[2,8,2,16,384]{4,3,2,1,0:T(8,128)(2,1)S(1)}, bf16[2,8,2,16,384]{4,3,2,1,0:T(8,128)(2,1)S(1)}, u32[]{:S(2)}, u32[]{:S(2)}) collective-permute-start(bf16[2,8,2,16,384]{4,3,2,1,0:T(8,128)(2,1)S(1)} %pad_maximum_fusion.2.refs_5_), channel_id=1, source_target_pairs={{0,4},{4,8},{8,12},{12,0},{1,5},{5,9},{9,13},{13,1},{2,6},{6,10},{... | collective-permute-start | bytes 1179656 | tf_op jit(solution)/shard_map/ppermute | solution.py:34
  69.0 25.6 %collective-permute-start.11 = (bf16[4,2,16,2048]{3,2,1,0:T(8,128)(2,1)}, bf16[4,2,16,2048]{3,2,1,0:T(8,128)(2,1)}, u32[]{:S(2)}, u32[]{:S(2)}) collective-permute-start(bf16[4,2,16,2048]{3,2,1,0:T(8,128)(2,1)} %bitcast.19), channel_id=1, source_target_pairs={{0,12},{4,0},{8,4},{12,8},{1,13},{5,1},{9,5},{13,9},{2,14},{6,2},{... | collective-permute-start | bytes 1572872 | tf_op jit(solution)/shard_map/ppermute | solution.py:39
  70.3 23.6 %collective-permute-start.12 = (bf16[2,8,2,16,384]{4,3,2,1,0:T(8,128)(2,1)S(1)}, bf16[2,8,2,16,384]{4,3,2,1,0:T(8,128)(2,1)S(1)}, u32[]{:S(2)}, u32[]{:S(2)}) collective-permute-start(bf16[2,8,2,16,384]{4,3,2,1,0:T(8,128)(2,1)S(1)} %pad_maximum_fusion.2.refs_5_), channel_id=1, source_target_pairs={{0,12},{4,0},{8,4},{12,8},{1,13},{5,1},{9,5},{13,9},{2,14},{6,2},{... | collective-permute-start | bytes 1179656 | tf_op jit(solution)/shard_map/ppermute | solution.py:39
  71.3 29.1 %collective-permute-start.16 = (bf16[1,128,1280]{2,1,0:T(8,128)(2,1)S(1)}, bf16[1,128,1280]{2,1,0:T(8,128)(2,1)S(1)}, u32[]{:S(2)}, u32[]{:S(2)}) collective-permute-start(bf16[1,128,1280]{2,1,0:T(8,128)(2,1)S(1)} %slice.93), channel_id=1, source_target_pairs={{0,32},{32,64},{64,96},{96,0},{1,33},{33,65},{65,97},{97,1},{2,34}... | collective-permute-start | bytes 983048 | tf_op jit(solution)/shard_map/ppermute | solution.py:34
  90.3 10.2 %collective-permute-start.17 = (bf16[1,128,1280]{2,1,0:T(8,128)(2,1)S(1)}, bf16[1,128,1280]{2,1,0:T(8,128)(2,1)S(1)}, u32[]{:S(2)}, u32[]{:S(2)}) collective-permute-start(bf16[1,128,1280]{2,1,0:T(8,128)(2,1)S(1)} %slice.94), channel_id=1, source_target_pairs={{0,96},{32,0},{64,32},{96,64},{1,97},{33,1},{65,33},{97,65},{2,98}... | collective-permute-start | bytes 983048 | tf_op jit(solution)/shard_map/ppermute | solution.py:39
  93.9 6.5 %collective-permute-start.18 = (bf16[2,64,768]{2,1,0:T(8,128)(2,1)S(1)}, bf16[2,64,768]{2,1,0:T(8,128)(2,1)S(1)}, u32[]{:S(2)}, u32[]{:S(2)}) collective-permute-start(bf16[2,64,768]{2,1,0:T(8,128)(2,1)S(1)} %pad_maximum_fusion.4), channel_id=1, source_target_pairs={{0,16},{16,0},{1,17},{17,1},{2,18},{18,2},{3,19},{19,3},{4,20},{20... | collective-permute-start | bytes 589832 | tf_op jit(solution)/shard_map/ppermute | solution.py:43
  94.0 7.7 %collective-permute-start.14 = (bf16[1,8,2,16,384]{4,3,2,1,0:T(8,128)(2,1)S(1)}, bf16[1,8,2,16,384]{4,3,2,1,0:T(8,128)(2,1)S(1)}, u32[]{:S(2)}, u32[]{:S(2)}) collective-permute-start(bf16[1,8,2,16,384]{4,3,2,1,0:T(8,128)(2,1)S(1)} %slice.91), channel_id=1, source_target_pairs={{0,4},{4,8},{8,12},{12,0},{1,5},{5,9},{9,13},{13,1},{2,6},{6,10},{... | collective-permute-start | bytes 589832 | tf_op jit(solution)/shard_map/ppermute | solution.py:34
  94.5 7.2 %collective-permute-start.15 = (bf16[1,8,2,16,384]{4,3,2,1,0:T(8,128)(2,1)S(1)}, bf16[1,8,2,16,384]{4,3,2,1,0:T(8,128)(2,1)S(1)}, u32[]{:S(2)}, u32[]{:S(2)}) collective-permute-start(bf16[1,8,2,16,384]{4,3,2,1,0:T(8,128)(2,1)S(1)} %slice.92), channel_id=1, source_target_pairs={{0,12},{4,0},{8,4},{12,8},{1,13},{5,1},{9,5},{13,9},{2,14},{6,2},{... | collective-permute-start | bytes 589832 | tf_op jit(solution)/shard_map/ppermute | solution.py:39
  123.0 22.5 %collective-permute-start.30 = (f32[64,24,256]{2,1,0:T(8,128)}, f32[64,24,256]{2,1,0:T(8,128)}, u32[]{:S(2)}, u32[]{:S(2)}) collective-permute-start(f32[64,24,256]{2,1,0:T(8,128)} %get-tuple-element.22), channel_id=1, source_target_pairs={{0,1},{1,0},{2,3},{3,2},{4,5},{5,4},{6,7},{7,6},{8,9},{9,8},{10,11... | collective-permute-start | bytes 4718600 | tf_op jit(solution)/shard_map/ppermute | solution.py:43
  123.1 25.0 %all-to-all-start.1 = ((bf16[8,128,512]{2,1,0:T(8,128)(2,1)}), bf16[8,128,512]{2,1,0:T(8,128)(2,1)S(1)}, u32[]{:S(2)}, u32[]{:S(2)}) async-start(bf16[8,128,512]{2,1,0:T(8,128)(2,1)} %get-tuple-element.17), calls=%async_computation.1 | async-start | bytes 2097152 | tf_op jit(solution)/shard_map/all_to_all | solution.py:380
  126.7 18.9 %copy-start.6 = (f32[64,24,256]{2,1,0:T(8,128)S(1)}, f32[64,24,256]{2,1,0:T(8,128)}, u32[]{:S(2)}) copy-start(f32[64,24,256]{2,1,0:T(8,128)} %get-tuple-element.21) | copy-start | bytes 4718596
  126.7 15.2 %collective-permute-start.19 = (bf16[4,2,16,2048]{3,2,1,0:T(8,128)(2,1)}, bf16[4,2,16,2048]{3,2,1,0:T(8,128)(2,1)}, u32[]{:S(2)}, u32[]{:S(2)}) collective-permute-start(bf16[4,2,16,2048]{3,2,1,0:T(8,128)(2,1)} %bitcast.18), channel_id=1, source_target_pairs={{0,12},{4,0},{8,4},{12,8},{1,13},{5,1},{9,5},{13,9},{2,14},{6,2},{... | collective-permute-start | bytes 1572872 | tf_op jit(solution)/shard_map/ppermute | solution.py:39
  131.0 26.3 %collective-permute-start.23 = (bf16[8,2,16,2048]{3,2,1,0:T(8,128)(2,1)S(1)}, bf16[8,2,16,2048]{3,2,1,0:T(8,128)(2,1)}, u32[]{:S(2)}, u32[]{:S(2)}) collective-permute-start(bf16[8,2,16,2048]{3,2,1,0:T(8,128)(2,1)S(1)} %bitcast.53), channel_id=1, source_target_pairs={{0,1},{1,0},{2,3},{3,2},{4,5},{5,4},{6,7},{7,6},{8,9},{9,8},{10,11... | collective-permute-start | bytes 3145736 | tf_op jit(solution)/shard_map/ppermute | solution.py:43
  131.3 25.7 %collective-permute-start.20 = (bf16[4,2,16,2048]{3,2,1,0:T(8,128)(2,1)}, bf16[4,2,16,2048]{3,2,1,0:T(8,128)(2,1)}, u32[]{:S(2)}, u32[]{:S(2)}) collective-permute-start(bf16[4,2,16,2048]{3,2,1,0:T(8,128)(2,1)} %bitcast.19), channel_id=1, source_target_pairs={{0,4},{4,8},{8,12},{12,0},{1,5},{5,9},{9,13},{13,1},{2,6},{6,10},{... | collective-permute-start | bytes 1572872 | tf_op jit(solution)/shard_map/ppermute | solution.py:34
  131.3 26.9 %collective-permute-start.21 = (bf16[4,2,16,2048]{3,2,1,0:T(8,128)(2,1)}, bf16[4,2,16,2048]{3,2,1,0:T(8,128)(2,1)}, u32[]{:S(2)}, u32[]{:S(2)}) collective-permute-start(bf16[4,2,16,2048]{3,2,1,0:T(8,128)(2,1)} %collective-permute-done.10.refs_3_), channel_id=1, source_target_pairs={{0,4},{4,8},{8,12},{12,0},{1,5},{5,9},{9,13},{13,1},{2,6},{6,10},{... | collective-permute-start | bytes 1572872 | tf_op jit(solution)/shard_map/ppermute | solution.py:34
  141.9 16.3 %collective-permute-start.22 = (bf16[4,2,16,2048]{3,2,1,0:T(8,128)(2,1)}, bf16[4,2,16,2048]{3,2,1,0:T(8,128)(2,1)}, u32[]{:S(2)}, u32[]{:S(2)}) collective-permute-start(bf16[4,2,16,2048]{3,2,1,0:T(8,128)(2,1)} %collective-permute-done.11.refs_2_), channel_id=1, source_target_pairs={{0,12},{4,0},{8,4},{12,8},{1,13},{5,1},{9,5},{13,9},{2,14},{6,2},{... | collective-permute-start | bytes 1572872 | tf_op jit(solution)/shard_map/ppermute | solution.py:39
  145.6 13.2 %collective-permute-start.24 = (bf16[4,2,16,2048]{3,2,1,0:T(8,128)(2,1)}, bf16[4,2,16,2048]{3,2,1,0:T(8,128)(2,1)}, u32[]{:S(2)}, u32[]{:S(2)}) collective-permute-start(bf16[4,2,16,2048]{3,2,1,0:T(8,128)(2,1)} %collective-permute-done.19.refs_1_), channel_id=1, source_target_pairs={{0,1},{1,0},{2,3},{3,2},{4,5},{5,4},{6,7},{7,6},{8,9},{9,8},{10,11... | collective-permute-start | bytes 1572872 | tf_op jit(solution)/shard_map/ppermute | solution.py:43
  148.1 25.5 %all-to-all-start.2 = ((bf16[64,24,256]{2,1,0:T(8,128)(2,1)}), bf16[64,24,256]{2,1,0:T(8,128)(2,1)}, u32[]{:S(2)}, u32[]{:S(2)}) async-start(bf16[64,24,256]{2,1,0:T(8,128)(2,1)} %add_convert_fusion), calls=%async_computation.2 | async-start | bytes 1572864 | tf_op jit(solution)/shard_map/all_to_all | solution.py:382
  157.0 2.2 %collective-permute-start.25 = (bf16[4,2,16,2048]{3,2,1,0:T(8,128)(2,1)}, bf16[4,2,16,2048]{3,2,1,0:T(8,128)(2,1)S(1)}, u32[]{:S(2)}, u32[]{:S(2)}) collective-permute-start(bf16[4,2,16,2048]{3,2,1,0:T(8,128)(2,1)} %collective-permute-done.11.refs_2_), channel_id=1, source_target_pairs={{0,1},{1,0},{2,3},{3,2},{4,5},{5,4},{6,7},{7,6},{8,9},{9,8},{10,11... | collective-permute-start | bytes 1572872 | tf_op jit(solution)/shard_map/ppermute | solution.py:43
  157.3 2.6 %collective-permute-start.26 = (bf16[4,2,16,2048]{3,2,1,0:T(8,128)(2,1)}, bf16[4,2,16,2048]{3,2,1,0:T(8,128)(2,1)S(1)}, u32[]{:S(2)}, u32[]{:S(2)}) collective-permute-start(bf16[4,2,16,2048]{3,2,1,0:T(8,128)(2,1)} %collective-permute-done.10.refs_3_), channel_id=1, source_target_pairs={{0,1},{1,0},{2,3},{3,2},{4,5},{5,4},{6,7},{7,6},{8,9},{9,8},{10,11... | collective-permute-start | bytes 1572872 | tf_op jit(solution)/shard_map/ppermute | solution.py:43
  158.2 2.5 %collective-permute-start.27 = (bf16[4,2,16,2048]{3,2,1,0:T(8,128)(2,1)}, bf16[4,2,16,2048]{3,2,1,0:T(8,128)(2,1)S(1)}, u32[]{:S(2)}, u32[]{:S(2)}) collective-permute-start(bf16[4,2,16,2048]{3,2,1,0:T(8,128)(2,1)} %collective-permute-done.20.refs_4_), channel_id=1, source_target_pairs={{0,1},{1,0},{2,3},{3,2},{4,5},{5,4},{6,7},{7,6},{8,9},{9,8},{10,11... | collective-permute-start | bytes 1572872 | tf_op jit(solution)/shard_map/ppermute | solution.py:43
  158.2 3.2 %collective-permute-start.28 = (bf16[4,2,16,2048]{3,2,1,0:T(8,128)(2,1)}, bf16[4,2,16,2048]{3,2,1,0:T(8,128)(2,1)S(1)}, u32[]{:S(2)}, u32[]{:S(2)}) collective-permute-start(bf16[4,2,16,2048]{3,2,1,0:T(8,128)(2,1)} %collective-permute-done.21.refs_5_), channel_id=1, source_target_pairs={{0,1},{1,0},{2,3},{3,2},{4,5},{5,4},{6,7},{7,6},{8,9},{9,8},{10,11... | collective-permute-start | bytes 1572872 | tf_op jit(solution)/shard_map/ppermute | solution.py:43
  158.7 3.5 %collective-permute-start.29 = (bf16[4,2,16,2048]{3,2,1,0:T(8,128)(2,1)}, bf16[4,2,16,2048]{3,2,1,0:T(8,128)(2,1)S(1)}, u32[]{:S(2)}, u32[]{:S(2)}) collective-permute-start(bf16[4,2,16,2048]{3,2,1,0:T(8,128)(2,1)} %collective-permute-done.22.refs_6_), channel_id=1, source_target_pairs={{0,1},{1,0},{2,3},{3,2},{4,5},{5,4},{6,7},{7,6},{8,9},{9,8},{10,11... | collective-permute-start | bytes 1572872 | tf_op jit(solution)/shard_map/ppermute | solution.py:43
  162.2 1.0 copy-start.3
